TPU v7x, 256 devices: a whole 4x4x8 slice. The times are simulated.
256 devices in a mesh: rad: 16 (over y, x_lo, core), azi: 16 (over x_hi, z).
Axes of the slice: x: 4 (x_hi: 2, x_lo: 2; x = x_hi * 2 + x_lo), y: 4, z: 8, core: 2. Of those that a mesh axis runs over, the one named last changes fastest.
Arguments:
- positions: float32 [3, 4194304], P(None, ('rad', 'azi')), may hold values from 0 to 1
- velocities: float32 [3, 4194304], P(None, ('rad', 'azi')), may hold values from -3 to 3
- masses: float32 [4194304], P(('rad', 'azi')), may hold values from 0.5 to 2
- neighbours: int32 [32768, 4], P(('rad', 'azi')), may hold values from 0 to 143, as said below
- shear_offsets: int32 [2, 16], replicated, may hold values from 0 to 15
- destinations: int32 [32768], P(('rad', 'azi')), may hold values from 0 to 15, as said below
- deposit_cells: int32 [2, 4194304], P(None, ('rad', 'azi')), may hold values from 0 to 4095
- old_potential: float32 [1024, 1024], P('rad', 'azi'), may hold values from -6 to 6
Outputs:
- migrated: float32 [7, 16777216], P(None, ('rad', 'azi'))
- potential: float32 [1024, 1024], P('rad', 'azi')
Inputs may be any that keep to these rules, and one draw needn't show every extreme that they name: `neighbours`: entries index a device's table of 128 own tiles and 16 ghost tiles; the first entry of each tile's list is the tile itself, and each ghost tile is listed by some tile of every device. `destinations`: one device sends at most 32 tiles to any one azimuthal strip and a device receives at most 512 tiles; in every radial strip one azimuthal strip receives exactly 32 tiles from each device of that radial strip.
All inputs are finite; a program needn't handle non-finite values.
Results may differ from a plain program's by a relative error of at most 0.0003.
Values sent between devices are 32-bit elements; how exact they have to be, the bound alone decides.
No kernel may reach another device: no remote copies, remote signals or barrier semaphores. Data moves between devices by JAX's collectives and lax.ppermute only.
A program may use at most 64 MiB of HBM per device.

v0:
```python
import math

import jax
import jax.numpy as jnp
from jax import lax
from jax.sharding import PartitionSpec as P

EDGE = 4
STEPS = 2


TIME_STEP = 0.1
ORBIT_FREQ = 0.3
CONTACT_STIFF = 0.15
INV_WIDTH = 4.0
GRAV_SCALE = 0.01


def shifted(value, axis, steps):
    count = lax.axis_size(axis)
    pairs = [(source, (source + steps) % count) for source in range(count)]
    return lax.ppermute(value, axis, pairs)


def padded_2(cells, sides, width):
    for axis, dim in sides:
        count = lax.axis_size(axis)
        head = lax.slice_in_dim(cells, 0, width, axis=dim)
        tail = lax.slice_in_dim(cells, cells.shape[dim] - width, cells.shape[dim], axis=dim)
        cells = jnp.concatenate(
            [
                lax.ppermute(tail, axis, [(i, (i + 1) % count) for i in range(count)]),
                cells,
                lax.ppermute(head, axis, [((i + 1) % count, i) for i in range(count)]),
            ],
            axis=dim,
        )
    return cells


def contact_forces(own_tiles, table_all, neighbour_rows):
    groups = own_tiles.shape[1] // 4
    own_groups = jnp.transpose(own_tiles.reshape(4, groups, 4, -1), (1, 0, 2, 3))
    row_groups = neighbour_rows.reshape(groups, 4, -1)

    def one_group(group_args):
        own_part, row_part = group_args
        others = jnp.take(table_all, row_part, axis=1)
        offsets = own_part[:3, :, None, :, None] - others[:3, :, :, None, :]
        distance = jnp.sum(offsets * offsets, axis=0)
        weights = others[3][:, :, None, :] * jnp.exp(-INV_WIDTH * distance)
        return CONTACT_STIFF * jnp.sum(offsets * weights[None], axis=(2, 4))

    result = lax.map(one_group, (own_groups, row_groups))
    return jnp.transpose(result, (1, 0, 2, 3)).reshape(3, own_tiles.shape[1], -1)


def phase_table(rows, cols, length):
    row_ids = jnp.arange(rows, dtype=jnp.int32)
    col_ids = jnp.arange(cols, dtype=jnp.int32)
    phases = row_ids[:, None] * col_ids[None, :] % length
    angles = phases.astype(jnp.float32) * (2.0 * jnp.pi / length)
    return (jnp.cos(angles), jnp.sin(angles))


def dft_tables(length):
    first = 1
    for factor in range(1, math.isqrt(length) + 1):
        if length % factor == 0:
            first = factor
    second = length // first
    return (
        first,
        second,
        phase_table(first, first, first),
        phase_table(second, second, second),
        phase_table(second, first, length),
    )


def complex_product(real_part, imag_part, table, sign):
    cosine, sine_table = table
    both = jnp.stack([real_part, imag_part])
    with_cos = jnp.dot(both, cosine, precision=lax.Precision.HIGHEST)
    with_sin = jnp.dot(both, sine_table, precision=lax.Precision.HIGHEST)
    return (with_cos[0] - sign * with_sin[1], with_cos[1] + sign * with_sin[0])


def transform(pencil, tables, inverse):
    first, second, table_first, table_second, twiddle = tables
    length = first * second
    sign = 1.0 if inverse else -1.0
    rows = pencil.shape[1]
    real_part = jnp.swapaxes(pencil[0].reshape(rows, first, second), 1, 2)
    imag_part = jnp.swapaxes(pencil[1].reshape(rows, first, second), 1, 2)
    real_part, imag_part = complex_product(real_part, imag_part, table_first, sign)
    twist_cos, twist_sin = twiddle
    twist_sin = sign * twist_sin
    real_part, imag_part = (
        real_part * twist_cos - imag_part * twist_sin,
        imag_part * twist_cos + real_part * twist_sin,
    )
    real_part = jnp.swapaxes(real_part, 1, 2)
    imag_part = jnp.swapaxes(imag_part, 1, 2)
    real_part, imag_part = complex_product(real_part, imag_part, table_second, sign)
    real_part = jnp.swapaxes(real_part, 1, 2).reshape(rows, length)
    imag_part = jnp.swapaxes(imag_part, 1, 2).reshape(rows, length)
    if inverse:
        return jnp.stack([real_part / length, imag_part / length])
    return jnp.stack([real_part, imag_part])


def green_values(wave_x, wave_y, size_x, size_y):
    eigen_x = 4.0 * jnp.sin(jnp.pi * wave_x.astype(jnp.float32) / size_x) ** 2
    eigen_y = 4.0 * jnp.sin(jnp.pi * wave_y.astype(jnp.float32) / size_y) ** 2
    lam_grid = eigen_x[:, None] + eigen_y[None, :]
    at_zero = (wave_x[:, None] == 0) & (wave_y[None, :] == 0)
    return jnp.where(at_zero, 0.0, -GRAV_SCALE / jnp.where(at_zero, 1.0, lam_grid))


def along_radial(blocks, tables, inverse):
    turned = jnp.swapaxes(blocks, 1, 2)
    pencil = lax.all_to_all(turned, "rad", split_axis=1, concat_axis=2, tiled=True)
    pencil = transform(pencil, tables, inverse)
    turned = lax.all_to_all(pencil, "rad", split_axis=2, concat_axis=1, tiled=True)
    return jnp.swapaxes(turned, 1, 2)


def along_azimuth(blocks, tables, inverse):
    pencil = lax.all_to_all(blocks, "azi", split_axis=1, concat_axis=2, tiled=True)
    pencil = transform(pencil, tables, inverse)
    return lax.all_to_all(pencil, "azi", split_axis=2, concat_axis=1, tiled=True)


def solve_potential(density, tables_x, tables_y, rad_place, azi_place, rad_count, azi_count):
    grid_x, grid_y = density.shape
    size_x = grid_x * rad_count
    size_y = grid_y * azi_count
    blocks = jnp.stack([density, jnp.zeros_like(density)])
    blocks = along_radial(blocks, tables_x, False)
    blocks = along_azimuth(blocks, tables_y, False)
    wave_x = rad_place * grid_x + jnp.arange(grid_x, dtype=jnp.int32)
    wave_y = azi_place * grid_y + jnp.arange(grid_y, dtype=jnp.int32)
    blocks = blocks * green_values(wave_x, wave_y, size_x, size_y)[None]
    blocks = along_azimuth(blocks, tables_y, True)
    blocks = along_radial(blocks, tables_x, True)
    return blocks[0]


def ghost_table(carried, offsets_now, rad_place, azi_place, rad_count, azi_count):
    from_below = shifted(carried[:, EDGE : 2 * EDGE], "rad", 1)
    from_above = shifted(carried[:, :EDGE], "rad", -1)
    amount_below = offsets_now[rad_place]
    amount_above = (azi_count - offsets_now[(rad_place + 1) % rad_count]) % azi_count
    stacked = jnp.stack([from_below, from_above])
    all_rows = lax.all_gather(stacked[None], "azi", axis=0, tiled=True)
    source_below = (azi_place - amount_below) % azi_count
    source_above = (azi_place - amount_above) % azi_count
    sheared_below = lax.dynamic_index_in_dim(all_rows, source_below, 0, keepdims=False)[0]
    sheared_above = lax.dynamic_index_in_dim(all_rows, source_above, 0, keepdims=False)[1]
    from_left = shifted(carried[:, 3 * EDGE : 4 * EDGE], "azi", 1)
    from_right = shifted(carried[:, 2 * EDGE : 3 * EDGE], "azi", -1)
    sheared_below = sheared_below.at[0].add(-1.0)
    sheared_above = sheared_above.at[0].add(1.0)
    from_left = from_left.at[1].add(-1.0)
    from_right = from_right.at[1].add(1.0)
    return jnp.concatenate([carried, sheared_below, sheared_above, from_left, from_right], axis=1)


def local(
    positions,
    velocities,
    masses,
    neighbours,
    shear_offsets,
    destinations,
    deposit_cells,
    old_potential,
):
    rad_count = lax.axis_size("rad")
    azi_count = lax.axis_size("azi")
    rad_place = lax.axis_index("rad")
    azi_place = lax.axis_index("azi")
    tile_count = neighbours.shape[0]
    tile_size = positions.shape[1] // tile_count
    grid_x, grid_y = old_potential.shape
    tables_x = dft_tables(grid_x * rad_count)
    tables_y = dft_tables(grid_y * azi_count)
    place = positions
    speed = velocities
    potential_now = old_potential
    strip_x = (rad_place - rad_count // 2).astype(jnp.float32)
    for step_index in range(STEPS):
        cells_now = deposit_cells[step_index]
        padded = padded_2(potential_now, (("rad", 0), ("azi", 1)), 1)
        grad_x = -(padded[2:, 1:-1] - padded[:-2, 1:-1]) * 0.5
        grad_y = -(padded[1:-1, 2:] - padded[1:-1, :-2]) * 0.5
        grad_field = jnp.stack([grad_x, grad_y]).reshape(2, -1)
        gravity = jnp.take(grad_field, cells_now, axis=1)
        density = jax.ops.segment_sum(masses, cells_now, num_segments=grid_x * grid_y).reshape(
            grid_x, grid_y
        )
        next_potential = solve_potential(
            density, tables_x, tables_y, rad_place, azi_place, rad_count, azi_count
        )
        carried = jnp.concatenate([place, masses[None]], axis=0).reshape(4, tile_count, tile_size)
        table_all = ghost_table(
            carried, shear_offsets[step_index], rad_place, azi_place, rad_count, azi_count
        )
        forces = contact_forces(carried, table_all, neighbours).reshape(3, -1)
        tidal_x = place[0] + strip_x
        accel = jnp.stack(
            [
                forces[0]
                + gravity[0]
                + 2.0 * ORBIT_FREQ * speed[1]
                + 3.0 * ORBIT_FREQ**2 * tidal_x,
                forces[1] + gravity[1] - 2.0 * ORBIT_FREQ * speed[0],
                forces[2] - ORBIT_FREQ**2 * (place[2] - 0.5),
            ]
        )
        speed = speed + TIME_STEP * accel
        place = place + TIME_STEP * speed
        potential_now = next_potential
    final_state = jnp.concatenate([place, speed, masses[None]], axis=0).reshape(
        7, tile_count, tile_size
    )
    slot_cap = tile_count // 4
    capacity = slot_cap * azi_count
    strip_ids = jnp.arange(azi_count, dtype=jnp.int32)
    signed = (azi_place - destinations + azi_count // 2) % azi_count - azi_count // 2
    final_state = final_state.at[1].add(signed.astype(jnp.float32)[:, None])
    hit_table = (destinations[:, None] == strip_ids[None, :]).astype(jnp.int32)
    earlier = jnp.cumsum(hit_table, axis=0) - hit_table
    rank_slot = jnp.sum(earlier * hit_table, axis=1)
    target = destinations * slot_cap + rank_slot
    select = (jnp.arange(capacity, dtype=jnp.int32)[:, None] == target[None, :]).astype(jnp.float32)
    packed = jnp.einsum("st,ctp->csp", select, final_state, precision=lax.Precision.HIGHEST)
    packed = packed.reshape(7, azi_count, slot_cap * tile_size)
    arrived = lax.all_to_all(packed, "azi", split_axis=1, concat_axis=1, tiled=True)
    return (arrived.reshape(7, -1), potential_now)


def solution(mesh):
    placed = (
        P(None, ("rad", "azi")),
        P(None, ("rad", "azi")),
        P(("rad", "azi")),
        P(("rad", "azi"), None),
        P(),
        P(("rad", "azi")),
        P(None, ("rad", "azi")),
        P("rad", "azi"),
    )
    return jax.shard_map(
        local,
        mesh=mesh,
        in_specs=placed,
        out_specs=(P(None, ("rad", "azi")), P("rad", "azi")),
        check_vma=False,
    )
```

profile of v0, /device:TPU:32, one launch (start us, length us, event | category | flops | bytes accessed | tf_op | source)
XLA Modules:
  0.0 839.2 jit_solution(4852144124154031873)
XLA Ops:
  1.8 86.1 %scatter_custom_fusion.1 = f32[4096]{0:T(1024)S(1)} fusion(s32[16384]{0:T(1024)S(1)} %bitcast.667, f32[16384]{0:T(1024)} %param.36, f32[]{:T(128)} %constant.400.clone.1), kind=kCustom, calls=%fused_computation.361 | custom fusion | flops 16384 | bytes 16896 | tf_op jit(solution)/shard_map/scatter-add | solution.py:200
  88.7 5.5 all-to-all-start.9
  96.5 3.5 collective-permute-start.1
  108.8 85.8 %scatter_custom_fusion = f32[4096]{0:T(1024)S(1)} fusion(s32[16384]{0:T(1024)S(1)} %bitcast.666, f32[16384]{0:T(1024)S(1)} %copy-done.1, f32[]{:T(128)} %constant.400.clone.1), kind=kCustom, calls=%fused_computation.363 | custom fusion | flops 16384 | bytes 16388 | tf_op jit(solution)/shard_map/scatter-add | solution.py:200
  196.4 8.0 collective-permute-start.6
  205.8 2.2 collective-permute-done.7
  209.2 54.5 %gather_fusion.2 = f32[16384,2]{1,0:T(8,128)} fusion(f32[2,4096]{0,1:T(8,128)S(1)} %copy.651, s32[16384]{0:T(1024)S(1)} %fusion.107), kind=kCustom, calls=%fused_computation.1.clone | custom fusion | bytes 327680 | tf_op jit(solution)/shard_map/jit(_take)/gather | solution.py:199
  263.7 5.3 copy.652
  269.2 41.7 %all-gather = f32[32,4,4,128]{3,2,1,0:T(4,128)S(1)} all-gather(f32[2,4,4,128]{3,2,1,0:T(4,128)S(1)} %pad_maximum_fusion.77), channel_id=2, replica_groups=mesh['rad'=16,'azi'=16] {'azi'}, dimensions={0}, use_global_device_ids=true | all-gather | bytes 278528 | tf_op jit(solution)/shard_map/all_gather | solution.py:156
  311.2 68.4 %while.29 = (s32[]{:T(128)}, f32[32,3,4,128]{3,2,1,0:T(4,128)S(1)}, f32[32,4,4,128]{3,2,0,1:T(4,128)S(1)}, s32[32,4,4]{2,1,0:T(4,128)S(1)}, f32[4,144,128]{2,0,1:T(4,128)S(1)}, /*index=5*/s32[]{:T(128)}) while((s32[]{:T(128)}, f32[32,3,4,128]{3,2,1,0:T(4,128)S(1)}, f32[32,4,4,128]{3,2,0,1:T(4,128)S(1)}, s32[32,4,4]{2,1,0:T(4,128)S(1)}, ...), condition=%wide.region_3.5_spmd, body=%wide.region_0.0_spmd.sunk | while | flops 4990050 | bytes 4512241 | solution.py:54
  381.9 3.8 collective-permute-start.9
  386.8 2.7 collective-permute-done.10
  389.4 3.5 all-to-all-start
  395.4 3.6 all-to-all-done
  403.5 2.1 reshape.847
  405.6 3.5 all-to-all-start.1
  412.2 2.9 all-to-all-done.1
  415.2 3.9 all-to-all-start.10
  422.8 2.3 all-to-all-done.10
  425.1 7.9 all-to-all-start.2
  433.0 38.5 %all-gather.1 = f32[32,4,4,128]{3,2,1,0:T(4,128)S(1)} all-gather(f32[2,4,4,128]{3,2,1,0:T(4,128)S(1)} %pad_maximum_fusion.78), channel_id=3, replica_groups=mesh['rad'=16,'azi'=16] {'azi'}, dimensions={0}, use_global_device_ids=true | all-gather | bytes 278528 | tf_op jit(solution)/shard_map/all_gather | solution.py:156
  475.2 7.4 all-to-all-start.11
  484.5 6.9 all-to-all-done.11
  498.1 4.7 all-to-all-start.3
  505.8 5.7 all-to-all-done.3
  511.6 4.7 all-to-all-start.12
  519.1 5.9 all-to-all-done.12
  528.8 4.8 all-to-all-start.4
  534.6 7.8 all-to-all-done.4
  542.4 4.7 all-to-all-start.13
  548.9 7.0 all-to-all-done.13
  562.5 4.7 all-to-all-start.5
  570.2 5.7 all-to-all-done.5
  576.0 4.7 all-to-all-start.14
  580.7 68.0 %while.30 = (s32[]{:T(128)}, f32[32,3,4,128]{3,2,1,0:T(4,128)S(1)}, f32[32,4,4,128]{3,2,1,0:T(4,128)S(1)}, s32[32,4,4]{2,1,0:T(4,128)S(1)}, f32[4,144,128]{2,0,1:T(4,128)S(1)}, /*index=5*/s32[]{:T(128)}) while((s32[]{:T(128)}, f32[32,3,4,128]{3,2,1,0:T(4,128)S(1)}, f32[32,4,4,128]{3,2,1,0:T(4,128)S(1)}, s32[32,4,4]{2,1,0:T(4,128)S(1)}, ...), condition=%wide.region_7.10_spmd, body=%wide.region_4.9_spmd.sunk | while | flops 4990050 | bytes 4495857 | solution.py:54
  652.4 3.5 all-to-all-start.6
  659.7 2.3 all-to-all-done.6
  662.0 3.7 all-to-all-start.15
  667.6 4.2 all-to-all-done.15
  678.7 3.5 all-to-all-start.7
  682.3 6.0 all-to-all-done.7
  693.8 3.9 collective-permute-done.13
  702.4 3.7 all-to-all-start.16
  707.4 54.5 %gather_fusion.3 = f32[16384,2]{1,0:T(8,128)} fusion(f32[2,4096]{0,1:T(8,128)S(1)} %copy.707, s32[16384]{0:T(1024)S(1)} %fusion.108), kind=kCustom, calls=%fused_computation.3.clone | custom fusion | bytes 327680 | tf_op jit(solution)/shard_map/jit(_take)/gather | solution.py:199
  761.9 5.3 copy.708
  772.9 2.4 copy.714
  775.3 11.3 %all-to-all-start.8 = ((f32[7,16,4096]{2,0,1:T(8,128)}), f32[7,16,4096]{2,0,1:T(8,128)S(1)}, u32[]{:S(2)}, u32[]{:S(2)}) async-start(f32[7,16,4096]{2,0,1:T(8,128)} %copy.714), calls=%async_computation.8 | async-start | bytes 4194304 | tf_op jit(solution)/shard_map/all_to_all | solution.py:240
  790.2 47.3 %all-to-all-done.8 = f32[7,16,4096]{2,0,1:T(8,128)S(1)} async-done(((f32[7,16,4096]{2,0,1:T(8,128)}), f32[7,16,4096]{2,0,1:T(8,128)S(1)}, u32[]{:S(2)}, u32[]{:S(2)}) %all-to-all-start.8) | async-done | bytes 1835040 | tf_op jit(solution)/shard_map/all_to_all | solution.py:240
  (1153 shorter events, 235.0 us)
Async XLA Ops:
  0.6 108.1 %copy-start.1 = (f32[16384]{0:T(1024)S(1)}, f32[16384]{0:T(1024)}, u32[]{:S(2)}) copy-start(f32[16384]{0:T(1024)} %param.36) | copy-start | bytes 196612
  0.6 194.9 %copy-start.3 = (s32[128]{0:T(128)S(1)}, s32[128]{0:T(128)}, u32[]{:S(2)}) copy-start(s32[128]{0:T(128)} %param.39) | copy-start | bytes 1540
  0.7 195.6 %copy-start.4 = (s32[128,4]{0,1:T(4,128)S(1)}, s32[128,4]{0,1:T(4,128)}, u32[]{:S(2)}) copy-start(s32[128,4]{0,1:T(4,128)} %param.37) | copy-start | bytes 6148
  88.7 300.7 %all-to-all-start.9 = ((f32[16,1,512]{2,1,0:T(1,128)}), f32[16,1,512]{2,1,0:T(1,128)S(1)}, u32[]{:S(2)}, u32[]{:S(2)}) async-start(f32[16,1,512]{2,1,0:T(1,128)} %reshape.861), calls=%async_computation.9 | async-start | bytes 65536 | tf_op jit(solution)/shard_map/all_to_all | solution.py:123
  96.0 173.1 %collective-permute-start = (f32[4,4,128]{2,1,0:T(4,128)S(1)}, f32[4,4,128]{2,1,0:T(4,128)S(1)}, u32[]{:S(2)}, u32[]{:S(2)}) collective-permute-start(f32[4,4,128]{2,1,0:T(4,128)S(1)} %get-tuple-element.293), channel_id=1, source_target_pairs={{0,16},{16,32},{32,48},{48,64},{64,80},{80,96},{96,112},{112,128},... | collective-permute-start | bytes 24584 | tf_op jit(solution)/shard_map/ppermute | solution.py:22
  96.5 172.7 %collective-permute-start.1 = (f32[4,4,128]{2,1,0:T(4,128)S(1)}, f32[4,4,128]{2,1,0:T(4,128)S(1)}, u32[]{:S(2)}, u32[]{:S(2)}) collective-permute-start(f32[4,4,128]{2,1,0:T(4,128)S(1)} %get-tuple-element.294), channel_id=1, source_target_pairs={{0,240},{16,0},{32,16},{48,32},{64,48},{80,64},{96,80},{112,96},{1... | collective-permute-start | bytes 24584 | tf_op jit(solution)/shard_map/ppermute | solution.py:22
  99.9 210.9 %collective-permute-start.3 = (f32[4,4,128]{2,1,0:T(4,128)S(1)}, f32[4,4,128]{2,1,0:T(4,128)S(1)}, u32[]{:S(2)}, u32[]{:S(2)}) collective-permute-start(f32[4,4,128]{2,1,0:T(4,128)S(1)} %get-tuple-element.292), channel_id=1, source_target_pairs={{0,15},{1,0},{2,1},{3,2},{4,3},{5,4},{6,5},{7,6},{8,7},{9,8},{10,9... | collective-permute-start | bytes 24584 | tf_op jit(solution)/shard_map/ppermute | solution.py:22
  100.9 95.5 %collective-permute-start.4 = (f32[1,64]{0,1:T(8,128)S(1)}, f32[1,64]{0,1:T(8,128)S(1)}, u32[]{:S(2)}, u32[]{:S(2)}) collective-permute-start(f32[1,64]{0,1:T(8,128)S(1)} %copy.644), channel_id=1, source_target_pairs={{16,0},{32,16},{48,32},{64,48},{80,64},{96,80},{112,96},{128,112},... | collective-permute-start | bytes 776 | tf_op jit(solution)/shard_map/ppermute | solution.py:34
  101.3 95.0 %collective-permute-start.5 = (f32[1,64]{0,1:T(8,128)S(1)}, f32[1,64]{0,1:T(8,128)S(1)}, u32[]{:S(2)}, u32[]{:S(2)}) collective-permute-start(f32[1,64]{0,1:T(8,128)S(1)} %copy.646), channel_id=1, source_target_pairs={{0,16},{16,32},{32,48},{48,64},{64,80},{80,96},{96,112},{112,128},... | collective-permute-start | bytes 776 | tf_op jit(solution)/shard_map/ppermute | solution.py:32
  196.4 9.3 %collective-permute-start.6 = (f32[66,1]{0,1:T(1,128)S(1)}, f32[66,1]{0,1:T(1,128)S(1)}, u32[]{:S(2)}, u32[]{:S(2)}) collective-permute-start(f32[66,1]{0,1:T(1,128)S(1)} %get-tuple-element.314), channel_id=1, source_target_pairs={{1,0},{2,1},{3,2},{4,3},{5,4},{6,5},{7,6},{8,7},{9,8},{10,9},{11,1... | collective-permute-start | bytes 800 | tf_op jit(solution)/shard_map/ppermute | solution.py:34
  204.5 3.5 collective-permute-start.7
  205.8 105.2 %collective-permute-start.2 = (f32[4,4,128]{2,1,0:T(4,128)S(1)}, f32[4,4,128]{2,1,0:T(4,128)S(1)}, u32[]{:S(2)}, u32[]{:S(2)}) collective-permute-start(f32[4,4,128]{2,1,0:T(4,128)S(1)} %get-tuple-element.295), channel_id=1, source_target_pairs={{0,1},{1,2},{2,3},{3,4},{4,5},{5,6},{6,7},{7,8},{8,9},{9,10},{10,1... | collective-permute-start | bytes 24584 | tf_op jit(solution)/shard_map/ppermute | solution.py:22
  311.2 68.5 %copy-start = (f32[3,16384]{1,0:T(4,128)S(1)}, f32[3,16384]{1,0:T(4,128)}, u32[]{:S(2)}) copy-start(f32[3,16384]{1,0:T(4,128)} %param.34) | copy-start | bytes 589828
  311.2 68.5 %copy-start.2 = (f32[3,16384]{1,0:T(4,128)S(1)}, f32[3,16384]{1,0:T(4,128)}, u32[]{:S(2)}) copy-start(f32[3,16384]{1,0:T(4,128)} %param.35) | copy-start | bytes 589828
  380.6 6.1 collective-permute-start.11
  381.8 37.2 %collective-permute-start.8 = (f32[4,4,128]{2,1,0:T(4,128)S(1)}, f32[4,4,128]{2,1,0:T(4,128)S(1)}, u32[]{:S(2)}, u32[]{:S(2)}) collective-permute-start(f32[4,4,128]{2,1,0:T(4,128)S(1)} %get-tuple-element.284), channel_id=1, source_target_pairs={{0,16},{16,32},{32,48},{48,64},{64,80},{80,96},{96,112},{112,128},... | collective-permute-start | bytes 24584 | tf_op jit(solution)/shard_map/ppermute | solution.py:22
  381.9 37.2 %collective-permute-start.9 = (f32[4,4,128]{2,1,0:T(4,128)S(1)}, f32[4,4,128]{2,1,0:T(4,128)S(1)}, u32[]{:S(2)}, u32[]{:S(2)}) collective-permute-start(f32[4,4,128]{2,1,0:T(4,128)S(1)} %get-tuple-element.285), channel_id=1, source_target_pairs={{0,240},{16,0},{32,16},{48,32},{64,48},{80,64},{96,80},{112,96},{1... | collective-permute-start | bytes 24584 | tf_op jit(solution)/shard_map/ppermute | solution.py:22
  385.8 3.7 collective-permute-start.10
  389.4 9.5 %all-to-all-start = ((f32[16,1,512]{2,1,0:T(1,128)}), f32[16,1,512]{2,1,0:T(1,128)S(1)}, u32[]{:S(2)}, u32[]{:S(2)}) async-start(f32[16,1,512]{2,1,0:T(1,128)} %reshape.845), calls=%async_computation | async-start | bytes 65536 | tf_op jit(solution)/shard_map/all_to_all | solution.py:123
  405.6 9.5 %all-to-all-start.1 = ((f32[16,1,512]{2,1,0:T(1,128)}), f32[16,1,512]{2,1,0:T(1,128)S(1)}, u32[]{:S(2)}, u32[]{:S(2)}) async-start(f32[16,1,512]{2,1,0:T(1,128)} %reshape.847), calls=%async_computation.1 | async-start | bytes 65536 | tf_op jit(solution)/shard_map/all_to_all | solution.py:125
  415.2 9.9 %all-to-all-start.10 = ((f32[16,1,512]{2,1,0:T(1,128)}), f32[16,1,512]{2,1,0:T(1,128)S(1)}, u32[]{:S(2)}, u32[]{:S(2)}) async-start(f32[16,1,512]{2,1,0:T(1,128)} %reshape.863), calls=%async_computation.10 | async-start | bytes 65536 | tf_op jit(solution)/shard_map/all_to_all | solution.py:125
  425.1 50.1 %all-to-all-start.2 = ((f32[16,1,512]{2,1,0:T(1,128)}), f32[16,1,512]{2,1,0:T(1,128)S(1)}, u32[]{:S(2)}, u32[]{:S(2)}) async-start(f32[16,1,512]{2,1,0:T(1,128)} %reshape.849), calls=%async_computation.2 | async-start | bytes 65536 | tf_op jit(solution)/shard_map/all_to_all | solution.py:130
  475.2 16.2 %all-to-all-start.11 = ((f32[16,1,512]{2,1,0:T(1,128)}), f32[16,1,512]{2,1,0:T(1,128)S(1)}, u32[]{:S(2)}, u32[]{:S(2)}) async-start(f32[16,1,512]{2,1,0:T(1,128)} %reshape.865), calls=%async_computation.11 | async-start | bytes 65536 | tf_op jit(solution)/shard_map/all_to_all | solution.py:130
  498.1 13.5 %all-to-all-start.3 = ((f32[16,1,512]{2,1,0:T(1,128)}), f32[16,1,512]{2,1,0:T(1,128)S(1)}, u32[]{:S(2)}, u32[]{:S(2)}) async-start(f32[16,1,512]{2,1,0:T(1,128)} %reshape.851), calls=%async_computation.3 | async-start | bytes 65536 | tf_op jit(solution)/shard_map/all_to_all | solution.py:132
  511.6 13.5 %all-to-all-start.12 = ((f32[16,1,512]{2,1,0:T(1,128)}), f32[16,1,512]{2,1,0:T(1,128)S(1)}, u32[]{:S(2)}, u32[]{:S(2)}) async-start(f32[16,1,512]{2,1,0:T(1,128)} %reshape.867), calls=%async_computation.12 | async-start | bytes 65536 | tf_op jit(solution)/shard_map/all_to_all | solution.py:132
  528.8 13.6 %all-to-all-start.4 = ((f32[16,1,512]{2,1,0:T(1,128)}), f32[16,1,512]{2,1,0:T(1,128)S(1)}, u32[]{:S(2)}, u32[]{:S(2)}) async-start(f32[16,1,512]{2,1,0:T(1,128)} %reshape.853), calls=%async_computation.4 | async-start | bytes 65536 | tf_op jit(solution)/shard_map/all_to_all | solution.py:130
  542.4 13.5 %all-to-all-start.13 = ((f32[16,1,512]{2,1,0:T(1,128)}), f32[16,1,512]{2,1,0:T(1,128)S(1)}, u32[]{:S(2)}, u32[]{:S(2)}) async-start(f32[16,1,512]{2,1,0:T(1,128)} %reshape.869), calls=%async_computation.13 | async-start | bytes 65536 | tf_op jit(solution)/shard_map/all_to_all | solution.py:130
  562.5 13.5 %all-to-all-start.5 = ((f32[16,1,512]{2,1,0:T(1,128)}), f32[16,1,512]{2,1,0:T(1,128)S(1)}, u32[]{:S(2)}, u32[]{:S(2)}) async-start(f32[16,1,512]{2,1,0:T(1,128)} %reshape.855), calls=%async_computation.5 | async-start | bytes 65536 | tf_op jit(solution)/shard_map/all_to_all | solution.py:132
  576.0 76.4 %all-to-all-start.14 = ((f32[16,1,512]{2,1,0:T(1,128)}), f32[16,1,512]{2,1,0:T(1,128)S(1)}, u32[]{:S(2)}, u32[]{:S(2)}) async-start(f32[16,1,512]{2,1,0:T(1,128)} %reshape.871), calls=%async_computation.14 | async-start | bytes 65536 | tf_op jit(solution)/shard_map/all_to_all | solution.py:132
  652.4 9.5 %all-to-all-start.6 = ((f32[16,1,512]{2,1,0:T(1,128)}), f32[16,1,512]{2,1,0:T(1,128)S(1)}, u32[]{:S(2)}, u32[]{:S(2)}) async-start(f32[16,1,512]{2,1,0:T(1,128)} %reshape.857), calls=%async_computation.6 | async-start | bytes 65536 | tf_op jit(solution)/shard_map/all_to_all | solution.py:123
  662.0 9.7 %all-to-all-start.15 = ((f32[16,1,512]{2,1,0:T(1,128)}), f32[16,1,512]{2,1,0:T(1,128)S(1)}, u32[]{:S(2)}, u32[]{:S(2)}) async-start(f32[16,1,512]{2,1,0:T(1,128)} %reshape.873), calls=%async_computation.15 | async-start | bytes 65536 | tf_op jit(solution)/shard_map/all_to_all | solution.py:123
  678.7 9.5 %all-to-all-start.7 = ((f32[16,1,512]{2,1,0:T(1,128)}), f32[16,1,512]{2,1,0:T(1,128)S(1)}, u32[]{:S(2)}, u32[]{:S(2)}) async-start(f32[16,1,512]{2,1,0:T(1,128)} %reshape.859), calls=%async_computation.7 | async-start | bytes 65536 | tf_op jit(solution)/shard_map/all_to_all | solution.py:125
  691.3 2.5 collective-permute-start.12
  692.2 5.4 collective-permute-start.13
  697.7 8.5 %collective-permute-start.14 = (f32[66,1]{0,1:T(1,128)S(1)}, f32[66,1]{0,1:T(1,128)S(1)}, u32[]{:S(2)}, u32[]{:S(2)}) collective-permute-start(f32[66,1]{0,1:T(1,128)S(1)} %get-tuple-element.310), channel_id=1, source_target_pairs={{1,0},{2,1},{3,2},{4,3},{5,4},{6,5},{7,6},{8,7},{9,8},{10,9},{11,1... | collective-permute-start | bytes 800 | tf_op jit(solution)/shard_map/ppermute | solution.py:34
  698.0 8.2 collective-permute-start.15
  702.4 72.9 %all-to-all-start.16 = ((f32[16,1,512]{2,1,0:T(1,128)}), f32[16,1,512]{2,1,0:T(1,128)S(1)}, u32[]{:S(2)}, u32[]{:S(2)}) async-start(f32[16,1,512]{2,1,0:T(1,128)} %reshape.875), calls=%async_computation.16 | async-start | bytes 65536 | tf_op jit(solution)/shard_map/all_to_all | solution.py:125
  775.3 62.2 %all-to-all-start.8 = ((f32[7,16,4096]{2,0,1:T(8,128)}), f32[7,16,4096]{2,0,1:T(8,128)S(1)}, u32[]{:S(2)}, u32[]{:S(2)}) async-start(f32[7,16,4096]{2,0,1:T(8,128)} %copy.714), calls=%async_computation.8 | async-start | bytes 4194304 | tf_op jit(solution)/shard_map/all_to_all | solution.py:240
where the time goes:
time: 849 us; the launch traced here: 839 us
  other arithmetic  275 us (32%)
  local copies, waits for them, and re-layouts  234 us (28%)
  waiting for transfers between devices  119 us (14%)
  starting transfers between devices  107 us (13%)
  blocking collectives  80.2 us (9%)
  matrix products  12.5 us (1%)
    scatter-add x2, other arithmetic, local(): jax.ops.segment_sum(masses, cells_now, num_segments=grid_x * grid_y)  172 us
    gather x4, local copies, waits for them, and re-layouts, local(): gravity = jnp.take(grad_field, cells_now, axis=1)  120 us
    all_gather x2, blocking collectives, ghost_table(): all_rows = lax.all_gather(stacked[None], 'azi', axis=0, tiled=True)  80.2 us
    all_to_all x1, waiting for transfers between devices, local(): lax.all_to_all(packed, 'azi', split_axis=1, concat_axis=1, tiled=True)  47.3 us
    reduce_sum x64, other arithmetic, one_group(): return CONTACT_STIFF * jnp.sum(offsets * weights[None], axis=(2, 4))  44.9 us
    unnamed x50, local copies, waits for them, and re-layouts  40.5 us
    gather x64, local copies, waits for them, and re-layouts, one_group(): others = jnp.take(table_all, row_part, axis=1)  37.6 us
    all_to_all x4, starting transfers between devices, along_azimuth(): lax.all_to_all(blocks, 'azi', split_axis=1, concat_axis=2, tiled=True)  24.8 us
  transfers between devices with their start and end apart: 33, of which 18 were waited for; matrix products, arithmetic and copies ran while one was open for 48% of the time, Pallas kernels for 0%

commit v1 on v0

v1 whole, which is shorter than its diff:
```python
import functools
import math

import jax
import jax.numpy as jnp
import ml_dtypes
import numpy as np
from jax import lax
from jax.experimental import pallas as pl
from jax.experimental.pallas import tpu as pltpu
from jax.sharding import PartitionSpec as P

T = 128
TILES = 128
EDGE = 4
LINKS = 4
GHOSTS = 16
G = 64
SLOT = 32
STEPS = 2
DT = 0.1
OMEGA = 0.3
STIFF = 0.15
GRAV = 0.01
CEXP = 4.0 * math.log2(math.e)
CHUNK = 1024
F32 = jnp.float32
BF16 = jnp.bfloat16
VMEM = pl.BlockSpec(memory_space=pltpu.VMEM)
SMEM = pl.BlockSpec(memory_space=pltpu.SMEM)
EW = EDGE * T
NN = (((1,), (0,)), ((), ()))
NT = (((1,), (1,)), ((), ()))
TN = (((0,), (0,)), ((), ()))


def params():
    return pltpu.CompilerParams(vmem_limit_bytes=48 * 1024 * 1024)


def cost(us):
    return pl.CostEstimate(flops=int(us * 1.0e9), bytes_accessed=int(us * 3.0e6), transcendentals=0)


def dot(a, b, dims=NN):
    return lax.dot_general(a, b, dims, preferred_element_type=F32)


def split2(a):
    high = a.astype(BF16)
    return high, (a - high.astype(F32)).astype(BF16)


def split3(a):
    high = a.astype(BF16).astype(F32)
    rest = a - high
    mid = rest.astype(BF16).astype(F32)
    return high, mid, rest - mid


@functools.lru_cache(maxsize=None)
def tables(length, count):
    ids = np.arange(length, dtype=np.int64)
    angle = (ids[:, None] * ids[None, :] % length).astype(np.float64) * (2.0 * np.pi / length)
    full = (np.cos(angle) + np.sin(angle)) / math.sqrt(length)
    high = full.astype(ml_dtypes.bfloat16)
    low = (full - high.astype(np.float64)).astype(ml_dtypes.bfloat16)
    block = length // count
    rows = (np.arange(count)[:, None] * block - 1 + np.arange(block + 16)[None, :]) % length
    lam = (4.0 * np.sin(np.pi * ids / length) ** 2).astype(np.float32)
    return high, low, high[rows], low[rows], lam


def edges_kernel(pos_ref, mass_ref, pot_ref, up_ref, down_ref, right_ref, left_ref):
    pot = pot_ref[...]
    turned = pot.T
    halo = {
        1: pot[G - 1 : G, :],
        0: pot[0:1, :],
        3: turned[G - 1 : G, :],
        2: turned[0:1, :],
    }
    for ref, part in ((up_ref, 1), (down_ref, 0), (right_ref, 3), (left_ref, 2)):
        lanes = pl.ds(part * EW, EW)
        ref[0:3, 0:EW] = pos_ref[0:3, lanes]
        ref[3:4, 0:EW] = mass_ref[0:1, lanes]
        ref[:, EW : EW + 128] = jnp.zeros((4, 128), F32)
        ref[0:1, EW : EW + G] = halo[part]


def edges(pos, mass, pot):
    shape = jax.ShapeDtypeStruct((4, EW + 128), F32)
    return pl.pallas_call(
        edges_kernel,
        grid=(1,),
        in_specs=[
            pl.BlockSpec((3, 4 * EW), lambda i: (0, 0)),
            pl.BlockSpec((1, 4 * EW), lambda i: (0, 0)),
            pl.BlockSpec((G, G), lambda i: (0, 0)),
        ],
        out_specs=[pl.BlockSpec((4, EW + 128), lambda i: (0, 0))] * 4,
        out_shape=[shape] * 4,
        compiler_params=params(),
        cost_estimate=cost(1),
        name="edges",
    )(pos, mass, pot)


def density_kernel(cells_ref, mass_ref, dest_ref, dens_ref, target_ref, count_ref, acc_ref):
    lanes = cells_ref.shape[1]
    row = lax.broadcasted_iota(jnp.int32, (G, CHUNK), 0)
    acc_ref[...] = jnp.zeros_like(acc_ref)

    def body(j, carry):
        part = pl.ds(pl.multiple_of(j * CHUNK, CHUNK), CHUNK)
        mass = mass_ref[0:1, part]
        pieces = split3(mass)
        for s in range(STEPS):
            cell = cells_ref[s : s + 1, part]
            hit_x = row == (cell >> 6)
            hit_y = jnp.where(row == (cell & (G - 1)), 1.0, 0.0).astype(BF16)
            left = jnp.concatenate(
                [jnp.where(hit_x, piece, 0.0).astype(BF16) for piece in pieces], axis=0
            )
            acc_ref[s] += dot(left, hit_y, NT)
        return carry

    lax.fori_loop(0, lanes // CHUNK, body, 0)
    both = []
    for s in range(STEPS):
        both.append(acc_ref[s, 0:G] + acc_ref[s, G : 2 * G] + acc_ref[s, 2 * G : 3 * G])
    whole = jnp.concatenate(both, axis=1)
    for d in range(dens_ref.shape[0]):
        dens_ref[d] = whole

    for d in range(count_ref.shape[0]):
        count_ref[d] = 0

    def slot(t, carry):
        d = dest_ref[t]
        k = count_ref[d]
        target_ref[t] = d * SLOT + k
        count_ref[d] = k + 1
        return carry

    lax.fori_loop(0, TILES, slot, 0)


def densities(cells, mass, dest, copies, azi_count):
    return pl.pallas_call(
        density_kernel,
        in_specs=[VMEM, VMEM, SMEM],
        out_specs=[VMEM, SMEM],
        out_shape=[
            jax.ShapeDtypeStruct((copies, G, 2 * G), F32),
            jax.ShapeDtypeStruct((TILES,), jnp.int32),
        ],
        scratch_shapes=[
            pltpu.SMEM((azi_count,), jnp.int32),
            pltpu.VMEM((STEPS, 3 * G, G), F32),
        ],
        compiler_params=params(),
        cost_estimate=cost(7),
        name="densities",
    )(cells, mass, dest)


def dot3(a_high, a_low, b, dims=NN):
    b_high, b_low = split2(b)
    return dot(a_high, b_high, dims) + dot(a_high, b_low, dims) + dot(a_low, b_high, dims)


def forward_x_kernel(place_ref, high_ref, low_ref, dens_ref, out_ref):
    values = dens_ref[...].reshape(-1, 2 * G)
    lines = dot3(high_ref[0, 1 : G + 1], low_ref[0, 1 : G + 1], values)
    turned = lines.T
    whole = jnp.concatenate([turned[0:G], turned[G : 2 * G]], axis=1)
    for d in range(out_ref.shape[0]):
        out_ref[d] = whole


def solve_y_kernel(place_ref, high_ref, low_ref, some_high_ref, some_low_ref, lam_y_ref, lam_x_ref, in_ref, out_ref):
    values = in_ref[...].reshape(-1, 2 * G)
    lam_x = lam_x_ref[0, 0:1, :]
    mean = jnp.sum(values, axis=0, keepdims=True) * (1.0 / values.shape[0])
    values = values - jnp.where(lam_x == 0.0, mean, 0.0)
    modes = dot3(high_ref[...], low_ref[...], values)
    lam = lam_y_ref[...] + lam_x
    at_zero = lam == 0.0
    modes = modes * jnp.where(at_zero, 0.0, -GRAV / jnp.where(at_zero, 1.0, lam))
    lines = dot3(some_high_ref[0], some_low_ref[0], modes)
    inner = lines[1 : G + 1].T
    first = jnp.concatenate([inner[0:G], inner[G : 2 * G]], axis=1)
    for d in range(out_ref.shape[0]):
        out_ref[d, 0:G] = first
        out_ref[d, G : G + 8] = jnp.zeros((8, 2 * G), F32)
        out_ref[d, G : G + 1] = lines[0:1]
        out_ref[d, G + 1 : G + 2] = lines[G + 1 : G + 2]


def inverse_x_kernel(place_ref, high_ref, low_ref, in_ref, grad_ref, pot_ref, all_ref, halo_ref, turn_ref):
    count = in_ref.shape[0]
    halo_ref[...] = jnp.zeros_like(halo_ref)
    for d in range(count):
        all_ref[d * G : (d + 1) * G] = in_ref[d, 0:G]
        halo_ref[:, d * G : (d + 1) * G] = in_ref[d, G : G + 8, 0:G]
    grid = dot3(high_ref[0], low_ref[0], all_ref[...])
    pot_ref[...] = grid[1 : G + 1, G : 2 * G]
    b_high, b_low = split2(halo_ref[...])
    a_high, a_low = high_ref[0, 1 : G + 1], low_ref[0, 1 : G + 1]
    sides = dot(b_high, a_high, NT) + dot(b_low, a_high, NT) + dot(b_high, a_low, NT)
    grad_x = -(grid[2 : G + 2, 0:G] - grid[0:G, 0:G]) * 0.5
    turn_ref[8 : G + 8] = grid[1 : G + 1, 0:G].T
    turn_ref[7:8] = sides[0:1]
    turn_ref[G + 8 : G + 9] = sides[1:2]
    grad_y = (-(turn_ref[9 : G + 9] - turn_ref[7 : G + 7]) * 0.5).T
    write_gradient(grad_ref, grad_x, grad_y)


def write_gradient(grad_ref, grad_x, grad_y):
    for c, part in enumerate((grad_x, grad_y)):
        for p, piece in enumerate(split3(part)):
            grad_ref[c * G : (c + 1) * G, p * G : (p + 1) * G] = piece


def placed_block(shape):
    return pl.BlockSpec((1,) + shape, lambda i, place: (place[0],) + (0,) * len(shape))


def whole_block(shape):
    return pl.BlockSpec(shape, lambda i, place: (0,) * len(shape))


def placed_call(kernel, name, place, ins, outs, scratch=(), us=3):
    in_specs = [placed_block(a.shape[1:]) if by else whole_block(a.shape) for a, by in ins]
    return pl.pallas_call(
        kernel,
        grid_spec=pltpu.PrefetchScalarGridSpec(
            num_scalar_prefetch=1,
            grid=(1,),
            in_specs=in_specs,
            out_specs=[whole_block(o.shape) for o in outs],
            scratch_shapes=list(scratch),
        ),
        out_shape=list(outs),
        compiler_params=params(),
        cost_estimate=cost(us),
        name=name,
    )(place, *[a for a, _ in ins])


def exchange(value, axis):
    return lax.all_to_all(value, axis, split_axis=0, concat_axis=0, tiled=True)


def old_gradient(pot_ref, up_ref, down_ref, right_ref, left_ref, grad_ref, turn_ref):
    pot = pot_ref[...]
    turn_ref[8 : G + 8] = pot
    turn_ref[7:8] = up_ref[0:1, EW : EW + G]
    turn_ref[G + 8 : G + 9] = down_ref[0:1, EW : EW + G]
    grad_x = -(turn_ref[9 : G + 9] - turn_ref[7 : G + 7]) * 0.5
    turn_ref[8 : G + 8] = pot.T
    turn_ref[7:8] = right_ref[0:1, EW : EW + G]
    turn_ref[G + 8 : G + 9] = left_ref[0:1, EW : EW + G]
    grad_y = (-(turn_ref[9 : G + 9] - turn_ref[7 : G + 7]) * 0.5).T
    write_gradient(grad_ref, grad_x, grad_y)


def features(pos, mass, work_ref, i_ref, j_ref, r_ref, lanes, own):
    width = pos.shape[1]
    q = pos - 0.5
    norm = -CEXP * jnp.sum(q * q, axis=0, keepdims=True)
    one = jnp.ones_like(norm)
    n_high, n_mid, n_low = split3(norm)
    q_high, q_mid, q_low = split3(q)
    zero = jnp.zeros((8, width), F32)

    def write(groups, target_ref):
        for k, (three, last) in enumerate(groups):
            work_ref[4 * k : 4 * k + 3, 0:width] = three
            work_ref[4 * k + 3 : 4 * k + 4, 0:width] = last
        work_ref[24:32, 0:width] = zero
        target_ref[:, lanes] = work_ref[0:32, 0:width].astype(BF16)

    write(
        (
            (q_high, one),
            (q_mid, n_mid),
            (q_high, one),
            (q_low, n_low),
            (q_high, one),
            (q_mid, n_high),
        ),
        j_ref,
    )
    if own:
        a_high, a_mid, a_low = split3(q * (2.0 * CEXP))
        write(
            (
                (a_high, n_high),
                (a_high, one),
                (a_mid, n_mid),
                (a_high, one),
                (a_low, n_low),
                (a_mid, one),
            ),
            i_ref,
        )
    weighted = q * mass
    w_high = weighted.astype(BF16).astype(F32)
    m_high = mass.astype(BF16).astype(F32)
    work_ref[0:3, 0:width] = w_high
    work_ref[3:4, 0:width] = m_high
    work_ref[4:7, 0:width] = weighted - w_high
    work_ref[7:8, 0:width] = mass - m_high
    work_ref[8:16, 0:width] = zero
    r_ref[:, lanes] = work_ref[0:16, 0:width].astype(BF16)


def step_kernel(last, *refs):
    if last:
        (ints_ref, nbr_ref, target_ref, pos_ref, vel_ref, mass_ref, cells_ref, far_ref, right_ref, left_ref,
         grad_in_ref, pack_ref, i_ref, j_ref, r_ref, work_ref, grad_ref) = refs
    else:
        (ints_ref, nbr_ref, target_ref, pos_ref, vel_ref, mass_ref, cells_ref, far_ref, right_ref, left_ref,
         up_ref, down_ref, pot_ref, new_pos_ref, new_vel_ref, up_out, down_out, right_out, left_out, pack_ref,
         i_ref, j_ref, r_ref, work_ref, grad_ref, turn_ref, split_ref) = refs
    if last:
        grad_ref[...] = grad_in_ref[...].astype(BF16)
    else:
        old_gradient(pot_ref, up_ref, down_ref, right_ref, left_ref, split_ref, turn_ref)
        grad_ref[...] = split_ref[...].astype(BF16)
    pack_ref[...] = jnp.zeros_like(pack_ref)
    own_lanes = TILES * T

    def prepare(j, carry):
        lanes = pl.ds(pl.multiple_of(j * CHUNK, CHUNK), CHUNK)
        features(pos_ref[0:3, lanes], mass_ref[0:1, lanes], work_ref, i_ref, j_ref, r_ref, lanes, True)
        return carry

    lax.fori_loop(0, own_lanes // CHUNK, prepare, 0)

    below = far_ref[ints_ref[0], 0:4, :]
    above = far_ref[ints_ref[1], 4:8, :]
    sub = lax.broadcasted_iota(jnp.int32, (3, EW), 0)
    for e, (ghost, axis, move) in enumerate(
        ((below, 0, -1.0), (above, 0, 1.0), (right_ref[0:4, 0:EW], 1, -1.0), (left_ref[0:4, 0:EW], 1, 1.0))
    ):
        place = ghost[0:3] + jnp.where(sub == axis, move, 0.0)
        lanes = slice(own_lanes + e * EW, own_lanes + (e + 1) * EW)
        features(place, ghost[3:4], work_ref, i_ref, j_ref, r_ref, lanes, False)

    strip_x = ints_ref[2].astype(F32)
    row = lax.broadcasted_iota(jnp.int32, (G, T), 0)

    def tile(t, carry):
        own = pl.ds(pl.multiple_of(t * T, T), T)
        picks = [pl.ds(pl.multiple_of(nbr_ref[t, n] * T, T), T) for n in range(LINKS)]
        others = jnp.concatenate([j_ref[:, p] for p in picks], axis=1)
        right = jnp.concatenate([r_ref[:, p] for p in picks], axis=1)
        weights = jnp.exp2(dot(i_ref[:, own], others, TN)).astype(BF16)
        sums = dot(right, weights, NT)
        pos = pos_ref[0:3, own]
        vel = vel_ref[0:3, own]
        total = sums[0:4] + sums[4:8]
        contact = STIFF * ((pos - 0.5) * total[3:4] - total[0:3])
        cell = cells_ref[last : last + 1, own]
        hit_y = jnp.where(row == (cell & (G - 1)), 1.0, 0.0).astype(BF16)
        hit_x = row == (cell >> 6)
        field = dot(grad_ref[...], jnp.concatenate([hit_y] * 3, axis=0))
        grav_x = jnp.sum(jnp.where(hit_x, field[0:G], 0.0), axis=0, keepdims=True)
        grav_y = jnp.sum(jnp.where(hit_x, field[G : 2 * G], 0.0), axis=0, keepdims=True)
        acc_x = contact[0:1] + grav_x + 2.0 * OMEGA * vel[1:2] + 3.0 * OMEGA**2 * (pos[0:1] + strip_x)
        acc_y = contact[1:2] + grav_y - 2.0 * OMEGA * vel[0:1]
        acc_z = contact[2:3] - OMEGA**2 * (pos[2:3] - 0.5)
        speed = vel + DT * jnp.concatenate([acc_x, acc_y, acc_z], axis=0)
        target = target_ref[t]
        d = target // SLOT
        k = target % SLOT
        if last:
            for c in range(3):
                pack_ref[d, pl.ds(k * 3 + c, 1), :] = speed[c : c + 1]
        else:
            place = pos + DT * speed
            new_pos_ref[0:3, own] = place
            new_vel_ref[0:3, own] = speed
            pack_ref[d, k, 0:3, :] = place
            pack_ref[d, k, 3:4, :] = mass_ref[0:1, own]
        return carry

    lax.fori_loop(0, TILES, tile, 0, unroll=4)
    if not last:
        for ref, part in ((up_out, 1), (down_out, 0), (right_out, 3), (left_out, 2)):
            lanes = slice(part * EW, (part + 1) * EW)
            ref[0:3, :] = new_pos_ref[0:3, lanes]
            ref[3:4, :] = mass_ref[0:1, lanes]


def step(last, ints, nbr, target, pos, vel, mass, cells, far, right, left, more, azi_count):
    lanes = TILES * T
    if last:
        outs = [jax.ShapeDtypeStruct((azi_count, SLOT * 3, T), F32)]
        out_specs = [VMEM]
    else:
        outs = [jax.ShapeDtypeStruct((3, lanes), F32)] * 2 + [jax.ShapeDtypeStruct((4, EW), F32)] * 4
        outs += [jax.ShapeDtypeStruct((azi_count, SLOT, 4, T), F32)]
        out_specs = [VMEM] * 7
    scratch = [
        pltpu.VMEM((32, lanes), BF16),
        pltpu.VMEM((32, lanes + GHOSTS * T), BF16),
        pltpu.VMEM((16, lanes + GHOSTS * T), BF16),
        pltpu.VMEM((32, CHUNK), F32),
        pltpu.VMEM((2 * G, 3 * G), BF16),
    ]
    if not last:
        scratch += [pltpu.VMEM((G + 16, G), F32), pltpu.VMEM((2 * G, 3 * G), F32)]
    return pl.pallas_call(
        functools.partial(step_kernel, last),
        in_specs=[SMEM] * 3 + [VMEM] * (7 + len(more)),
        out_specs=out_specs,
        out_shape=outs,
        scratch_shapes=scratch,
        compiler_params=params(),
        cost_estimate=cost(20),
        name=f"step_{last}",
    )(ints, nbr, target, pos, vel, mass, cells, far, right, left, *more)


def assemble_kernel(azi_count, ints_ref, place_ref, speed_ref, out_ref):
    b = ints_ref[3]

    def group(g, carry):
        a = g // (SLOT // 8)
        h = g % (SLOT // 8)
        signed = lax.rem(a - b + azi_count // 2 + azi_count, azi_count) - azi_count // 2
        move = signed.astype(F32)
        speeds = speed_ref[a, pl.ds(pl.multiple_of(h * 24, 8), 24), :]
        sub = lax.broadcasted_iota(jnp.int32, (3, T), 0)
        for k in range(8):
            four = place_ref[a, h * 8 + k]
            speed = speeds[3 * k : 3 * k + 3]
            mass = four[3:4]
            place = four[0:3] + DT * speed
            place = place + jnp.where((sub == 1) & (mass > 0.0), move, 0.0)
            lanes = pl.ds(pl.multiple_of((g * 8 + k) * T, T), T)
            out_ref[0:3, lanes] = place
            out_ref[3:6, lanes] = speed
            out_ref[6:7, lanes] = mass
        return carry

    lax.fori_loop(0, azi_count * SLOT // 8, group, 0)


def assemble(ints, place, speed):
    azi_count = place.shape[0]
    return pl.pallas_call(
        functools.partial(assemble_kernel, azi_count),
        in_specs=[SMEM, VMEM, VMEM],
        out_specs=VMEM,
        out_shape=jax.ShapeDtypeStruct((7, azi_count * SLOT * T), F32),
        compiler_params=params(),
        cost_estimate=cost(4),
        name="assemble",
    )(ints, place, speed)


def shifted(value, axis, steps):
    count = lax.axis_size(axis)
    return lax.ppermute(value, axis, [(i, (i + steps) % count) for i in range(count)])


def local(positions, velocities, masses, neighbours, shear_offsets, destinations, deposit_cells, old_potential):
    rad_count = lax.axis_size("rad")
    azi_count = lax.axis_size("azi")
    r = lax.axis_index("rad")
    a = lax.axis_index("azi")
    mass = masses.reshape(1, -1)
    r_place = r.reshape(1).astype(jnp.int32)
    a_place = a.reshape(1).astype(jnp.int32)

    def ints(s):
        below = (a - shear_offsets[s, r]) % azi_count
        above = (a + shear_offsets[s, (r + 1) % rad_count]) % azi_count
        return jnp.stack([below, above, r - rad_count // 2, a]).astype(jnp.int32)

    def ghosts(up, down, right, left):
        up = shifted(up, "rad", 1)
        down = shifted(down, "rad", -1)
        right = shifted(right, "azi", 1)
        left = shifted(left, "azi", -1)
        both = jnp.concatenate([up[:, :EW], down[:, :EW]], axis=0)
        far = exchange(jnp.broadcast_to(both[None], (azi_count,) + both.shape), "azi")
        return far, up, down, right, left

    first, second = ints(0), ints(1)
    up, down, right, left = edges(positions, mass, old_potential)
    far, up, down, right, left = ghosts(up, down, right, left)

    dens, target = densities(deposit_cells, mass, destinations, rad_count, azi_count)
    high_x, low_x, rows_high_x, rows_low_x, lam_x = tables(G * rad_count, rad_count)
    high_y, low_y, rows_high_y, rows_low_y, lam_y = tables(G * azi_count, azi_count)
    lam_cols = np.tile(lam_x.reshape(rad_count, 1, G), (1, 8, 2))
    lam_rows = np.ascontiguousarray(np.broadcast_to(lam_y[:, None], (G * azi_count, 2 * G)))
    dens = exchange(dens, "rad")
    (lines,) = placed_call(
        forward_x_kernel, "forward_x", r_place,
        ((jnp.asarray(rows_high_x), True), (jnp.asarray(rows_low_x), True), (dens, False)),
        (jax.ShapeDtypeStruct((azi_count, G, 2 * G), F32),),
    )
    lines = exchange(lines, "azi")
    at = jnp.stack([r, a]).astype(jnp.int32)
    some = lambda table: pl.BlockSpec((1,) + table.shape[1:], lambda i, place: (place[1], 0, 0))
    (solved,) = pl.pallas_call(
        solve_y_kernel,
        grid_spec=pltpu.PrefetchScalarGridSpec(
            num_scalar_prefetch=1,
            grid=(1,),
            in_specs=[
                whole_block(high_y.shape), whole_block(low_y.shape), some(rows_high_y), some(rows_low_y),
                whole_block(lam_rows.shape), placed_block(lam_cols.shape[1:]), whole_block(lines.shape),
            ],
            out_specs=[whole_block((rad_count, G + 8, 2 * G))],
        ),
        out_shape=[jax.ShapeDtypeStruct((rad_count, G + 8, 2 * G), F32)],
        compiler_params=params(),
        cost_estimate=cost(6),
        name="solve_y",
    )(at, high_y, low_y, rows_high_y, rows_low_y, lam_rows, lam_cols, lines)
    solved = exchange(solved, "rad")
    gradient, potential = placed_call(
        inverse_x_kernel, "inverse_x", r_place,
        ((jnp.asarray(rows_high_x), True), (jnp.asarray(rows_low_x), True), (solved, False)),
        (jax.ShapeDtypeStruct((2 * G, 3 * G), F32), jax.ShapeDtypeStruct((G, G), F32)),
        (pltpu.VMEM((G * rad_count, 2 * G), F32), pltpu.VMEM((8, G * rad_count), F32), pltpu.VMEM((G + 16, G), F32)),
    )

    place, speed, up_1, down_1, right_1, left_1, pack_place = step(
        0, first, neighbours, target, positions, velocities, mass, deposit_cells, far, right, left,
        (up, down, old_potential), azi_count,
    )
    far_1, _, _, right_1, left_1 = ghosts(up_1, down_1, right_1, left_1)
    pack_place = exchange(pack_place, "azi")
    (pack_speed,) = step(
        1, second, neighbours, target, place, speed, mass, deposit_cells, far_1, right_1, left_1,
        (gradient,), azi_count,
    )
    pack_speed = exchange(pack_speed, "azi")
    return assemble(second, pack_place, pack_speed), potential


def solution(mesh):
    placed = (
        P(None, ("rad", "azi")),
        P(None, ("rad", "azi")),
        P(("rad", "azi")),
        P(("rad", "azi"), None),
        P(),
        P(("rad", "azi")),
        P(None, ("rad", "azi")),
        P("rad", "azi"),
    )
    return jax.shard_map(
        local,
        mesh=mesh,
        in_specs=placed,
        out_specs=(P(None, ("rad", "azi")), P("rad", "azi")),
        check_vma=False,
    )
```

time: 849 us -> 213 us (0.25); the launches traced: 839 us -> 212 us
  other arithmetic: 275 us -> 0.25 us
  local copies, waits for them, and re-layouts: 234 us -> 13 us
  waiting for transfers between devices: 119 us -> 22.2 us
  Pallas kernels: 0 us -> 84.7 us
  starting transfers between devices: 107 us -> 57.1 us
  blocking collectives: 80.2 us -> 31.4 us
  matrix products: 12.5 us -> 0 us
    scatter-add x8 -> x0, other arithmetic: 172 us -> none  [the longest x2 172 us: local(): jax.ops.segment_sum(masses, cells_now, num_segments=grid_x * grid_y)]
    gather x68 -> x0, local copies, waits for them, and re-layouts: 157 us -> none  [the longest x4 120 us: local(): gravity = jnp.take(grad_field, cells_now, axis=1)]
    all_to_all x17 -> x6, waiting for transfers between devices: 108 us -> 14.4 us  [exchange(): return lax.all_to_all(value, axis, split_axis=0, concat_axis=0, tiled=True)]
    pallas_call x0 -> x8, Pallas kernels: none -> 84.7 us  [the longest x2 64.2 us: step(): pl.pallas_call(functools.partial(step_kernel, last), in_specs=[SMEM] * 3...]
    all_gather x2 -> x0, blocking collectives: 80.2 us -> none  [ghost_table(): all_rows = lax.all_gather(stacked[None], 'azi', axis=0, tiled=True)]
    reduce_sum x129 -> x0, other arithmetic: 69.5 us -> none  [the longest x64 44.9 us: one_group(): return CONTACT_STIFF * jnp.sum(offsets * weights[None], axis=(2, 4))]
    all_to_all x17 -> x6, starting transfers between devices: 85.5 us -> 45.3 us  [exchange(): return lax.all_to_all(value, axis, split_axis=0, concat_axis=0, tiled=True)]
    all_to_all x0 -> x1, blocking collectives: none -> 31.4 us  [exchange(): return lax.all_to_all(value, axis, split_axis=0, concat_axis=0, tiled=True)]
  transfers between devices with their start and end apart: 33 -> 14, of which waited for: 18 -> 6; matrix products, arithmetic and copies ran while one was open for 48% -> 0% of each run, Pallas kernels for 0% -> 34%
where the time goes in v1:
time: 213 us; the launch traced here: 212 us
  Pallas kernels  84.7 us (40%)
  starting transfers between devices  57.1 us (27%)
  blocking collectives  31.4 us (15%)
  waiting for transfers between devices  22.2 us (10%)
  local copies, waits for them, and re-layouts  13 us (6%)
  between operations  3.26 us (2%)
    pallas_call x2, Pallas kernels, step(): pl.pallas_call(functools.partial(step_kernel, last), in_specs=[SMEM] * 3...  64.2 us
    all_to_all x6, starting transfers between devices, exchange(): return lax.all_to_all(value, axis, split_axis=0, concat_axis=0, tiled=True)  45.3 us
    all_to_all x1, blocking collectives, exchange(): return lax.all_to_all(value, axis, split_axis=0, concat_axis=0, tiled=True)  31.4 us
    all_to_all x6, waiting for transfers between devices, exchange(): return lax.all_to_all(value, axis, split_axis=0, concat_axis=0, tiled=True)  14.4 us
    ppermute x8, starting transfers between devices, shifted(): lax.ppermute(value, axis, [(i, (i + steps) % count) for i in range(count)])  11.8 us
    unnamed x35, local copies, waits for them, and re-layouts  10.9 us
    pallas_call x1, Pallas kernels, densities(): pl.pallas_call(density_kernel, in_specs=[VMEM, VMEM, SMEM], out_specs=[VM...  8.32 us
    ppermute x8, waiting for transfers between devices, shifted(): lax.ppermute(value, axis, [(i, (i + steps) % count) for i in range(count)])  7.87 us
  transfers between devices with their start and end apart: 14, of which 6 were waited for; matrix products, arithmetic and copies ran while one was open for 0% of the time, Pallas kernels for 34%

profile of v1, /device:TPU:32, one launch (start us, length us, event | category | flops | bytes accessed | tf_op | source)
XLA Modules:
  0.0 212.0 jit_solution(5281612807470639417)
XLA Ops:
  0.6 0.0 copy-start.2
  0.6 0.9 copy-done.2
  1.5 0.8 copy-done.4
  2.4 0.7 copy-done.7
  3.0 8.3 %densities.1 = (f32[16,64,128]{2,1,0:T(8,128)}, s32[128]{0:T(128)S(1)}) custom-call(s32[2,16384]{1,0:T(2,128)S(1)} %copy-done.2, f32[1,16384]{1,0:T(1,128)S(1)} %bitcast.12, s32[128]{0:T(128)S(1)} %copy-done.7), custom_call_target="tpu_custom_call" | custom-call | flops 7000000000 | bytes 21000000 | tf_op jit(solution)/shard_map/densities/pallas_call | solution.py:150
  11.4 5.5 %all-to-all-start.3 = ((f32[16,64,128]{2,1,0:T(8,128)}), f32[16,64,128]{2,1,0:T(8,128)S(1)}, u32[]{:S(2)}, u32[]{:S(2)}) async-start(f32[16,64,128]{2,1,0:T(8,128)} %get-tuple-element.29), calls=%async_computation.3 | async-start | bytes 1048576 | tf_op jit(solution)/shard_map/all_to_all | solution.py:253
  16.9 0.1 edges.1
  17.0 0.4 collective-permute-start
  17.5 3.5 %collective-permute-start.1 = (f32[4,640]{1,0:T(4,128)S(1)}, f32[4,640]{1,0:T(4,128)S(1)}, u32[]{:S(2)}, u32[]{:S(2)}) collective-permute-start(f32[4,640]{1,0:T(4,128)S(1)} %get-tuple-element.19), channel_id=1, source_target_pairs={{0,240},{16,0},{32,16},{48,32},{64,48},{80,64},{96,80},{112,96},{1... | collective-permute-start | bytes 30728 | tf_op jit(solution)/shard_map/ppermute | solution.py:469
  20.9 6.6 %collective-permute-done.refs_10_ = f32[4,640]{1,0:T(4,128)S(1)} collective-permute-done((f32[4,640]{1,0:T(4,128)S(1)}, f32[4,640]{1,0:T(4,128)S(1)}, u32[]{:S(2)}, u32[]{:S(2)}) %collective-permute-start) | collective-permute-done | bytes 10272 | tf_op jit(solution)/shard_map/ppermute | solution.py:469
  27.5 0.3 all-to-all-done.3.dens_ref
  27.9 0.7 broadcast_in_dim.4
  28.6 10.8 %all-to-all-start = ((f32[16,8,512]{2,1,0:T(8,128)}), f32[16,8,512]{2,1,0:T(8,128)S(1)}, u32[]{:S(2)}, u32[]{:S(2)}) async-start(f32[16,8,512]{2,1,0:T(8,128)} %broadcast_in_dim.4), calls=%async_computation | async-start | bytes 524288 | tf_op jit(solution)/shard_map/all_to_all | solution.py:253
  39.3 1.5 collective-permute-start.2
  40.8 0.6 collective-permute-start.3
  41.4 0.6 constant_dynamic-slice_fusion.1
  43.3 0.1 copy.16.refs_1_
  43.4 0.1 add_add_fusion.1.refs_0_
  43.5 1.7 copy-done.9
  45.2 2.2 %forward_x.1 = f32[16,64,128]{2,1,0:T(8,128)} custom-call(s32[1]{0:T(128)} %bitcast.11.place_ref, bf16[16,80,1024]{2,1,0:T(8,128)(2,1)S(1)} %copy-done.9, bf16[16,80,1024]{2,1,0:T(8,128)(2,1)} %constant.57.clone.low_ref.some_low_ref, f32[16,64,128]{2,1,0:T(8,128)S(1)} %all-to-all-done.3.dens_ref), custom_call_target="tpu_custom_call" | custom-call | flops 3000000000 | bytes 9000000 | tf_op jit(solution)/shard_map/forward_x/pallas_call | solution.py:236
  47.4 3.3 %all-to-all-done.refs_7_ = f32[16,8,512]{2,1,0:T(8,128)S(1)} async-done(((f32[16,8,512]{2,1,0:T(8,128)}), f32[16,8,512]{2,1,0:T(8,128)S(1)}, u32[]{:S(2)}, u32[]{:S(2)}) %all-to-all-start) | async-done | bytes 262176 | tf_op jit(solution)/shard_map/all_to_all | solution.py:253
  50.7 7.6 %all-to-all-start.4 = ((f32[16,64,128]{2,1,0:T(8,128)}), f32[16,64,128]{2,1,0:T(8,128)S(1)}, u32[]{:S(2)}, u32[]{:S(2)}) async-start(f32[16,64,128]{2,1,0:T(8,128)} %forward_x.1), calls=%async_computation.4 | async-start | bytes 1048576 | tf_op jit(solution)/shard_map/all_to_all | solution.py:253
  58.3 0.0 copy-start.13
  58.3 0.0 copy-start.14
  58.3 32.7 %step_0.1 = (f32[3,16384]{1,0:T(4,128)S(1)}, f32[3,16384]{1,0:T(4,128)S(1)}, f32[4,512]{1,0:T(4,128)S(1)}, f32[4,512]{1,0:T(4,128)S(1)}, f32[4,512]{1,0:T(4,128)...) custom-call(s32[4]{0:T(128)S(1)} %add_add_fusion.1.refs_0_, s32[128,4]{1,0:T(8,128)S(1)} %copy.16.refs_1_, ...), custom_call_target="tpu_custom_call" | custom-call | flops 20000000000 | bytes 60000000 | tf_op jit(solution)/shard_map/step_0/pallas_call | solution.py:417
  91.1 3.9 %collective-permute-start.5 = (f32[4,512]{1,0:T(4,128)S(1)}, f32[4,512]{1,0:T(4,128)S(1)}, u32[]{:S(2)}, u32[]{:S(2)}) collective-permute-start(f32[4,512]{1,0:T(4,128)S(1)} %get-tuple-element.26), channel_id=1, source_target_pairs={{0,240},{16,0},{32,16},{48,32},{64,48},{80,64},{96,80},{112,96},{1... | collective-permute-start | bytes 24584 | tf_op jit(solution)/shard_map/ppermute | solution.py:469
  94.9 0.1 pad_add_fusion.place_ref
  95.0 1.3 collective-permute-done.4
  96.3 0.0 collective-permute-done.5
  96.3 0.7 broadcast_in_dim.5
  97.0 9.6 %all-to-all-start.2 = ((f32[16,8,512]{2,1,0:T(8,128)}), f32[16,8,512]{2,1,0:T(8,128)S(1)}, u32[]{:S(2)}, u32[]{:S(2)}) async-start(f32[16,8,512]{2,1,0:T(8,128)} %broadcast_in_dim.5), calls=%async_computation.2 | async-start | bytes 524288 | tf_op jit(solution)/shard_map/all_to_all | solution.py:253
  106.7 0.0 copy-start.11
  106.7 1.6 copy-done.11
  108.3 1.6 copy-done.12
  109.9 4.9 %solve_y.1 = f32[16,72,128]{2,1,0:T(8,128)} custom-call(s32[2]{0:T(128)S(1)} %pad_add_fusion.place_ref, bf16[1024,1024]{1,0:T(8,128)(2,1)S(1)} %copy-done.12, bf16[1024,1024]{1,0:T(8,128)(2,1)S(1)} %copy-done.11, bf16[16,80,1024]{2,1,0:T(8,128)(2,1)} %constant.56.clone.high_ref.some_high_ref, bf16[16,80,1024]{2,1,0:T(8,128)(2,1)} %constant.57.clone.low_ref.some_low_ref, ...), custom_call_target="tpu_custom_call" | custom-call | flops 6000000000 | bytes 18000000 | tf_op jit(solution)/shard_map/solve_y/pallas_call | solution.py:513
  114.8 2.5 %all-to-all-done.2.refs_7_ = f32[16,8,512]{2,1,0:T(8,128)S(1)} async-done(((f32[16,8,512]{2,1,0:T(8,128)}), f32[16,8,512]{2,1,0:T(8,128)S(1)}, u32[]{:S(2)}, u32[]{:S(2)}) %all-to-all-start.2) | async-done | bytes 262176 | tf_op jit(solution)/shard_map/all_to_all | solution.py:253
  117.3 3.6 %all-to-all-start.5 = ((f32[16,72,128]{2,1,0:T(8,128)}), f32[16,72,128]{2,1,0:T(8,128)S(1)}, u32[]{:S(2)}, u32[]{:S(2)}) async-start(f32[16,72,128]{2,1,0:T(8,128)} %solve_y.1), calls=%async_computation.5 | async-start | bytes 1179648 | tf_op jit(solution)/shard_map/all_to_all | solution.py:253
  122.1 0.1 add_add_fusion.refs_0_.ints_ref
  122.2 0.4 collective-permute-start.6
  122.6 1.6 collective-permute-start.7
  124.2 8.3 %all-to-all-done.5.in_ref = f32[16,72,128]{2,1,0:T(8,128)S(1)} async-done(((f32[16,72,128]{2,1,0:T(8,128)}), f32[16,72,128]{2,1,0:T(8,128)S(1)}, u32[]{:S(2)}, u32[]{:S(2)}) %all-to-all-start.5) | async-done | bytes 589856 | tf_op jit(solution)/shard_map/all_to_all | solution.py:253
  132.5 8.2 %all-to-all-start.1 = ((f32[16,32,4,128]{3,2,1,0:T(4,128)}), f32[16,32,4,128]{3,2,1,0:T(4,128)S(1)}, u32[]{:S(2)}, u32[]{:S(2)}) async-start(f32[16,32,4,128]{3,2,1,0:T(4,128)} %get-tuple-element.22), calls=%async_computation.1 | async-start | bytes 2097152 | tf_op jit(solution)/shard_map/all_to_all | solution.py:253
  140.7 1.7 copy-done.8
  142.4 1.7 copy-done.10
  144.2 1.2 inverse_x.1
  145.4 31.5 %step_1.1 = f32[16,96,128]{2,1,0:T(8,128)S(1)} custom-call(s32[4]{0:T(128)S(1)} %add_add_fusion.refs_0_.ints_ref, s32[128,4]{1,0:T(8,128)S(1)} %copy.16.refs_1_, s32[128]{0:T(128)S(1)} %get-tuple-element.17.refs_2_, f32[3,16384]{1,0:T(4,128)S(1)} %get-tuple-element.23.refs_3_, f32[3,16384]{1,0:T(4,128)S(1)} %get-tuple-element.24.refs_4_, ...), custom_call_target="tpu_custom_call" | custom-call | flops 20000000000 | bytes 60000000 | tf_op jit(solution)/shard_map/step_1/pallas_call | solution.py:417
  176.8 31.4 %all_to_all.35.speed_ref = f32[16,96,128]{2,1,0:T(8,128)S(1)} all-to-all(f32[16,96,128]{2,1,0:T(8,128)S(1)} %step_1.1), channel_id=1, replica_groups=mesh['rad'=16,'azi'=16] {'azi'}, dimensions={0} | all-to-all | bytes 1572864 | tf_op jit(solution)/shard_map/all_to_all | solution.py:253
  208.3 3.7 %assemble.1 = f32[7,65536]{1,0:T(8,128)} custom-call(s32[4]{0:T(128)S(1)} %add_add_fusion.refs_0_.ints_ref, f32[16,32,4,128]{3,2,1,0:T(4,128)S(1)} %all-to-all-done.1.place_ref, f32[16,96,128]{2,1,0:T(8,128)S(1)} %all_to_all.35.speed_ref), custom_call_target="tpu_custom_call" | custom-call | flops 4000000000 | bytes 12000000 | tf_op jit(solution)/shard_map/assemble/pallas_call | solution.py:456
  (34 shorter events, 0.1 us)
Async XLA Ops:
  0.6 0.9 copy-start.2
  1.5 0.8 copy-start.4
  2.4 0.7 copy-start.7
  3.0 13.9 %copy-start = (f32[3,16384]{1,0:T(4,128)S(1)}, f32[3,16384]{1,0:T(4,128)}, u32[]{:S(2)}) copy-start(f32[3,16384]{1,0:T(4,128)} %refs_3_.1) | copy-start | bytes 589828
  3.0 13.9 %copy-start.5 = (f32[16384]{0:T(1024)S(1)}, f32[16384]{0:T(1024)}, u32[]{:S(2)}) copy-start(f32[16384]{0:T(1024)} %param.16) | copy-start | bytes 196612
  3.0 13.9 %copy-start.6 = (f32[64,64]{1,0:T(8,128)S(1)}, f32[64,64]{1,0:T(8,128)}, u32[]{:S(2)}) copy-start(f32[64,64]{1,0:T(8,128)} %refs_12_.1) | copy-start | bytes 49156
  11.4 16.5 %all-to-all-start.3 = ((f32[16,64,128]{2,1,0:T(8,128)}), f32[16,64,128]{2,1,0:T(8,128)S(1)}, u32[]{:S(2)}, u32[]{:S(2)}) async-start(f32[16,64,128]{2,1,0:T(8,128)} %get-tuple-element.29), calls=%async_computation.3 | async-start | bytes 1048576 | tf_op jit(solution)/shard_map/all_to_all | solution.py:253
  16.9 24.5 %copy-start.15 = (s32[2,16]{1,0:T(2,128)S(1)}, s32[2,16]{1,0:T(2,128)}, u32[]{:S(2)}) copy-start(s32[2,16]{1,0:T(2,128)} %param.18) | copy-start | bytes 388
  16.9 26.3 %copy-start.16 = (s32[128,4]{0,1:T(4,128)S(1)}, s32[128,4]{0,1:T(4,128)}, u32[]{:S(2)}) copy-start(s32[128,4]{0,1:T(4,128)} %param.17) | copy-start | bytes 6148
  17.0 10.5 %collective-permute-start = (f32[4,640]{1,0:T(4,128)S(1)}, f32[4,640]{1,0:T(4,128)S(1)}, u32[]{:S(2)}, u32[]{:S(2)}) collective-permute-start(f32[4,640]{1,0:T(4,128)S(1)} %get-tuple-element.18), channel_id=1, source_target_pairs={{0,16},{16,32},{32,48},{48,64},{64,80},{80,96},{96,112},{112,128},... | collective-permute-start | bytes 30728 | tf_op jit(solution)/shard_map/ppermute | solution.py:469
  17.5 10.0 %collective-permute-start.1 = (f32[4,640]{1,0:T(4,128)S(1)}, f32[4,640]{1,0:T(4,128)S(1)}, u32[]{:S(2)}, u32[]{:S(2)}) collective-permute-start(f32[4,640]{1,0:T(4,128)S(1)} %get-tuple-element.19), channel_id=1, source_target_pairs={{0,240},{16,0},{32,16},{48,32},{64,48},{80,64},{96,80},{112,96},{1... | collective-permute-start | bytes 30728 | tf_op jit(solution)/shard_map/ppermute | solution.py:469
  28.6 22.1 %all-to-all-start = ((f32[16,8,512]{2,1,0:T(8,128)}), f32[16,8,512]{2,1,0:T(8,128)S(1)}, u32[]{:S(2)}, u32[]{:S(2)}) async-start(f32[16,8,512]{2,1,0:T(8,128)} %broadcast_in_dim.4), calls=%async_computation | async-start | bytes 524288 | tf_op jit(solution)/shard_map/all_to_all | solution.py:253
  39.3 18.9 %collective-permute-start.2 = (f32[4,640]{1,0:T(4,128)S(1)}, f32[4,640]{1,0:T(4,128)S(1)}, u32[]{:S(2)}, u32[]{:S(2)}) collective-permute-start(f32[4,640]{1,0:T(4,128)S(1)} %get-tuple-element.20), channel_id=1, source_target_pairs={{0,1},{1,2},{2,3},{3,4},{4,5},{5,6},{6,7},{7,8},{8,9},{9,10},{10,1... | collective-permute-start | bytes 30728 | tf_op jit(solution)/shard_map/ppermute | solution.py:469
  40.8 17.5 %collective-permute-start.3 = (f32[4,640]{1,0:T(4,128)S(1)}, f32[4,640]{1,0:T(4,128)S(1)}, u32[]{:S(2)}, u32[]{:S(2)}) collective-permute-start(f32[4,640]{1,0:T(4,128)S(1)} %get-tuple-element.21), channel_id=1, source_target_pairs={{0,15},{1,0},{2,1},{3,2},{4,3},{5,4},{6,5},{7,6},{8,7},{9,8},{10,9... | collective-permute-start | bytes 30728 | tf_op jit(solution)/shard_map/ppermute | solution.py:469
  43.5 1.7 copy-start.9
  45.2 13.1 %copy-start.1 = (f32[3,16384]{1,0:T(4,128)S(1)}, f32[3,16384]{1,0:T(4,128)}, u32[]{:S(2)}) copy-start(f32[3,16384]{1,0:T(4,128)} %refs_4_.1) | copy-start | bytes 589828
  45.2 13.1 %copy-start.3 = (s32[2,16384]{1,0:T(2,128)S(1)}, s32[2,16384]{1,0:T(2,128)}, u32[]{:S(2)}) copy-start(s32[2,16384]{1,0:T(2,128)} %refs_6_.3) | copy-start | bytes 393220
  50.7 45.6 %all-to-all-start.4 = ((f32[16,64,128]{2,1,0:T(8,128)}), f32[16,64,128]{2,1,0:T(8,128)S(1)}, u32[]{:S(2)}, u32[]{:S(2)}) async-start(f32[16,64,128]{2,1,0:T(8,128)} %forward_x.1), calls=%async_computation.4 | async-start | bytes 1048576 | tf_op jit(solution)/shard_map/all_to_all | solution.py:253
  58.3 48.4 %copy-start.13 = (f32[1024,128]{1,0:T(8,128)S(1)}, f32[1024,128]{1,0:T(8,128)}, u32[]{:S(2)}) copy-start(f32[1024,128]{1,0:T(8,128)} %constant.60.clone.lam_y_ref) | copy-start | bytes 1572868
  58.3 48.4 %copy-start.14 = (f32[16,8,128]{2,1,0:T(8,128)S(1)}, f32[16,8,128]{2,1,0:T(8,128)}, u32[]{:S(2)}) copy-start(f32[16,8,128]{2,1,0:T(8,128)} %constant.61.clone.lam_x_ref) | copy-start | bytes 196612
  91.1 5.2 %collective-permute-start.4 = (f32[4,512]{1,0:T(4,128)S(1)}, f32[4,512]{1,0:T(4,128)S(1)}, u32[]{:S(2)}, u32[]{:S(2)}) collective-permute-start(f32[4,512]{1,0:T(4,128)S(1)} %get-tuple-element.25), channel_id=1, source_target_pairs={{0,16},{16,32},{32,48},{48,64},{64,80},{80,96},{96,112},{112,128},... | collective-permute-start | bytes 24584 | tf_op jit(solution)/shard_map/ppermute | solution.py:469
  91.1 5.2 %collective-permute-start.5 = (f32[4,512]{1,0:T(4,128)S(1)}, f32[4,512]{1,0:T(4,128)S(1)}, u32[]{:S(2)}, u32[]{:S(2)}) collective-permute-start(f32[4,512]{1,0:T(4,128)S(1)} %get-tuple-element.26), channel_id=1, source_target_pairs={{0,240},{16,0},{32,16},{48,32},{64,48},{80,64},{96,80},{112,96},{1... | collective-permute-start | bytes 24584 | tf_op jit(solution)/shard_map/ppermute | solution.py:469
  97.0 20.3 %all-to-all-start.2 = ((f32[16,8,512]{2,1,0:T(8,128)}), f32[16,8,512]{2,1,0:T(8,128)S(1)}, u32[]{:S(2)}, u32[]{:S(2)}) async-start(f32[16,8,512]{2,1,0:T(8,128)} %broadcast_in_dim.5), calls=%async_computation.2 | async-start | bytes 524288 | tf_op jit(solution)/shard_map/all_to_all | solution.py:253
  106.7 1.6 copy-start.11
  108.3 1.6 copy-start.12
  117.3 15.2 %all-to-all-start.5 = ((f32[16,72,128]{2,1,0:T(8,128)}), f32[16,72,128]{2,1,0:T(8,128)S(1)}, u32[]{:S(2)}, u32[]{:S(2)}) async-start(f32[16,72,128]{2,1,0:T(8,128)} %solve_y.1), calls=%async_computation.5 | async-start | bytes 1179648 | tf_op jit(solution)/shard_map/all_to_all | solution.py:253
  122.2 23.2 %collective-permute-start.6 = (f32[4,512]{1,0:T(4,128)S(1)}, f32[4,512]{1,0:T(4,128)S(1)}, u32[]{:S(2)}, u32[]{:S(2)}) collective-permute-start(f32[4,512]{1,0:T(4,128)S(1)} %get-tuple-element.27), channel_id=1, source_target_pairs={{0,1},{1,2},{2,3},{3,4},{4,5},{5,6},{6,7},{7,8},{8,9},{9,10},{10,1... | collective-permute-start | bytes 24584 | tf_op jit(solution)/shard_map/ppermute | solution.py:469
  122.6 22.8 %collective-permute-start.7 = (f32[4,512]{1,0:T(4,128)S(1)}, f32[4,512]{1,0:T(4,128)S(1)}, u32[]{:S(2)}, u32[]{:S(2)}) collective-permute-start(f32[4,512]{1,0:T(4,128)S(1)} %get-tuple-element.28), channel_id=1, source_target_pairs={{0,15},{1,0},{2,1},{3,2},{4,3},{5,4},{6,5},{7,6},{8,7},{9,8},{10,9... | collective-permute-start | bytes 24584 | tf_op jit(solution)/shard_map/ppermute | solution.py:469
  132.5 44.3 %all-to-all-start.1 = ((f32[16,32,4,128]{3,2,1,0:T(4,128)}), f32[16,32,4,128]{3,2,1,0:T(4,128)S(1)}, u32[]{:S(2)}, u32[]{:S(2)}) async-start(f32[16,32,4,128]{3,2,1,0:T(4,128)} %get-tuple-element.22), calls=%async_computation.1 | async-start | bytes 2097152 | tf_op jit(solution)/shard_map/all_to_all | solution.py:253
  140.7 1.7 copy-start.8
  142.4 1.7 copy-start.10

commit v2 on v1

v2 whole, which is shorter than its diff:
```python
import functools
import math

import jax
import jax.numpy as jnp
import ml_dtypes
import numpy as np
from jax import lax
from jax.experimental import pallas as pl
from jax.experimental.pallas import tpu as pltpu
from jax.sharding import PartitionSpec as P

T = 128
TILES = 128
EDGE = 4
LINKS = 4
GHOSTS = 16
G = 64
SLOT = 32
STEPS = 2
DT = 0.1
OMEGA = 0.3
STIFF = 0.15
GRAV = 0.01
CEXP = 4.0 * math.log2(math.e)
CHUNK = 1024
GROUP = 16
F32 = jnp.float32
BF16 = jnp.bfloat16
VMEM = pl.BlockSpec(memory_space=pltpu.VMEM)
HBM = pl.BlockSpec(memory_space=pltpu.HBM)
SMEM = pl.BlockSpec(memory_space=pltpu.SMEM)
EW = EDGE * T
HALO = EW + EW // 2
NN = (((1,), (0,)), ((), ()))
NT = (((1,), (1,)), ((), ()))
TN = (((0,), (0,)), ((), ()))


def params(mib=48):
    return pltpu.CompilerParams(vmem_limit_bytes=mib * 1024 * 1024)


def cost(us):
    return pl.CostEstimate(flops=int(us * 1.0e9), bytes_accessed=int(us * 3.0e6), transcendentals=0)


def dot(a, b, dims=NN):
    return lax.dot_general(a, b, dims, preferred_element_type=F32)


def split2(a):
    high = a.astype(BF16)
    return high, (a - high.astype(F32)).astype(BF16)


def split3(a):
    high = a.astype(BF16).astype(F32)
    rest = a - high
    mid = rest.astype(BF16).astype(F32)
    return high, mid, rest - mid


@functools.lru_cache(maxsize=None)
def tables(length, count):
    ids = np.arange(length, dtype=np.int64)
    angle = (ids[:, None] * ids[None, :] % length).astype(np.float64) * (2.0 * np.pi / length)
    full = (np.cos(angle) + np.sin(angle)) / math.sqrt(length)
    high = full.astype(ml_dtypes.bfloat16)
    low = (full - high.astype(np.float64)).astype(ml_dtypes.bfloat16)
    block = length // count
    rows = (np.arange(count)[:, None] * block - 1 + np.arange(block + 16)[None, :]) % length
    lam = (4.0 * np.sin(np.pi * ids / length) ** 2).astype(np.float32)
    return high, low, high[rows], low[rows], lam


def places():
    r, a, count = lax.axis_index("rad"), lax.axis_index("azi"), lax.axis_size("azi")
    return r, a, lax.rem(a + count - 1, count), lax.rem(a + 1, count)


def write_edges(pos_ref, mass_ref, out_ref):
    count = out_ref.shape[0]

    def rows(part, half, width):
        lanes = pl.ds(part * EW + half * width, width)
        return jnp.concatenate([pos_ref[0:3, lanes], mass_ref[0:1, lanes]], axis=0)

    up, down = rows(1, 0, EW), rows(0, 0, EW)
    right = [rows(3, half, EW // 2) for half in range(2)]
    left = [rows(2, half, EW // 2) for half in range(2)]
    for d in range(count):
        out_ref[d, 0:4, 0:EW] = up
        out_ref[d, 4:8, 0:EW] = down
    for d in range(count):
        for half in range(2):
            out_ref[d, 4 * half : 4 * half + 4, EW : EW + EW // 2] = right[half]
    _, _, previous, _ = places()
    for half in range(2):
        out_ref[previous, 4 * half : 4 * half + 4, EW : EW + EW // 2] = left[half]


def edges_kernel(pos_ref, mass_ref, pot_ref, out_ref):
    write_edges(pos_ref, mass_ref, out_ref)
    _, _, previous, _ = places()
    turned = pot_ref[...].T
    for d in range(out_ref.shape[0]):
        out_ref[d, 0:1, HALO : HALO + G] = turned[G - 1 : G, :]
    out_ref[previous, 0:1, HALO : HALO + G] = turned[0:1, :]


def edges(pos, mass, pot, azi_count):
    return pl.pallas_call(
        edges_kernel,
        grid=(1,),
        in_specs=[
            pl.BlockSpec((3, 4 * EW), lambda i: (0, 0)),
            pl.BlockSpec((1, 4 * EW), lambda i: (0, 0)),
            pl.BlockSpec((G, G), lambda i: (0, 0)),
        ],
        out_specs=pl.BlockSpec((azi_count, 8, HALO + 128), lambda i: (0, 0, 0)),
        out_shape=jax.ShapeDtypeStruct((azi_count, 8, HALO + 128), F32),
        compiler_params=params(60),
        cost_estimate=cost(1),
        name="edges",
    )(pos, mass, pot)


def pick_kernel(s, halo, shear_ref, far_ref, *refs):
    up_ref, down_ref = refs[-2:]
    r, a, _, _ = places()
    count = far_ref.shape[0]
    up_source = lax.rem(a + count - shear_ref[s, lax.rem(r + 1, shear_ref.shape[1])], count)
    down_source = lax.rem(a + shear_ref[s, r], count)
    up_ref[:, 0:EW] = far_ref[up_source, 0:4, 0:EW]
    down_ref[:, 0:EW] = far_ref[down_source, 4:8, 0:EW]
    if halo:
        pot_ref = refs[0]
        for ref, row in ((up_ref, G - 1), (down_ref, 0)):
            ref[:, EW : EW + 128] = jnp.zeros((4, 128), F32)
            ref[0:1, EW : EW + G] = pot_ref[row : row + 1, :]


def pick(s, shear, far, *pot):
    shape = jax.ShapeDtypeStruct((4, EW + 128 * len(pot)), F32)
    return pl.pallas_call(
        functools.partial(pick_kernel, s, len(pot) > 0),
        in_specs=[SMEM] + [VMEM] * (1 + len(pot)),
        out_specs=[VMEM] * 2,
        out_shape=[shape] * 2,
        compiler_params=params(),
        cost_estimate=cost(0.5),
        name="pick",
    )(shear, far, *pot)


def density_kernel(cells_ref, mass_ref, dest_ref, dens_ref, target_ref, count_ref, acc_ref):
    lanes = cells_ref.shape[1]
    row = lax.broadcasted_iota(jnp.int32, (G, CHUNK), 0)
    acc_ref[...] = jnp.zeros_like(acc_ref)

    def body(j, carry):
        part = pl.ds(pl.multiple_of(j * CHUNK, CHUNK), CHUNK)
        mass = mass_ref[0:1, part]
        pieces = split3(mass)
        for s in range(STEPS):
            cell = cells_ref[s : s + 1, part]
            hit_x = row == (cell >> 6)
            hit_y = jnp.where(row == (cell & (G - 1)), 1.0, 0.0).astype(BF16)
            left = jnp.concatenate(
                [jnp.where(hit_x, piece, 0.0).astype(BF16) for piece in pieces], axis=0
            )
            acc_ref[s] += dot(left, hit_y, NT)
        return carry

    lax.fori_loop(0, lanes // CHUNK, body, 0, unroll=4)
    both = []
    for s in range(STEPS):
        both.append(acc_ref[s, 0:G] + acc_ref[s, G : 2 * G] + acc_ref[s, 2 * G : 3 * G])
    whole = jnp.concatenate(both, axis=1)
    dens_ref[0] = whole

    for d in range(count_ref.shape[0]):
        count_ref[d] = 0

    def slot(t, carry):
        d = dest_ref[t]
        k = count_ref[d]
        target_ref[t] = d * SLOT + k
        count_ref[d] = k + 1
        return carry

    lax.fori_loop(0, TILES, slot, 0)


def densities(cells, mass, dest, azi_count):
    return pl.pallas_call(
        density_kernel,
        in_specs=[VMEM, VMEM, SMEM],
        out_specs=[VMEM, SMEM],
        out_shape=[
            jax.ShapeDtypeStruct((1, G, 2 * G), F32),
            jax.ShapeDtypeStruct((TILES,), jnp.int32),
        ],
        scratch_shapes=[
            pltpu.SMEM((azi_count,), jnp.int32),
            pltpu.VMEM((STEPS, 3 * G, G), F32),
        ],
        compiler_params=params(),
        cost_estimate=cost(7),
        name="densities",
    )(cells, mass, dest)


def dot3(a_high, a_low, b, dims=NN):
    b_high, b_low = split2(b)
    return dot(a_high, b_high, dims) + dot(a_high, b_low, dims) + dot(a_low, b_high, dims)


def fetch(pairs, sem_ref):
    copies = [pltpu.make_async_copy(s, d, sem_ref.at[i]) for i, (s, d) in enumerate(pairs)]
    for copy in copies:
        copy.start()
    return copies


def forward_x_kernel(high_ref, low_ref, dens_ref, more_ref, out_ref, all_ref, h_ref, l_ref, sem_ref):
    r, _, _, _ = places()
    for ref, p, d in blocks_of((dens_ref, more_ref)):
        all_ref[pl.ds(pl.multiple_of(d * G, G), G)] = ref[p]
    for copy in fetch(((high_ref.at[r], h_ref), (low_ref.at[r], l_ref)), sem_ref):
        copy.wait()
    values = all_ref[...]
    lines = dot3(h_ref[1 : G + 1], l_ref[1 : G + 1], values)
    turned = lines.T
    whole = jnp.concatenate([turned[0:G], turned[G : 2 * G]], axis=1)
    for d in range(out_ref.shape[0]):
        out_ref[d] = whole


def solve_y_kernel(high_ref, low_ref, some_high_ref, some_low_ref, lam_y_ref, lam_x_ref, in_ref, out_ref,
                   h_ref, l_ref, sh_ref, sl_ref, lam_ref, modes_ref, sem_ref):
    r, a, _, _ = places()
    size = h_ref.shape[0]
    part = size // 4
    pairs = [(lam_x_ref.at[r], lam_ref)]
    for p in range(4):
        rows = pl.ds(p * part, part)
        pairs += [(high_ref.at[rows], h_ref.at[rows]), (low_ref.at[rows], l_ref.at[rows])]
    pairs += [(some_high_ref.at[a], sh_ref), (some_low_ref.at[a], sl_ref)]
    copies = fetch(pairs, sem_ref)
    values = in_ref[...].reshape(-1, 2 * G)
    copies[0].wait()
    lam_x = lam_ref[0:1, :]
    mean = jnp.sum(values, axis=0, keepdims=True) * (1.0 / size)
    values = values - jnp.where(lam_x == 0.0, mean, 0.0)
    for p in range(4):
        rows = slice(p * part, (p + 1) * part)
        copies[1 + 2 * p].wait()
        copies[2 + 2 * p].wait()
        modes = dot3(h_ref[rows], l_ref[rows], values)
        lam = lam_y_ref[rows] + lam_x
        at_zero = lam == 0.0
        modes_ref[rows] = modes * jnp.where(at_zero, 0.0, -GRAV / jnp.where(at_zero, 1.0, lam))
    copies[9].wait()
    copies[10].wait()
    lines = dot3(sh_ref[...], sl_ref[...], modes_ref[...])
    inner = lines[1 : G + 1].T
    first = jnp.concatenate([inner[0:G], inner[G : 2 * G]], axis=1)
    out_ref[0, 0:G] = first
    out_ref[0, G : G + 8] = jnp.zeros((8, 2 * G), F32)
    out_ref[0, G : G + 1] = lines[0:1]
    out_ref[0, G + 1 : G + 2] = lines[G + 1 : G + 2]


def inverse_x_kernel(high_ref, low_ref, in_ref, more_ref, grad_ref, pot_ref, all_ref, halo_ref, side_ref,
                     turn_ref, h_ref, l_ref, sem_ref):
    r, _, _, _ = places()
    copies = fetch(((high_ref.at[r], h_ref), (low_ref.at[r], l_ref)), sem_ref)
    halo_ref[...] = jnp.zeros_like(halo_ref)
    for ref, p, d in blocks_of((in_ref, more_ref)):
        all_ref[pl.ds(pl.multiple_of(d * G, G), G)] = ref[p, 0:G]
        side_ref[d] = ref[p, G : G + 8, 0:G]
    for d in range(side_ref.shape[0]):
        halo_ref[:, d * G : (d + 1) * G] = side_ref[d]
    for copy in copies:
        copy.wait()
    grid = dot3(h_ref[...], l_ref[...], all_ref[...])
    pot_ref[...] = grid[1 : G + 1, G : 2 * G]
    b_high, b_low = split2(halo_ref[...])
    a_high, a_low = h_ref[1 : G + 1], l_ref[1 : G + 1]
    sides = dot(b_high, a_high, NT) + dot(b_low, a_high, NT) + dot(b_high, a_low, NT)
    grad_x = -(grid[2 : G + 2, 0:G] - grid[0:G, 0:G]) * 0.5
    turn_ref[8 : G + 8] = grid[1 : G + 1, 0:G].T
    turn_ref[7:8] = sides[0:1]
    turn_ref[G + 8 : G + 9] = sides[1:2]
    grad_y = (-(turn_ref[9 : G + 9] - turn_ref[7 : G + 7]) * 0.5).T
    write_gradient(grad_ref, grad_x, grad_y)


def write_gradient(grad_ref, grad_x, grad_y):
    for c, part in enumerate((grad_x, grad_y)):
        for p, piece in enumerate(split3(part)):
            grad_ref[c * G : (c + 1) * G, p * G : (p + 1) * G] = piece


def solve_call(kernel, name, tables_in, arrays, outs, scratch, us):
    return pl.pallas_call(
        kernel,
        in_specs=[HBM] * len(tables_in) + [VMEM] * len(arrays),
        out_specs=[VMEM] * len(outs),
        out_shape=list(outs),
        scratch_shapes=list(scratch),
        compiler_params=params(60),
        cost_estimate=cost(us),
        name=name,
    )(*tables_in, *arrays)


def gathered(value, axis):
    count = lax.axis_size(axis)
    d = count // 2
    parts = [value]
    while d:
        whole = jnp.concatenate(parts, axis=0) if len(parts) > 1 else parts[0]
        parts = [whole, lax.ppermute(whole, axis, [(i, i ^ d) for i in range(count)])]
        d //= 2
    return parts


def blocks_of(refs):
    r, _, _, _ = places()
    half = refs[0].shape[0]
    bits = (2 * half).bit_length() - 1
    for p in range(2 * half):
        partner = sum((p >> bit & 1) << (bits - 1 - bit) for bit in range(bits))
        yield refs[p // half], p % half, r ^ partner


def exchange(value, axis):
    return lax.all_to_all(value, axis, split_axis=0, concat_axis=0, tiled=True)


def old_gradient(pot_ref, up_ref, down_ref, before, after, grad_ref, turn_ref):
    pot = pot_ref[...]
    turn_ref[8 : G + 8] = pot
    turn_ref[7:8] = up_ref[0:1, EW : EW + G]
    turn_ref[G + 8 : G + 9] = down_ref[0:1, EW : EW + G]
    grad_x = -(turn_ref[9 : G + 9] - turn_ref[7 : G + 7]) * 0.5
    turn_ref[8 : G + 8] = pot.T
    turn_ref[7:8] = before
    turn_ref[G + 8 : G + 9] = after
    grad_y = (-(turn_ref[9 : G + 9] - turn_ref[7 : G + 7]) * 0.5).T
    write_gradient(grad_ref, grad_x, grad_y)


def features(pos, mass, work_ref, i_ref, j_ref, r_ref, lanes, own):
    width = pos.shape[1]
    q = pos - 0.5
    norm = -CEXP * jnp.sum(q * q, axis=0, keepdims=True)
    one = jnp.ones_like(norm)
    n_high, n_mid, n_low = split3(norm)
    q_high, q_mid, q_low = split3(q)
    zero = jnp.zeros((8, width), F32)

    def write(groups, target_ref):
        for k, (three, last) in enumerate(groups):
            work_ref[4 * k : 4 * k + 3, 0:width] = three
            work_ref[4 * k + 3 : 4 * k + 4, 0:width] = last
        work_ref[24:32, 0:width] = zero
        target_ref[:, lanes] = work_ref[0:32, 0:width].astype(BF16)

    write(
        (
            (q_high, one),
            (q_mid, n_mid),
            (q_high, one),
            (q_low, n_low),
            (q_high, one),
            (q_mid, n_high),
        ),
        j_ref,
    )
    if own:
        a_high, a_mid, a_low = split3(q * (2.0 * CEXP))
        write(
            (
                (a_high, n_high),
                (a_high, one),
                (a_mid, n_mid),
                (a_high, one),
                (a_low, n_low),
                (a_mid, one),
            ),
            i_ref,
        )
    weighted = q * mass
    w_high = weighted.astype(BF16).astype(F32)
    m_high = mass.astype(BF16).astype(F32)
    work_ref[0:3, 0:width] = w_high
    work_ref[3:4, 0:width] = m_high
    work_ref[4:7, 0:width] = weighted - w_high
    work_ref[7:8, 0:width] = mass - m_high
    work_ref[8:16, 0:width] = zero
    r_ref[:, lanes] = work_ref[0:16, 0:width].astype(BF16)


def step_kernel(last, *refs):
    if last:
        (nbr_ref, target_ref, pos_ref, vel_ref, mass_ref, cells_ref, far_ref, up_ref, down_ref,
         grad_in_ref, pack_ref, i_ref, j_ref, r_ref, work_ref, grad_ref) = refs
    else:
        (nbr_ref, target_ref, pos_ref, vel_ref, mass_ref, cells_ref, far_ref, up_ref, down_ref,
         pot_ref, new_pos_ref, new_vel_ref, edges_ref, pack_ref,
         i_ref, j_ref, r_ref, work_ref, grad_ref, turn_ref, split_ref) = refs
    r, _, previous, following = places()
    if last:
        grad_ref[...] = grad_in_ref[...].astype(BF16)
    else:
        before = far_ref[previous, 0:1, HALO : HALO + G]
        after = far_ref[following, 0:1, HALO : HALO + G]
        old_gradient(pot_ref, up_ref, down_ref, before, after, split_ref, turn_ref)
        grad_ref[...] = split_ref[...].astype(BF16)
    pack_ref[...] = jnp.zeros_like(pack_ref)
    own_lanes = TILES * T

    def prepare(j, carry):
        lanes = pl.ds(pl.multiple_of(j * CHUNK, CHUNK), CHUNK)
        features(pos_ref[0:3, lanes], mass_ref[0:1, lanes], work_ref, i_ref, j_ref, r_ref, lanes, True)
        return carry

    lax.fori_loop(0, own_lanes // CHUNK, prepare, 0)

    first_ghost = own_lanes
    for ghost, axis, move in (
        (up_ref[0:4, 0:EW], 0, -1.0),
        (down_ref[0:4, 0:EW], 0, 1.0),
        (far_ref[previous, 0:4, EW:HALO], 1, -1.0),
        (far_ref[previous, 4:8, EW:HALO], 1, -1.0),
        (far_ref[following, 0:4, EW:HALO], 1, 1.0),
        (far_ref[following, 4:8, EW:HALO], 1, 1.0),
    ):
        width = ghost.shape[1]
        sub = lax.broadcasted_iota(jnp.int32, (3, width), 0)
        place = ghost[0:3] + jnp.where(sub == axis, move, 0.0)
        lanes = slice(first_ghost, first_ghost + width)
        features(place, ghost[3:4], work_ref, i_ref, j_ref, r_ref, lanes, False)
        first_ghost += width

    strip_x = (r - lax.axis_size("rad") // 2).astype(F32)
    row = lax.broadcasted_iota(jnp.int32, (G, T), 0)

    wide_row = lax.broadcasted_iota(jnp.int32, (G, GROUP * T), 0)

    def tiles(g, carry):
        wide = pl.ds(pl.multiple_of(g * (GROUP * T), GROUP * T), GROUP * T)
        cell = cells_ref[last : last + 1, wide]
        hit_y = jnp.where(wide_row == (cell & (G - 1)), 1.0, 0.0).astype(BF16)
        hit_x = wide_row == (cell >> 6)
        field = dot(grad_ref[...], jnp.concatenate([hit_y] * 3, axis=0))
        exponents = []
        rights = []
        for u in range(GROUP):
            t = g * GROUP + u
            own = pl.ds(pl.multiple_of(t * T, T), T)
            picks = [pl.ds(pl.multiple_of(nbr_ref[t, n] * T, T), T) for n in range(LINKS)]
            others = jnp.concatenate([j_ref[:, p] for p in picks], axis=1)
            rights.append(jnp.concatenate([r_ref[:, p] for p in picks], axis=1))
            exponents.append(dot(others, i_ref[:, own], TN))
        weights = [jnp.exp2(e).astype(BF16) for e in exponents]
        sums = jnp.concatenate([dot(x, y) for x, y in zip(rights, weights)], axis=1)
        grav_x = jnp.sum(jnp.where(hit_x, field[0:G], 0.0), axis=0, keepdims=True)
        grav_y = jnp.sum(jnp.where(hit_x, field[G : 2 * G], 0.0), axis=0, keepdims=True)
        pos = pos_ref[0:3, wide]
        vel = vel_ref[0:3, wide]
        total = sums[0:4] + sums[4:8]
        contact = STIFF * ((pos - 0.5) * total[3:4] - total[0:3])
        acc_x = contact[0:1] + grav_x + 2.0 * OMEGA * vel[1:2] + 3.0 * OMEGA**2 * (pos[0:1] + strip_x)
        acc_y = contact[1:2] + grav_y - 2.0 * OMEGA * vel[0:1]
        acc_z = contact[2:3] - OMEGA**2 * (pos[2:3] - 0.5)
        speed = vel + DT * jnp.concatenate([acc_x, acc_y, acc_z], axis=0)
        if not last:
            place = pos + DT * speed
            new_pos_ref[0:3, wide] = place
            new_vel_ref[0:3, wide] = speed
        for u in range(GROUP):
            target = target_ref[g * GROUP + u]
            d = target // SLOT
            k = target % SLOT
            part = slice(u * T, (u + 1) * T)
            if last:
                for c in range(3):
                    pack_ref[d, pl.ds(k * 3 + c, 1), :] = speed[c : c + 1, part]
            else:
                pack_ref[d, k, 0:3, :] = place[:, part]
                pack_ref[d, k, 3:4, :] = mass_ref[0:1, pl.ds(pl.multiple_of(g * (GROUP * T) + u * T, T), T)]
        return carry

    lax.fori_loop(0, TILES // GROUP, tiles, 0)
    if not last:
        write_edges(new_pos_ref, mass_ref, edges_ref)


def step(last, nbr, target, pos, vel, mass, cells, far, up, down, more, azi_count):
    lanes = TILES * T
    if last:
        outs = [jax.ShapeDtypeStruct((azi_count, SLOT * 3, T), F32)]
        out_specs = [VMEM]
    else:
        outs = [jax.ShapeDtypeStruct((3, lanes), F32)] * 2
        outs += [jax.ShapeDtypeStruct((azi_count, 8, HALO), F32)]
        outs += [jax.ShapeDtypeStruct((azi_count, SLOT, 4, T), F32)]
        out_specs = [VMEM] * 4
    scratch = [
        pltpu.VMEM((32, lanes), BF16),
        pltpu.VMEM((32, lanes + GHOSTS * T), BF16),
        pltpu.VMEM((16, lanes + GHOSTS * T), BF16),
        pltpu.VMEM((32, CHUNK), F32),
        pltpu.VMEM((2 * G, 3 * G), BF16),
    ]
    if not last:
        scratch += [pltpu.VMEM((G + 16, G), F32), pltpu.VMEM((2 * G, 3 * G), F32)]
    return pl.pallas_call(
        functools.partial(step_kernel, last),
        in_specs=[SMEM] * 2 + [VMEM] * (7 + len(more)),
        out_specs=out_specs,
        out_shape=outs,
        scratch_shapes=scratch,
        compiler_params=params(),
        cost_estimate=cost(14),
        name=f"step_{last}",
    )(nbr, target, pos, vel, mass, cells, far, up, down, *more)


def assemble_kernel(azi_count, place_ref, speed_ref, out_ref):
    _, b, _, _ = places()

    def group(g, carry):
        a = g // (SLOT // 8)
        h = g % (SLOT // 8)
        signed = lax.rem(a - b + azi_count // 2 + azi_count, azi_count) - azi_count // 2
        move = signed.astype(F32)
        speeds = speed_ref[a, pl.ds(pl.multiple_of(h * 24, 8), 24), :]
        sub = lax.broadcasted_iota(jnp.int32, (3, T), 0)
        for k in range(8):
            four = place_ref[a, h * 8 + k]
            speed = speeds[3 * k : 3 * k + 3]
            mass = four[3:4]
            place = four[0:3] + DT * speed
            place = place + jnp.where((sub == 1) & (mass > 0.0), move, 0.0)
            lanes = pl.ds(pl.multiple_of((g * 8 + k) * T, T), T)
            out_ref[0:3, lanes] = place
            out_ref[3:6, lanes] = speed
            out_ref[6:7, lanes] = mass
        return carry

    lax.fori_loop(0, azi_count * SLOT // 8, group, 0)


def assemble(place, speed):
    azi_count = place.shape[0]
    return pl.pallas_call(
        functools.partial(assemble_kernel, azi_count),
        in_specs=[VMEM, VMEM],
        out_specs=VMEM,
        out_shape=jax.ShapeDtypeStruct((7, azi_count * SLOT * T), F32),
        compiler_params=params(),
        cost_estimate=cost(4),
        name="assemble",
    )(place, speed)


def shifted(value, axis, steps):
    count = lax.axis_size(axis)
    return lax.ppermute(value, axis, [(i, (i + steps) % count) for i in range(count)])


def local(positions, velocities, masses, neighbours, shear_offsets, destinations, deposit_cells, old_potential):
    rad_count = lax.axis_size("rad")
    azi_count = lax.axis_size("azi")
    mass = masses.reshape(1, -1)

    sent = edges(positions, mass, old_potential, azi_count)
    cells_after, sent = lax.optimization_barrier((deposit_cells, sent))
    far = exchange(sent, "azi")
    dens, target = densities(cells_after, mass, destinations, azi_count)
    up, down = pick(0, shear_offsets, far, old_potential)
    up, down = shifted(up, "rad", 1), shifted(down, "rad", -1)

    high_x, low_x, rows_high_x, rows_low_x, lam_x = tables(G * rad_count, rad_count)
    high_y, low_y, rows_high_y, rows_low_y, lam_y = tables(G * azi_count, azi_count)
    lam_cols = np.tile(lam_x.reshape(rad_count, 1, G), (1, 8, 2))
    lam_rows = np.ascontiguousarray(np.broadcast_to(lam_y[:, None], (G * azi_count, 2 * G)))
    size_x, size_y = G * rad_count, G * azi_count
    block = lambda size: pltpu.VMEM((G + 16, size), BF16)
    dens, dens_more = gathered(dens, "rad")
    dens, dens_more, far = lax.optimization_barrier((dens, dens_more, far))
    (lines,) = solve_call(
        forward_x_kernel, "forward_x", (rows_high_x, rows_low_x), (dens, dens_more),
        (jax.ShapeDtypeStruct((azi_count, G, 2 * G), F32),),
        (pltpu.VMEM((size_x, 2 * G), F32), block(size_x), block(size_x), pltpu.SemaphoreType.DMA((2,))), 2,
    )
    lines = exchange(lines, "azi")
    place, speed, sent_1, pack_place = step(
        0, neighbours, target, positions, velocities, mass, deposit_cells, far, up, down,
        (old_potential,), azi_count,
    )
    lines, sent_1 = lax.optimization_barrier((lines, sent_1))
    far_1 = exchange(sent_1, "azi")
    full = pltpu.VMEM((size_y, size_y), BF16)
    (solved,) = pl.pallas_call(
        solve_y_kernel,
        in_specs=[HBM] * 4 + [VMEM, HBM, VMEM],
        out_specs=[VMEM],
        out_shape=[jax.ShapeDtypeStruct((1, G + 8, 2 * G), F32)],
        scratch_shapes=[
            full, full, block(size_y), block(size_y), pltpu.VMEM((8, 2 * G), F32),
            pltpu.VMEM((size_y, 2 * G), F32), pltpu.SemaphoreType.DMA((11,)),
        ],
        compiler_params=params(60),
        cost_estimate=cost(5),
        name="solve_y",
    )(high_y, low_y, rows_high_y, rows_low_y, lam_rows, lam_cols, lines)
    solved, solved_more = gathered(solved, "rad")
    gradient, potential = solve_call(
        inverse_x_kernel, "inverse_x", (rows_high_x, rows_low_x), (solved, solved_more),
        (jax.ShapeDtypeStruct((2 * G, 3 * G), F32), jax.ShapeDtypeStruct((G, G), F32)),
        (pltpu.VMEM((size_x, 2 * G), F32), pltpu.VMEM((8, size_x), F32),
         pltpu.VMEM((rad_count, 8, G), F32), pltpu.VMEM((G + 16, G), F32),
         block(size_x), block(size_x), pltpu.SemaphoreType.DMA((2,))), 2,
    )

    up_1, down_1 = pick(1, shear_offsets, far_1)
    pack_place, up_1, down_1 = lax.optimization_barrier((pack_place, up_1, down_1))
    up_1, down_1 = shifted(up_1, "rad", 1), shifted(down_1, "rad", -1)
    pack_place = exchange(pack_place, "azi")
    (pack_speed,) = step(
        1, neighbours, target, place, speed, mass, deposit_cells, far_1, up_1, down_1,
        (gradient,), azi_count,
    )
    pack_place, pack_speed = lax.optimization_barrier((pack_place, pack_speed))
    pack_speed = exchange(pack_speed, "azi")
    return assemble(pack_place, pack_speed), potential


def solution(mesh):
    placed = (
        P(None, ("rad", "azi")),
        P(None, ("rad", "azi")),
        P(("rad", "azi")),
        P(("rad", "azi"), None),
        P(),
        P(("rad", "azi")),
        P(None, ("rad", "azi")),
        P("rad", "azi"),
    )
    return jax.shard_map(
        local,
        mesh=mesh,
        in_specs=placed,
        out_specs=(P(None, ("rad", "azi")), P("rad", "azi")),
        check_vma=False,
    )
```

time: 213 us -> 163 us (0.77)
  Pallas kernels: 84.7 us -> 53.5 us
  local copies, waits for them, and re-layouts: 13 us -> 2.51 us
  starting transfers between devices: 57.1 us -> 49.3 us
  between operations: 3.26 us -> 0.95 us
    pallas_call x6 -> x8, Pallas kernels: 76.3 us -> 45.5 us  [the longest x2 28.7 us: step(): pl.pallas_call(functools.partial(step_kernel, last), in_specs=[SMEM] * 2...]
    ppermute x0 -> x8, waiting for transfers between devices: none -> 19.4 us  [gathered(): lax.ppermute(whole, axis, [(i, i ^ d) for i in range(count)])]
    all_to_all x6 -> x4, waiting for transfers between devices: 14.4 us -> 3.95 us  [exchange(): return lax.all_to_all(value, axis, split_axis=0, concat_axis=0, tiled=True)]
    all_to_all x6 -> x4, starting transfers between devices: 45.3 us -> 36.1 us  [exchange(): return lax.all_to_all(value, axis, split_axis=0, concat_axis=0, tiled=True)]
    unnamed x35 -> x34, local copies, waits for them, and re-layouts: 10.9 us -> 2.5 us
    ppermute x8 -> x4, waiting for transfers between devices: 7.87 us -> 0.01 us  [shifted(): lax.ppermute(value, axis, [(i, (i + steps) % count) for i in range(count)])]
    ppermute x0 -> x8, starting transfers between devices: none -> 5.28 us  [gathered(): lax.ppermute(whole, axis, [(i, i ^ d) for i in range(count)])]
    ppermute x8 -> x4, starting transfers between devices: 11.8 us -> 7.84 us  [shifted(): lax.ppermute(value, axis, [(i, (i + steps) % count) for i in range(count)])]
  transfers between devices with their start and end apart: 14 -> 16, of which waited for: 6 -> 5; matrix products, arithmetic and copies ran while one was open for 0% -> 1% of each run, Pallas kernels for 34% -> 26%
where the time goes in v2:
time: 163 us; the launch traced here: 162 us
  Pallas kernels  53.5 us (33%)
  starting transfers between devices  49.3 us (30%)
  blocking collectives  30.9 us (19%)
  waiting for transfers between devices  23.4 us (14%)
  local copies, waits for them, and re-layouts  2.51 us (2%)
    all_to_all x4, starting transfers between devices, exchange(): return lax.all_to_all(value, axis, split_axis=0, concat_axis=0, tiled=True)  36.1 us
    all_to_all x1, blocking collectives, exchange(): return lax.all_to_all(value, axis, split_axis=0, concat_axis=0, tiled=True)  30.9 us
    pallas_call x2, Pallas kernels, step(): pl.pallas_call(functools.partial(step_kernel, last), in_specs=[SMEM] * 2...  28.7 us
    ppermute x8, waiting for transfers between devices, gathered(): lax.ppermute(whole, axis, [(i, i ^ d) for i in range(count)])  19.4 us
    ppermute x4, starting transfers between devices, shifted(): lax.ppermute(value, axis, [(i, (i + steps) % count) for i in range(count)])  7.84 us
    pallas_call x2, Pallas kernels, solve_call(): pl.pallas_call(kernel, in_specs=[HBM] * len(tables_in) + [VMEM] * len(arr...  6.64 us
    pallas_call x1, Pallas kernels, densities(): pl.pallas_call(density_kernel, in_specs=[VMEM, VMEM, SMEM], out_specs=[VM...  6.26 us
    pallas_call x1, Pallas kernels, local(): pl.pallas_call(solve_y_kernel, in_specs=[HBM] * 4 + [VMEM, HBM, VMEM], ou...  5.87 us
  transfers between devices with their start and end apart: 16, of which 5 were waited for; matrix products, arithmetic and copies ran while one was open for 1% of the time, Pallas kernels for 26%

profile of v2, /device:TPU:32, one launch (start us, length us, event | category | flops | bytes accessed | tf_op | source)
XLA Modules:
  0.0 162.1 jit_solution(3590701017194800505)
XLA Ops:
  0.7 1.7 %edges.1 = f32[16,8,896]{2,1,0:T(8,128)} custom-call(f32[3,16384]{1,0:T(4,128)} %refs_2_.1, f32[1,16384]{1,0:T(1,128)} %bitcast.1, f32[64,64]{1,0:T(8,128)} %refs_9_.1), custom_call_target="tpu_custom_call" | custom-call | flops 1000000000 | bytes 3000000 | tf_op jit(solution)/shard_map/edges/pallas_call | solution.py:113
  2.4 0.0 copy-start.12
  2.4 0.0 copy-start.4
  2.4 0.0 copy-start.5
  2.4 6.3 %densities.1 = (f32[1,64,128]{2,1,0:T(8,128)S(1)}, s32[128]{0:T(128)S(1)}) custom-call(s32[2,16384]{1,0:T(2,128)S(1)} %copy-done.2, f32[1,16384]{1,0:T(1,128)S(1)} %bitcast.2, s32[128]{0:T(128)S(1)} %copy-done.6), custom_call_target="tpu_custom_call" | custom-call | flops 7000000000 | bytes 21000000 | tf_op jit(solution)/shard_map/densities/pallas_call | solution.py:197
  8.7 3.3 %collective-permute-start = (f32[1,64,128]{2,1,0:T(8,128)S(1)}, f32[1,64,128]{2,1,0:T(8,128)S(1)}, u32[]{:S(2)}, u32[]{:S(2)}) collective-permute-start(f32[1,64,128]{2,1,0:T(8,128)S(1)} %get-tuple-element.28), channel_id=1, source_target_pairs={{0,128},{16,144},{32,160},{48,176},{64,192},{80,208},{96,224},{112... | collective-permute-start | bytes 98312 | tf_op jit(solution)/shard_map/ppermute | solution.py:326
  11.9 11.0 %all-to-all-start = ((f32[16,8,896]{2,1,0:T(8,128)}), f32[16,8,896]{2,1,0:T(8,128)S(1)}, u32[]{:S(2)}, u32[]{:S(2)}) async-start(f32[16,8,896]{2,1,0:T(8,128)} %edges.1), calls=%async_computation | async-start | bytes 917504 | tf_op jit(solution)/shard_map/all_to_all | solution.py:341
  23.0 0.0 collective-permute-done
  23.0 0.8 collective-permute-start.1
  23.8 3.6 %collective-permute-done.1 = f32[2,64,128]{2,1,0:T(8,128)S(1)} collective-permute-done((f32[2,64,128]{2,1,0:T(8,128)S(1)}, f32[2,64,128]{2,1,0:T(8,128)S(1)}, u32[]{:S(2)}, u32[]{:S(2)}) %collective-permute-start.1) | collective-permute-done | bytes 65568 | tf_op jit(solution)/shard_map/ppermute | solution.py:326
  27.4 0.7 collective-permute-start.2
  28.1 5.5 %collective-permute-done.2 = f32[4,64,128]{2,1,0:T(8,128)S(1)} collective-permute-done((f32[4,64,128]{2,1,0:T(8,128)S(1)}, f32[4,64,128]{2,1,0:T(8,128)S(1)}, u32[]{:S(2)}, u32[]{:S(2)}) %collective-permute-start.2) | collective-permute-done | bytes 131104 | tf_op jit(solution)/shard_map/ppermute | solution.py:326
  33.6 0.1 collective-permute-start.3
  33.7 0.1 copy.16.refs_0_
  33.8 3.9 %all-to-all-done.far_ref.refs_6_ = f32[16,8,896]{2,1,0:T(8,128)S(1)} async-done(((f32[16,8,896]{2,1,0:T(8,128)}), f32[16,8,896]{2,1,0:T(8,128)S(1)}, u32[]{:S(2)}, u32[]{:S(2)}) %all-to-all-start) | async-done | bytes 458784 | tf_op jit(solution)/shard_map/all_to_all | solution.py:341
  37.8 0.6 pick.2
  38.4 0.1 collective-permute-start.4
  38.5 0.0 copy-start
  38.5 0.0 copy-start.1
  38.5 3.8 %collective-permute-start.5 = (f32[4,640]{1,0:T(4,128)S(1)}, f32[4,640]{1,0:T(4,128)S(1)}, u32[]{:S(2)}, u32[]{:S(2)}) collective-permute-start(f32[4,640]{1,0:T(4,128)S(1)} %get-tuple-element.32), channel_id=1, source_target_pairs={{0,240},{16,0},{32,16},{48,32},{64,48},{80,64},{96,80},{112,96},{1... | collective-permute-start | bytes 30728 | tf_op jit(solution)/shard_map/ppermute | solution.py:575
  42.3 0.7 copy-done.14
  43.0 3.3 %forward_x.1 = f32[16,64,128]{2,1,0:T(8,128)} custom-call(bf16[16,80,1024]{2,1,0:T(8,128)(2,1)} %constant.12.clone.high_ref.some_high_ref, bf16[16,80,1024]{2,1,0:T(8,128)(2,1)} %constant.13.clone.low_ref.some_low_ref, f32[8,64,128]{2,1,0:T(8,128)} %copy-done.11, f32[8,64,128]{2,1,0:T(8,128)} %copy-done.14), custom_call_target="tpu_custom_call" | custom-call | flops 2000000000 | bytes 6000000 | tf_op jit(solution)/shard_map/forward_x/pallas_call | solution.py:308
  46.3 6.0 %all-to-all-start.1 = ((f32[16,64,128]{2,1,0:T(8,128)}), f32[16,64,128]{2,1,0:T(8,128)S(1)}, u32[]{:S(2)}, u32[]{:S(2)}) async-start(f32[16,64,128]{2,1,0:T(8,128)} %forward_x.1), calls=%async_computation.1 | async-start | bytes 1048576 | tf_op jit(solution)/shard_map/all_to_all | solution.py:341
  52.4 0.0 collective-permute-done.4.refs_7_
  52.4 15.0 %step_0.1 = (f32[3,16384]{1,0:T(4,128)S(1)}, f32[3,16384]{1,0:T(4,128)S(1)}, f32[16,8,768]{2,1,0:T(8,128)}, f32[16,32,4,128]{3,2,1,0:T(4,128)}) custom-call(s32[128,4]{1,0:T(8,128)S(1)} %copy.16.refs_0_, s32[128]{0:T(128)S(1)} %get-tuple-element.27.refs_1_, f32[3,16384]{1,0:T(4,128)S(1)} %copy-done, f32[3,16384]{1,0:T(4,128)S(1)} %copy-done.1, ...), custom_call_target="tpu_custom_call" | custom-call | flops 14000000000 | bytes 42000000 | tf_op jit(solution)/shard_map/step_0/pallas_call | solution.py:523
  67.4 0.0 all-to-all-done.1.in_ref
  67.4 9.6 %all-to-all-start.2 = ((f32[16,8,768]{2,1,0:T(8,128)}), f32[16,8,768]{2,1,0:T(8,128)S(1)}, u32[]{:S(2)}, u32[]{:S(2)}) async-start(f32[16,8,768]{2,1,0:T(8,128)} %get-tuple-element.37), calls=%async_computation.2 | async-start | bytes 786432 | tf_op jit(solution)/shard_map/all_to_all | solution.py:341
  77.1 5.9 %solve_y.1 = f32[1,72,128]{2,1,0:T(8,128)} custom-call(bf16[1024,1024]{1,0:T(8,128)(2,1)} %constant.14.clone.high_ref, bf16[1024,1024]{1,0:T(8,128)(2,1)} %constant.15.clone.low_ref, bf16[16,80,1024]{2,1,0:T(8,128)(2,1)} %constant.12.clone.high_ref.some_high_ref, bf16[16,80,1024]{2,1,0:T(8,128)(2,1)} %constant.13.clone.low_ref.some_low_ref, ...), custom_call_target="tpu_custom_call" | custom-call | flops 5000000000 | bytes 15000000 | tf_op jit(solution)/shard_map/solve_y/pallas_call | solution.py:611
  82.9 0.1 collective-permute-start.8
  83.0 6.0 %collective-permute-done.8 = f32[1,72,128]{2,1,0:T(8,128)S(1)} collective-permute-done((f32[1,72,128]{2,1,0:T(8,128)}, f32[1,72,128]{2,1,0:T(8,128)S(1)}, u32[]{:S(2)}, u32[]{:S(2)}) %collective-permute-start.8) | collective-permute-done | bytes 36896 | tf_op jit(solution)/shard_map/ppermute | solution.py:326
  89.0 0.8 pad_maximum_fusion.3
  89.8 4.3 %collective-permute-done.9 = f32[2,72,128]{2,1,0:T(8,128)S(1)} collective-permute-done((f32[2,72,128]{2,1,0:T(8,128)S(1)}, f32[2,72,128]{2,1,0:T(8,128)S(1)}, u32[]{:S(2)}, u32[]{:S(2)}) %collective-permute-start.9) | collective-permute-done | bytes 73760 | tf_op jit(solution)/shard_map/ppermute | solution.py:326
  94.1 0.8 pad_maximum_fusion.1
  94.9 0.3 collective-permute-start.10
  95.2 0.0 all-to-all-done.2.far_ref.refs_6_
  95.2 0.6 pick.3
  95.8 9.4 %all-to-all-start.3 = ((f32[16,32,4,128]{3,2,1,0:T(4,128)}), f32[16,32,4,128]{3,2,1,0:T(4,128)S(1)}, u32[]{:S(2)}, u32[]{:S(2)}) async-start(f32[16,32,4,128]{3,2,1,0:T(4,128)} %get-tuple-element.40), calls=%async_computation.3 | async-start | bytes 2097152 | tf_op jit(solution)/shard_map/all_to_all | solution.py:341
  105.2 0.0 collective-permute-done.10
  105.3 0.1 collective-permute-start.11
  105.4 0.5 collective-permute-start.6
  105.9 3.4 %collective-permute-start.7 = (f32[4,512]{1,0:T(4,128)S(1)}, f32[4,512]{1,0:T(4,128)S(1)}, u32[]{:S(2)}, u32[]{:S(2)}) collective-permute-start(f32[4,512]{1,0:T(4,128)S(1)} %get-tuple-element.44), channel_id=1, source_target_pairs={{0,240},{16,0},{32,16},{48,32},{64,48},{80,64},{96,80},{112,96},{1... | collective-permute-start | bytes 24584 | tf_op jit(solution)/shard_map/ppermute | solution.py:575
  109.3 0.0 collective-permute-done.11.more_ref
  109.3 0.7 copy-done.13
  110.0 3.3 %inverse_x.1 = (f32[128,192]{1,0:T(8,128)}, f32[64,64]{1,0:T(8,128)}) custom-call(bf16[16,80,1024]{2,1,0:T(8,128)(2,1)} %constant.12.clone.high_ref.some_high_ref, bf16[16,80,1024]{2,1,0:T(8,128)(2,1)} %constant.13.clone.low_ref.some_low_ref, f32[8,72,128]{2,1,0:T(8,128)} %copy-done.10, f32[8,72,128]{2,1,0:T(8,128)} %copy-done.13), custom_call_target="tpu_custom_call" | custom-call | flops 2000000000 | bytes 6000000 | tf_op jit(solution)/shard_map/inverse_x/pallas_call | solution.py:308
  113.4 0.9 copy-done.7
  114.3 13.7 %step_1.1 = f32[16,96,128]{2,1,0:T(8,128)S(1)} custom-call(s32[128,4]{1,0:T(8,128)S(1)} %copy.16.refs_0_, s32[128]{0:T(128)S(1)} %get-tuple-element.27.refs_1_, f32[3,16384]{1,0:T(4,128)S(1)} %get-tuple-element.41.refs_2_, f32[3,16384]{1,0:T(4,128)S(1)} %get-tuple-element.42.refs_3_, f32[1,16384]{1,0:T(1,128)S(1)} %bitcast.4, s32[2,16384]{1,0:T(2,128)S(1)} %copy-done.2, ...), custom_call_target="tpu_custom_call" | custom-call | flops 14000000000 | bytes 42000000 | tf_op jit(solution)/shard_map/step_1/pallas_call | solution.py:523
  128.0 30.9 %all_to_all.25.speed_ref = f32[16,96,128]{2,1,0:T(8,128)S(1)} all-to-all(f32[16,96,128]{2,1,0:T(8,128)S(1)} %step_1.1), channel_id=1, replica_groups=mesh['rad'=16,'azi'=16] {'azi'}, dimensions={0} | all-to-all | bytes 1572864 | tf_op jit(solution)/shard_map/all_to_all | solution.py:341
  158.9 3.2 %assemble.1 = f32[7,65536]{1,0:T(8,128)} custom-call(f32[16,32,4,128]{3,2,1,0:T(4,128)S(1)} %all-to-all-done.3.place_ref, f32[16,96,128]{2,1,0:T(8,128)S(1)} %all_to_all.25.speed_ref), custom_call_target="tpu_custom_call" | custom-call | flops 4000000000 | bytes 12000000 | tf_op jit(solution)/shard_map/assemble/pallas_call | solution.py:562
  (35 shorter events, 0.1 us)
Async XLA Ops:
  0.6 1.7 %copy-start.3 = (f32[16384]{0:T(1024)S(1)}, f32[16384]{0:T(1024)}, u32[]{:S(2)}) copy-start(f32[16384]{0:T(1024)} %param.16) | copy-start | bytes 196612
  0.6 1.7 %copy-start.2 = (s32[2,16384]{1,0:T(2,128)S(1)}, s32[2,16384]{1,0:T(2,128)}, u32[]{:S(2)}) copy-start(s32[2,16384]{1,0:T(2,128)} %refs_5_.3) | copy-start | bytes 393220
  0.7 1.7 %copy-start.6 = (s32[128]{0:T(128)S(1)}, s32[128]{0:T(128)}, u32[]{:S(2)}) copy-start(s32[128]{0:T(128)} %dest_ref.1) | copy-start | bytes 1540
  2.4 31.4 %copy-start.12 = (s32[128,4]{0,1:T(4,128)S(1)}, s32[128,4]{0,1:T(4,128)}, u32[]{:S(2)}) copy-start(s32[128,4]{0,1:T(4,128)} %param.17) | copy-start | bytes 6148
  2.4 35.4 %copy-start.4 = (f32[64,64]{1,0:T(8,128)S(1)}, f32[64,64]{1,0:T(8,128)}, u32[]{:S(2)}) copy-start(f32[64,64]{1,0:T(8,128)} %refs_9_.1) | copy-start | bytes 49156
  2.4 35.4 %copy-start.5 = (s32[2,16]{1,0:T(2,128)S(1)}, s32[2,16]{1,0:T(2,128)}, u32[]{:S(2)}) copy-start(s32[2,16]{1,0:T(2,128)} %shear_ref.3) | copy-start | bytes 388
  8.7 14.3 %collective-permute-start = (f32[1,64,128]{2,1,0:T(8,128)S(1)}, f32[1,64,128]{2,1,0:T(8,128)S(1)}, u32[]{:S(2)}, u32[]{:S(2)}) collective-permute-start(f32[1,64,128]{2,1,0:T(8,128)S(1)} %get-tuple-element.28), channel_id=1, source_target_pairs={{0,128},{16,144},{32,160},{48,176},{64,192},{80,208},{96,224},{112... | collective-permute-start | bytes 98312 | tf_op jit(solution)/shard_map/ppermute | solution.py:326
  11.9 25.8 %all-to-all-start = ((f32[16,8,896]{2,1,0:T(8,128)}), f32[16,8,896]{2,1,0:T(8,128)S(1)}, u32[]{:S(2)}, u32[]{:S(2)}) async-start(f32[16,8,896]{2,1,0:T(8,128)} %edges.1), calls=%async_computation | async-start | bytes 917504 | tf_op jit(solution)/shard_map/all_to_all | solution.py:341
  23.0 4.4 %collective-permute-start.1 = (f32[2,64,128]{2,1,0:T(8,128)S(1)}, f32[2,64,128]{2,1,0:T(8,128)S(1)}, u32[]{:S(2)}, u32[]{:S(2)}) collective-permute-start(f32[2,64,128]{2,1,0:T(8,128)S(1)} %pad_maximum_fusion.4), channel_id=1, source_target_pairs={{0,64},{16,80},{32,96},{48,112},{64,0},{80,16},{96,32},{112,48},{1... | collective-permute-start | bytes 196616 | tf_op jit(solution)/shard_map/ppermute | solution.py:326
  27.4 6.2 %collective-permute-start.2 = (f32[4,64,128]{2,1,0:T(8,128)S(1)}, f32[4,64,128]{2,1,0:T(8,128)S(1)}, u32[]{:S(2)}, u32[]{:S(2)}) collective-permute-start(f32[4,64,128]{2,1,0:T(8,128)S(1)} %pad_maximum_fusion.2), channel_id=1, source_target_pairs={{0,32},{16,48},{32,0},{48,16},{64,96},{80,112},{96,64},{112,80},{1... | collective-permute-start | bytes 393224 | tf_op jit(solution)/shard_map/ppermute | solution.py:326
  33.6 8.7 %copy-start.11 = (f32[8,64,128]{2,1,0:T(8,128)}, f32[8,64,128]{2,1,0:T(8,128)S(1)}, u32[]{:S(2)}) copy-start(f32[8,64,128]{2,1,0:T(8,128)S(1)} %constant_dynamic-update-slice_fusion.dens_ref) | copy-start | bytes 786436
  33.6 8.7 %collective-permute-start.3 = (f32[8,64,128]{2,1,0:T(8,128)S(1)}, f32[8,64,128]{2,1,0:T(8,128)S(1)}, u32[]{:S(2)}, u32[]{:S(2)}) collective-permute-start(f32[8,64,128]{2,1,0:T(8,128)S(1)} %constant_dynamic-update-slice_fusion.dens_ref), channel_id=1, source_target_pairs={{0,16},{16,0},{32,48},{48,32},{64,80},{80,64},{96,112},{112,96},{1... | collective-permute-start | bytes 786440 | tf_op jit(solution)/shard_map/ppermute | solution.py:326
  38.4 14.0 %collective-permute-start.4 = (f32[4,640]{1,0:T(4,128)S(1)}, f32[4,640]{1,0:T(4,128)S(1)}, u32[]{:S(2)}, u32[]{:S(2)}) collective-permute-start(f32[4,640]{1,0:T(4,128)S(1)} %get-tuple-element.31), channel_id=1, source_target_pairs={{0,16},{16,32},{32,48},{48,64},{64,80},{80,96},{96,112},{112,128},... | collective-permute-start | bytes 30728 | tf_op jit(solution)/shard_map/ppermute | solution.py:575
  38.5 13.9 %copy-start = (f32[3,16384]{1,0:T(4,128)S(1)}, f32[3,16384]{1,0:T(4,128)}, u32[]{:S(2)}) copy-start(f32[3,16384]{1,0:T(4,128)} %refs_2_.1) | copy-start | bytes 589828
  38.5 13.9 %copy-start.1 = (f32[3,16384]{1,0:T(4,128)S(1)}, f32[3,16384]{1,0:T(4,128)}, u32[]{:S(2)}) copy-start(f32[3,16384]{1,0:T(4,128)} %refs_3_.1) | copy-start | bytes 589828
  38.5 13.9 %collective-permute-start.5 = (f32[4,640]{1,0:T(4,128)S(1)}, f32[4,640]{1,0:T(4,128)S(1)}, u32[]{:S(2)}, u32[]{:S(2)}) collective-permute-start(f32[4,640]{1,0:T(4,128)S(1)} %get-tuple-element.32), channel_id=1, source_target_pairs={{0,240},{16,0},{32,16},{48,32},{64,48},{80,64},{96,80},{112,96},{1... | collective-permute-start | bytes 30728 | tf_op jit(solution)/shard_map/ppermute | solution.py:575
  42.3 0.7 copy-start.14
  46.3 21.1 %all-to-all-start.1 = ((f32[16,64,128]{2,1,0:T(8,128)}), f32[16,64,128]{2,1,0:T(8,128)S(1)}, u32[]{:S(2)}, u32[]{:S(2)}) async-start(f32[16,64,128]{2,1,0:T(8,128)} %forward_x.1), calls=%async_computation.1 | async-start | bytes 1048576 | tf_op jit(solution)/shard_map/all_to_all | solution.py:341
  67.4 9.6 %copy-start.8 = (f32[16,64,128]{2,1,0:T(8,128)}, f32[16,64,128]{2,1,0:T(8,128)S(1)}, u32[]{:S(2)}) copy-start(f32[16,64,128]{2,1,0:T(8,128)S(1)} %all-to-all-done.1.in_ref) | copy-start | bytes 1572868
  67.4 27.8 %all-to-all-start.2 = ((f32[16,8,768]{2,1,0:T(8,128)}), f32[16,8,768]{2,1,0:T(8,128)S(1)}, u32[]{:S(2)}, u32[]{:S(2)}) async-start(f32[16,8,768]{2,1,0:T(8,128)} %get-tuple-element.37), calls=%async_computation.2 | async-start | bytes 786432 | tf_op jit(solution)/shard_map/all_to_all | solution.py:341
  82.9 6.1 %collective-permute-start.8 = (f32[1,72,128]{2,1,0:T(8,128)}, f32[1,72,128]{2,1,0:T(8,128)S(1)}, u32[]{:S(2)}, u32[]{:S(2)}) collective-permute-start(f32[1,72,128]{2,1,0:T(8,128)} %solve_y.1), channel_id=1, source_target_pairs={{0,128},{16,144},{32,160},{48,176},{64,192},{80,208},{96,224},{112... | collective-permute-start | bytes 110600 | tf_op jit(solution)/shard_map/ppermute | solution.py:326
  89.8 15.4 %copy-start.9 = (f32[1,72,128]{2,1,0:T(8,128)S(1)}, f32[1,72,128]{2,1,0:T(8,128)}, u32[]{:S(2)}) copy-start(f32[1,72,128]{2,1,0:T(8,128)} %solve_y.1) | copy-start | bytes 110596
  89.8 4.4 %collective-permute-start.9 = (f32[2,72,128]{2,1,0:T(8,128)S(1)}, f32[2,72,128]{2,1,0:T(8,128)S(1)}, u32[]{:S(2)}, u32[]{:S(2)}) collective-permute-start(f32[2,72,128]{2,1,0:T(8,128)S(1)} %pad_maximum_fusion.3), channel_id=1, source_target_pairs={{0,64},{16,80},{32,96},{48,112},{64,0},{80,16},{96,32},{112,48},{1... | collective-permute-start | bytes 221192 | tf_op jit(solution)/shard_map/ppermute | solution.py:326
  94.9 10.3 %collective-permute-start.10 = (f32[4,72,128]{2,1,0:T(8,128)S(1)}, f32[4,72,128]{2,1,0:T(8,128)S(1)}, u32[]{:S(2)}, u32[]{:S(2)}) collective-permute-start(f32[4,72,128]{2,1,0:T(8,128)S(1)} %pad_maximum_fusion.1), channel_id=1, source_target_pairs={{0,32},{16,48},{32,0},{48,16},{64,96},{80,112},{96,64},{112,80},{1... | collective-permute-start | bytes 442376 | tf_op jit(solution)/shard_map/ppermute | solution.py:326
  95.8 32.1 %all-to-all-start.3 = ((f32[16,32,4,128]{3,2,1,0:T(4,128)}), f32[16,32,4,128]{3,2,1,0:T(4,128)S(1)}, u32[]{:S(2)}, u32[]{:S(2)}) async-start(f32[16,32,4,128]{3,2,1,0:T(4,128)} %get-tuple-element.40), calls=%async_computation.3 | async-start | bytes 2097152 | tf_op jit(solution)/shard_map/all_to_all | solution.py:341
  105.3 4.0 %copy-start.10 = (f32[8,72,128]{2,1,0:T(8,128)}, f32[8,72,128]{2,1,0:T(8,128)S(1)}, u32[]{:S(2)}) copy-start(f32[8,72,128]{2,1,0:T(8,128)S(1)} %pad_maximum_fusion.in_ref) | copy-start | bytes 884740
  105.3 4.0 %collective-permute-start.11 = (f32[8,72,128]{2,1,0:T(8,128)S(1)}, f32[8,72,128]{2,1,0:T(8,128)S(1)}, u32[]{:S(2)}, u32[]{:S(2)}) collective-permute-start(f32[8,72,128]{2,1,0:T(8,128)S(1)} %pad_maximum_fusion.in_ref), channel_id=1, source_target_pairs={{0,16},{16,0},{32,48},{48,32},{64,80},{80,64},{96,112},{112,96},{1... | collective-permute-start | bytes 884744 | tf_op jit(solution)/shard_map/ppermute | solution.py:326
  105.4 8.0 %collective-permute-start.6 = (f32[4,512]{1,0:T(4,128)S(1)}, f32[4,512]{1,0:T(4,128)S(1)}, u32[]{:S(2)}, u32[]{:S(2)}) collective-permute-start(f32[4,512]{1,0:T(4,128)S(1)} %get-tuple-element.43), channel_id=1, source_target_pairs={{0,16},{16,32},{32,48},{48,64},{64,80},{80,96},{96,112},{112,128},... | collective-permute-start | bytes 24584 | tf_op jit(solution)/shard_map/ppermute | solution.py:575
  105.9 7.5 %collective-permute-start.7 = (f32[4,512]{1,0:T(4,128)S(1)}, f32[4,512]{1,0:T(4,128)S(1)}, u32[]{:S(2)}, u32[]{:S(2)}) collective-permute-start(f32[4,512]{1,0:T(4,128)S(1)} %get-tuple-element.44), channel_id=1, source_target_pairs={{0,240},{16,0},{32,16},{48,32},{64,48},{80,64},{96,80},{112,96},{1... | collective-permute-start | bytes 24584 | tf_op jit(solution)/shard_map/ppermute | solution.py:575
  109.3 0.7 copy-start.13
  113.4 0.9 copy-start.7

commit v3 on v2

--- a/solution.py
+++ b/solution.py
@@ -70,8 +70,29 @@
     low = (full - high.astype(np.float64)).astype(ml_dtypes.bfloat16)
     block = length // count
     rows = (np.arange(count)[:, None] * block - 1 + np.arange(block + 16)[None, :]) % length
-    lam = (4.0 * np.sin(np.pi * ids / length) ** 2).astype(np.float32)
-    return high, low, high[rows], low[rows], lam
+    return high[rows], low[rows]
+
+
+@functools.lru_cache(maxsize=None)
+def powers(length, count, far_length, far_count):
+    block = length // count
+    lam = 4.0 * np.sin(np.pi * np.arange(length) / length) ** 2
+    half = 0.5 * lam
+    q = 1.0 / (1.0 + half + np.sqrt(half * (half + 2.0)))
+    q[0] = 0.0
+    q = np.tile(q.reshape(count, 1, block), (1, 1, STEPS))
+    y = np.arange(G)[None, :, None]
+    strips = np.arange(far_count)[None, :, None]
+    safe = np.where(q == 0.0, 0.5, q)
+    rows = [
+        q ** (y + 1),
+        np.where(q == 0.0, 0.0, q ** (G * strips) / (1.0 - q**far_length)),
+        q,
+        np.where(q == 0.0, 0.0, -GRAV / (1.0 / safe - safe)),
+        q ** (2 ** np.arange(6)[None, :, None]),
+        q ** (G - y),
+    ]
+    return np.concatenate(rows, axis=1).astype(np.float32)
 
 
 def places():
@@ -207,7 +228,7 @@
             pltpu.VMEM((STEPS, 3 * G, G), F32),
         ],
         compiler_params=params(),
-        cost_estimate=cost(7),
+        cost_estimate=cost(0.3),
         name="densities",
     )(cells, mass, dest)
 
@@ -224,50 +245,75 @@
     return copies
 
 
-def forward_x_kernel(high_ref, low_ref, dens_ref, more_ref, out_ref, all_ref, h_ref, l_ref, sem_ref):
+def forward_x_kernel(high_ref, low_ref, power_ref, dens_ref, more_ref, edges_ref, sums_ref, sent_ref,
+                     ends_ref, all_ref, scan_ref, h_ref, l_ref, p_ref, sem_ref):
     r, _, _, _ = places()
+    copies = fetch(((high_ref.at[r], h_ref), (low_ref.at[r], l_ref), (power_ref.at[r], p_ref)), sem_ref)
     for ref, p, d in blocks_of((dens_ref, more_ref)):
         all_ref[pl.ds(pl.multiple_of(d * G, G), G)] = ref[p]
-    for copy in fetch(((high_ref.at[r], h_ref), (low_ref.at[r], l_ref)), sem_ref):
+    for copy in copies:
         copy.wait()
-    values = all_ref[...]
-    lines = dot3(h_ref[1 : G + 1], l_ref[1 : G + 1], values)
+    lines = dot3(h_ref[1 : G + 1], l_ref[1 : G + 1], all_ref[...])
     turned = lines.T
-    whole = jnp.concatenate([turned[0:G], turned[G : 2 * G]], axis=1)
-    for d in range(out_ref.shape[0]):
-        out_ref[d] = whole
-
-
-def solve_y_kernel(high_ref, low_ref, some_high_ref, some_low_ref, lam_y_ref, lam_x_ref, in_ref, out_ref,
-                   h_ref, l_ref, sh_ref, sl_ref, lam_ref, modes_ref, sem_ref):
+    value = jnp.concatenate([turned[0:G], turned[G : 2 * G]], axis=1)
+    doubling = p_ref.shape[0] - G - 6
+    scan_ref[...] = jnp.zeros_like(scan_ref)
+    for way in range(2):
+        total = value
+        for j in range(6):
+            scan_ref[32 : 32 + G] = total
+            first = 32 + (1 << j) * (1 if way else -1)
+            total = total + p_ref[doubling + j : doubling + j + 1] * scan_ref[first : first + G]
+        sums_ref[way] = total
+    sums_ref[2] = value
+    ends_ref[0:1] = sums_ref[0, G - 1 : G]
+    ends_ref[1:2] = sums_ref[1, 0:1]
+    ends_ref[2:3] = lines[0:1]
+    ends_ref[3:8] = jnp.zeros((5, 2 * G), F32)
+    for d in range(sent_ref.shape[0]):
+        sent_ref[d, :, 0:HALO] = edges_ref[d]
+        sent_ref[d, :, HALO : HALO + 2 * G] = ends_ref[...]
+
+
+def solve_y_kernel(power_ref, far_ref, sums_ref, out_ref, p_ref, line_ref, sem_ref):
     r, a, _, _ = places()
-    size = h_ref.shape[0]
-    part = size // 4
-    pairs = [(lam_x_ref.at[r], lam_ref)]
-    for p in range(4):
-        rows = pl.ds(p * part, part)
-        pairs += [(high_ref.at[rows], h_ref.at[rows]), (low_ref.at[rows], l_ref.at[rows])]
-    pairs += [(some_high_ref.at[a], sh_ref), (some_low_ref.at[a], sl_ref)]
-    copies = fetch(pairs, sem_ref)
-    values = in_ref[...].reshape(-1, 2 * G)
+    copies = fetch(((power_ref.at[r], p_ref),), sem_ref)
+    count = far_ref.shape[0]
+    size = count * G
+    lanes = slice(HALO, HALO + 2 * G)
+    row = lax.broadcasted_iota(jnp.int32, (G + 8, G), 0)
+    lane = lax.broadcasted_iota(jnp.int32, (G + 8, G), 1)
+    constant = []
+    for s in range(STEPS):
+        parts = [far_ref[b, 2:3, HALO + s * G : HALO + (s + 1) * G] for b in range(count)]
+        mean = jnp.sum(sum(parts), axis=1, keepdims=True) * (1.0 / size)
+        total = jnp.zeros((G + 8, G), F32)
+        for b in range(count):
+            n = (a - b) * G + row - 1 - lane
+            n = jnp.where(n < 0, n + size, n)
+            total += (n * (size - n)).astype(F32) * (parts[b] - mean)
+        constant.append(jnp.sum(total, axis=1, keepdims=True) * (GRAV / (2.0 * size)))
     copies[0].wait()
-    lam_x = lam_ref[0:1, :]
-    mean = jnp.sum(values, axis=0, keepdims=True) * (1.0 / size)
-    values = values - jnp.where(lam_x == 0.0, mean, 0.0)
-    for p in range(4):
-        rows = slice(p * part, (p + 1) * part)
-        copies[1 + 2 * p].wait()
-        copies[2 + 2 * p].wait()
-        modes = dot3(h_ref[rows], l_ref[rows], values)
-        lam = lam_y_ref[rows] + lam_x
-        at_zero = lam == 0.0
-        modes_ref[rows] = modes * jnp.where(at_zero, 0.0, -GRAV / jnp.where(at_zero, 1.0, lam))
-    copies[9].wait()
-    copies[10].wait()
-    lines = dot3(sh_ref[...], sl_ref[...], modes_ref[...])
+    start = jnp.zeros((1, 2 * G), F32)
+    stop = jnp.zeros((1, 2 * G), F32)
+    for m in range(count):
+        weight = p_ref[G + m : G + m + 1]
+        start += weight * far_ref[lax.rem(a + 2 * count - 1 - m, count), 0:1, lanes]
+        stop += weight * far_ref[lax.rem(a + 1 + m, count), 1:2, lanes]
+    q = p_ref[G + count : G + count + 1]
+    scale = p_ref[G + count + 1 : G + count + 2]
+    rising = sums_ref[0] + p_ref[0:G] * start
+    falling = sums_ref[1] + p_ref[p_ref.shape[0] - G : p_ref.shape[0]] * stop
+    line_ref[...] = jnp.zeros_like(line_ref)
+    line_ref[0:1] = (start + q * falling[0:1]) * scale
+    line_ref[1 : G + 1] = (rising + falling - sums_ref[2]) * scale
+    line_ref[G + 1 : G + 2] = (stop + q * rising[G - 1 : G]) * scale
+    lines = line_ref[...]
+    mode = lax.broadcasted_iota(jnp.int32, lines.shape, 1) + jnp.where(r == 0, 0, 4 * G)
+    for s in range(STEPS):
+        lines = jnp.where(mode == s * G, constant[s], lines)
     inner = lines[1 : G + 1].T
-    first = jnp.concatenate([inner[0:G], inner[G : 2 * G]], axis=1)
-    out_ref[0, 0:G] = first
+    out_ref[0, 0:G] = jnp.concatenate([inner[0:G], inner[G : 2 * G]], axis=1)
     out_ref[0, G : G + 8] = jnp.zeros((8, 2 * G), F32)
     out_ref[0, G : G + 1] = lines[0:1]
     out_ref[0, G + 1 : G + 2] = lines[G + 1 : G + 2]
@@ -317,15 +363,17 @@
     )(*tables_in, *arrays)
 
 
-def gathered(value, axis):
+def gathered(value, axis, after=None, stage=0):
     count = lax.axis_size(axis)
     d = count // 2
     parts = [value]
     while d:
         whole = jnp.concatenate(parts, axis=0) if len(parts) > 1 else parts[0]
+        if after is not None and d == count >> stage:
+            whole, after = lax.optimization_barrier((whole, after))
         parts = [whole, lax.ppermute(whole, axis, [(i, i ^ d) for i in range(count)])]
         d //= 2
-    return parts
+    return *parts, after
 
 
 def blocks_of(refs):
@@ -584,53 +632,40 @@
     cells_after, sent = lax.optimization_barrier((deposit_cells, sent))
     far = exchange(sent, "azi")
     dens, target = densities(cells_after, mass, destinations, azi_count)
+
+    rows_high, rows_low = tables(G * rad_count, rad_count)
+    power = powers(G * rad_count, rad_count, G * azi_count, azi_count)
+    size_x = G * rad_count
+    block = pltpu.VMEM((G + 16, size_x), BF16)
+    power_block = pltpu.VMEM(power.shape[1:], F32)
     up, down = pick(0, shear_offsets, far, old_potential)
+    dens, dens_more, (up, down) = gathered(dens, "rad", (up, down), 3)
     up, down = shifted(up, "rad", 1), shifted(down, "rad", -1)
-
-    high_x, low_x, rows_high_x, rows_low_x, lam_x = tables(G * rad_count, rad_count)
-    high_y, low_y, rows_high_y, rows_low_y, lam_y = tables(G * azi_count, azi_count)
-    lam_cols = np.tile(lam_x.reshape(rad_count, 1, G), (1, 8, 2))
-    lam_rows = np.ascontiguousarray(np.broadcast_to(lam_y[:, None], (G * azi_count, 2 * G)))
-    size_x, size_y = G * rad_count, G * azi_count
-    block = lambda size: pltpu.VMEM((G + 16, size), BF16)
-    dens, dens_more = gathered(dens, "rad")
-    dens, dens_more, far = lax.optimization_barrier((dens, dens_more, far))
-    (lines,) = solve_call(
-        forward_x_kernel, "forward_x", (rows_high_x, rows_low_x), (dens, dens_more),
-        (jax.ShapeDtypeStruct((azi_count, G, 2 * G), F32),),
-        (pltpu.VMEM((size_x, 2 * G), F32), block(size_x), block(size_x), pltpu.SemaphoreType.DMA((2,))), 2,
-    )
-    lines = exchange(lines, "azi")
-    place, speed, sent_1, pack_place = step(
-        0, neighbours, target, positions, velocities, mass, deposit_cells, far, up, down,
-        (old_potential,), azi_count,
-    )
-    lines, sent_1 = lax.optimization_barrier((lines, sent_1))
+    place, speed, edges_1, pack_place = step(
+        0, neighbours, target, positions, velocities, mass, deposit_cells, far, up, down, (old_potential,), azi_count,
+    )
+    sums, sent_1 = solve_call(
+        forward_x_kernel, "forward_x", (rows_high, rows_low, power), (dens, dens_more, edges_1),
+        (jax.ShapeDtypeStruct((3, G, 2 * G), F32), jax.ShapeDtypeStruct((azi_count, 8, HALO + 2 * G), F32)),
+        (pltpu.VMEM((8, 2 * G), F32), pltpu.VMEM((size_x, 2 * G), F32), pltpu.VMEM((2 * G, 2 * G), F32), block, block,
+         power_block, pltpu.SemaphoreType.DMA((3,))), 2,
+    )
     far_1 = exchange(sent_1, "azi")
-    full = pltpu.VMEM((size_y, size_y), BF16)
-    (solved,) = pl.pallas_call(
-        solve_y_kernel,
-        in_specs=[HBM] * 4 + [VMEM, HBM, VMEM],
-        out_specs=[VMEM],
-        out_shape=[jax.ShapeDtypeStruct((1, G + 8, 2 * G), F32)],
-        scratch_shapes=[
-            full, full, block(size_y), block(size_y), pltpu.VMEM((8, 2 * G), F32),
-            pltpu.VMEM((size_y, 2 * G), F32), pltpu.SemaphoreType.DMA((11,)),
-        ],
-        compiler_params=params(60),
-        cost_estimate=cost(5),
-        name="solve_y",
-    )(high_y, low_y, rows_high_y, rows_low_y, lam_rows, lam_cols, lines)
-    solved, solved_more = gathered(solved, "rad")
+    up_1, down_1 = pick(1, shear_offsets, far_1)
+    (solved,) = solve_call(
+        solve_y_kernel, "solve_y", (power,), (far_1, sums),
+        (jax.ShapeDtypeStruct((1, G + 8, 2 * G), F32),),
+        (power_block, pltpu.VMEM((G + 8, 2 * G), F32), pltpu.SemaphoreType.DMA((1,))), 2,
+    )
+    solved, solved_more, _ = gathered(solved, "rad")
     gradient, potential = solve_call(
-        inverse_x_kernel, "inverse_x", (rows_high_x, rows_low_x), (solved, solved_more),
+        inverse_x_kernel, "inverse_x", (rows_high, rows_low), (solved, solved_more),
         (jax.ShapeDtypeStruct((2 * G, 3 * G), F32), jax.ShapeDtypeStruct((G, G), F32)),
         (pltpu.VMEM((size_x, 2 * G), F32), pltpu.VMEM((8, size_x), F32),
          pltpu.VMEM((rad_count, 8, G), F32), pltpu.VMEM((G + 16, G), F32),
-         block(size_x), block(size_x), pltpu.SemaphoreType.DMA((2,))), 2,
-    )
-
-    up_1, down_1 = pick(1, shear_offsets, far_1)
+         block, block, pltpu.SemaphoreType.DMA((2,))), 2,
+    )
+
     pack_place, up_1, down_1 = lax.optimization_barrier((pack_place, up_1, down_1))
     up_1, down_1 = shifted(up_1, "rad", 1), shifted(down_1, "rad", -1)
     pack_place = exchange(pack_place, "azi")

time: 163 us -> 160 us (0.982)
  blocking collectives: 30.9 us -> 51.9 us
  starting transfers between devices: 49.3 us -> 36.3 us
  waiting for transfers between devices: 23.4 us -> 15.1 us
  Pallas kernels: 53.5 us -> 50.6 us
    all_to_all x1 -> x2, blocking collectives: 30.9 us -> 51.9 us  [exchange(): return lax.all_to_all(value, axis, split_axis=0, concat_axis=0, tiled=True)]
    all_to_all x4 -> x2, starting transfers between devices: 36.1 us -> 18.2 us  [exchange(): return lax.all_to_all(value, axis, split_axis=0, concat_axis=0, tiled=True)]
    ppermute x8, waiting for transfers between devices: 19.4 us -> 11.1 us  [gathered(): lax.ppermute(whole, axis, [(i, i ^ d) for i in range(count)])]
    pallas_call x1 -> x0, Pallas kernels: 5.87 us -> none  [local(): pl.pallas_call(solve_y_kernel, in_specs=[HBM] * 4 + [VMEM, HBM, VMEM], ou...]
    ppermute x8, starting transfers between devices: 5.28 us -> 10.2 us  [gathered(): lax.ppermute(whole, axis, [(i, i ^ d) for i in range(count)])]
    pallas_call x2 -> x3, Pallas kernels: 6.64 us -> 9.8 us  [solve_call(): pl.pallas_call(kernel, in_specs=[HBM] * len(tables_in) + [VMEM] * len(arr...]
    all_to_all x4 -> x2, waiting for transfers between devices: 3.95 us -> 3.23 us  [exchange(): return lax.all_to_all(value, axis, split_axis=0, concat_axis=0, tiled=True)]
  transfers between devices with their start and end apart: 16 -> 14, of which waited for: 5 -> 7; matrix products, arithmetic and copies ran while one was open for 1% -> 0% of each run, Pallas kernels for 26% -> 24%
where the time goes in v3:
time: 160 us
  blocking collectives  51.9 us (32%)
  Pallas kernels  50.6 us (32%)
  starting transfers between devices  36.3 us (23%)
  waiting for transfers between devices  15.1 us (9%)
  local copies, waits for them, and re-layouts  3.23 us (2%)
    all_to_all x2, blocking collectives, exchange(): return lax.all_to_all(value, axis, split_axis=0, concat_axis=0, tiled=True)  51.9 us
    pallas_call x2, Pallas kernels, step(): pl.pallas_call(functools.partial(step_kernel, last), in_specs=[SMEM] * 2...  28.5 us
    all_to_all x2, starting transfers between devices, exchange(): return lax.all_to_all(value, axis, split_axis=0, concat_axis=0, tiled=True)  18.2 us
    ppermute x8, waiting for transfers between devices, gathered(): lax.ppermute(whole, axis, [(i, i ^ d) for i in range(count)])  11.1 us
    ppermute x8, starting transfers between devices, gathered(): lax.ppermute(whole, axis, [(i, i ^ d) for i in range(count)])  10.2 us
    pallas_call x3, Pallas kernels, solve_call(): pl.pallas_call(kernel, in_specs=[HBM] * len(tables_in) + [VMEM] * len(arr...  9.8 us
    ppermute x4, starting transfers between devices, shifted(): lax.ppermute(value, axis, [(i, (i + steps) % count) for i in range(count)])  7.85 us
    pallas_call x1, Pallas kernels, densities(): pl.pallas_call(density_kernel, in_specs=[VMEM, VMEM, SMEM], out_specs=[VM...  6.25 us
  transfers between devices with their start and end apart: 14, of which 7 were waited for; matrix products, arithmetic and copies ran while one was open for 0% of the time, Pallas kernels for 24%

profile of v3, /device:TPU:32, one launch (start us, length us, event | category | flops | bytes accessed | tf_op | source)
XLA Modules:
  0.0 159.7 jit_solution(4403655495741682470)
XLA Ops:
  0.7 1.7 %edges.1 = f32[16,8,896]{2,1,0:T(8,128)} custom-call(f32[3,16384]{1,0:T(4,128)} %refs_2_.1, f32[1,16384]{1,0:T(1,128)} %bitcast.1, f32[64,64]{1,0:T(8,128)} %refs_9_.1), custom_call_target="tpu_custom_call" | custom-call | flops 1000000000 | bytes 3000000 | tf_op jit(solution)/shard_map/edges/pallas_call | solution.py:134
  2.4 11.2 %all-to-all-start = ((f32[16,8,896]{2,1,0:T(8,128)}), f32[16,8,896]{2,1,0:T(8,128)S(1)}, u32[]{:S(2)}, u32[]{:S(2)}) async-start(f32[16,8,896]{2,1,0:T(8,128)} %edges.1), calls=%async_computation | async-start | bytes 917504 | tf_op jit(solution)/shard_map/all_to_all | solution.py:389
  13.6 0.0 copy-done.4
  13.6 6.2 %densities.1 = (f32[1,64,128]{2,1,0:T(8,128)S(1)}, s32[128]{0:T(128)S(1)}) custom-call(s32[2,16384]{1,0:T(2,128)S(1)} %copy-done.4, f32[1,16384]{1,0:T(1,128)S(1)} %bitcast.2, s32[128]{0:T(128)S(1)} %copy-done.8), custom_call_target="tpu_custom_call" | custom-call | flops 300000000 | bytes 900000 | tf_op jit(solution)/shard_map/densities/pallas_call | solution.py:218
  19.9 3.3 %collective-permute-start = (f32[1,64,128]{2,1,0:T(8,128)S(1)}, f32[1,64,128]{2,1,0:T(8,128)S(1)}, u32[]{:S(2)}, u32[]{:S(2)}) collective-permute-start(f32[1,64,128]{2,1,0:T(8,128)S(1)} %get-tuple-element.29), channel_id=1, source_target_pairs={{0,128},{16,144},{32,160},{48,176},{64,192},{80,208},{96,224},{112... | collective-permute-start | bytes 98312 | tf_op jit(solution)/shard_map/ppermute | solution.py:374
  23.2 2.2 %collective-permute-done = f32[1,64,128]{2,1,0:T(8,128)S(1)} collective-permute-done((f32[1,64,128]{2,1,0:T(8,128)S(1)}, f32[1,64,128]{2,1,0:T(8,128)S(1)}, u32[]{:S(2)}, u32[]{:S(2)}) %collective-permute-start) | collective-permute-done | bytes 32800 | tf_op jit(solution)/shard_map/ppermute | solution.py:374
  25.4 1.6 collective-permute-start.1
  27.0 2.7 %collective-permute-done.1 = f32[2,64,128]{2,1,0:T(8,128)S(1)} collective-permute-done((f32[2,64,128]{2,1,0:T(8,128)S(1)}, f32[2,64,128]{2,1,0:T(8,128)S(1)}, u32[]{:S(2)}, u32[]{:S(2)}) %collective-permute-start.1) | collective-permute-done | bytes 65568 | tf_op jit(solution)/shard_map/ppermute | solution.py:374
  29.7 0.0 all-to-all-done.far_ref.refs_6_
  29.7 0.6 pick.2
  30.3 0.7 collective-permute-start.4
  31.0 0.1 copy.13.refs_0_
  31.1 0.1 collective-permute-start.2
  31.2 3.8 %collective-permute-start.3 = (f32[4,640]{1,0:T(4,128)S(1)}, f32[4,640]{1,0:T(4,128)S(1)}, u32[]{:S(2)}, u32[]{:S(2)}) collective-permute-start(f32[4,640]{1,0:T(4,128)S(1)} %get-tuple-element.33), channel_id=1, source_target_pairs={{0,240},{16,0},{32,16},{48,32},{64,48},{80,64},{96,80},{112,96},{1... | collective-permute-start | bytes 30728 | tf_op jit(solution)/shard_map/ppermute | solution.py:623
  35.0 0.4 collective-permute-done.4
  35.5 0.1 collective-permute-start.5
  35.6 0.8 collective-permute-done.2.refs_7_
  36.4 0.0 collective-permute-done.3.refs_8_
  36.4 14.8 %step_0.1 = (f32[3,16384]{1,0:T(4,128)S(1)}, f32[3,16384]{1,0:T(4,128)S(1)}, f32[16,8,768]{2,1,0:T(8,128)S(1)}, f32[16,32,4,128]{3,2,1,0:T(4,128)}) custom-call(s32[128,4]{1,0:T(8,128)S(1)} %copy.13.refs_0_, s32[128]{0:T(128)S(1)} %get-tuple-element.27.refs_1_, f32[3,16384]{1,0:T(4,128)S(1)} %copy-done.2, f32[3,16384]{1,0:T(4,128)S(1)} %copy-done.3, ...), custom_call_target="tpu_custom_call" | custom-call | flops 14000000000 | bytes 42000000 | tf_op jit(solution)/shard_map/step_0/pallas_call | solution.py:571
  51.3 0.8 copy-done.1
  52.0 0.0 collective-permute-done.5.more_ref
  52.0 0.7 copy-done.13
  52.7 3.6 %forward_x.1 = (f32[3,64,128]{2,1,0:T(8,128)}, f32[16,8,896]{2,1,0:T(8,128)}) custom-call(bf16[16,80,1024]{2,1,0:T(8,128)(2,1)} %constant.6.clone.high_ref, bf16[16,80,1024]{2,1,0:T(8,128)(2,1)} %constant.7.clone.low_ref, f32[16,152,128]{2,1,0:T(8,128)} %constant.8.clone.power_ref, f32[8,64,128]{2,1,0:T(8,128)} %copy-done.10, f32[8,64,128]{2,1,0:T(8,128)} %copy-done.13, ...), custom_call_target="tpu_custom_call" | custom-call | flops 2000000000 | bytes 6000000 | tf_op jit(solution)/shard_map/forward_x/pallas_call | solution.py:354
  56.3 24.7 %all_to_all.20.far_ref.refs_6_ = f32[16,8,896]{2,1,0:T(8,128)} all-to-all(f32[16,8,896]{2,1,0:T(8,128)} %get-tuple-element.37), channel_id=1, replica_groups=mesh['rad'=16,'azi'=16] {'azi'}, dimensions={0} | all-to-all | bytes 917504 | tf_op jit(solution)/shard_map/all_to_all | solution.py:389
  81.0 2.9 %solve_y.1 = f32[1,72,128]{2,1,0:T(8,128)} custom-call(f32[16,152,128]{2,1,0:T(8,128)} %constant.8.clone.power_ref, f32[16,8,896]{2,1,0:T(8,128)} %all_to_all.20.far_ref.refs_6_, f32[3,64,128]{2,1,0:T(8,128)} %get-tuple-element.45.sums_ref), custom_call_target="tpu_custom_call" | custom-call | flops 2000000000 | bytes 6000000 | tf_op jit(solution)/shard_map/solve_y/pallas_call | solution.py:354
  83.9 3.0 %collective-permute-start.8 = (f32[1,72,128]{2,1,0:T(8,128)}, f32[1,72,128]{2,1,0:T(8,128)S(1)}, u32[]{:S(2)}, u32[]{:S(2)}) collective-permute-start(f32[1,72,128]{2,1,0:T(8,128)} %solve_y.1), channel_id=1, source_target_pairs={{0,128},{16,144},{32,160},{48,176},{64,192},{80,208},{96,224},{112... | collective-permute-start | bytes 110600 | tf_op jit(solution)/shard_map/ppermute | solution.py:374
  87.0 2.7 %collective-permute-done.8 = f32[1,72,128]{2,1,0:T(8,128)S(1)} collective-permute-done((f32[1,72,128]{2,1,0:T(8,128)}, f32[1,72,128]{2,1,0:T(8,128)S(1)}, u32[]{:S(2)}, u32[]{:S(2)}) %collective-permute-start.8) | collective-permute-done | bytes 36896 | tf_op jit(solution)/shard_map/ppermute | solution.py:374
  89.7 0.8 pad_maximum_fusion.3
  90.5 1.3 collective-permute-start.9
  91.8 3.0 %collective-permute-done.9 = f32[2,72,128]{2,1,0:T(8,128)S(1)} collective-permute-done((f32[2,72,128]{2,1,0:T(8,128)S(1)}, f32[2,72,128]{2,1,0:T(8,128)S(1)}, u32[]{:S(2)}, u32[]{:S(2)}) %collective-permute-start.9) | collective-permute-done | bytes 73760 | tf_op jit(solution)/shard_map/ppermute | solution.py:374
  94.8 0.8 pad_maximum_fusion.1
  95.6 0.1 collective-permute-start.10
  95.7 0.6 pick.3
  96.3 7.1 %all-to-all-start.2 = ((f32[16,32,4,128]{3,2,1,0:T(4,128)}), f32[16,32,4,128]{3,2,1,0:T(4,128)S(1)}, u32[]{:S(2)}, u32[]{:S(2)}) async-start(f32[16,32,4,128]{3,2,1,0:T(4,128)} %get-tuple-element.40), calls=%async_computation.2 | async-start | bytes 2097152 | tf_op jit(solution)/shard_map/all_to_all | solution.py:389
  103.3 0.0 collective-permute-done.10
  103.4 0.1 collective-permute-start.11
  103.5 0.5 collective-permute-start.6
  104.0 3.4 %collective-permute-start.7 = (f32[4,512]{1,0:T(4,128)S(1)}, f32[4,512]{1,0:T(4,128)S(1)}, u32[]{:S(2)}, u32[]{:S(2)}) collective-permute-start(f32[4,512]{1,0:T(4,128)S(1)} %get-tuple-element.44), channel_id=1, source_target_pairs={{0,240},{16,0},{32,16},{48,32},{64,48},{80,64},{96,80},{112,96},{1... | collective-permute-start | bytes 24584 | tf_op jit(solution)/shard_map/ppermute | solution.py:623
  107.4 0.0 collective-permute-done.11.more_ref
  107.4 0.7 copy-done.15
  108.1 3.3 %inverse_x.1 = (f32[128,192]{1,0:T(8,128)}, f32[64,64]{1,0:T(8,128)}) custom-call(bf16[16,80,1024]{2,1,0:T(8,128)(2,1)} %constant.6.clone.high_ref, bf16[16,80,1024]{2,1,0:T(8,128)(2,1)} %constant.7.clone.low_ref, f32[8,72,128]{2,1,0:T(8,128)} %copy-done.12, f32[8,72,128]{2,1,0:T(8,128)} %copy-done.15), custom_call_target="tpu_custom_call" | custom-call | flops 2000000000 | bytes 6000000 | tf_op jit(solution)/shard_map/inverse_x/pallas_call | solution.py:354
  111.5 0.0 collective-permute-done.6.refs_7_
  111.5 0.0 collective-permute-done.7.refs_8_
  111.5 0.9 copy-done.9
  112.4 13.6 %step_1.1 = f32[16,96,128]{2,1,0:T(8,128)S(1)} custom-call(s32[128,4]{1,0:T(8,128)S(1)} %copy.13.refs_0_, s32[128]{0:T(128)S(1)} %get-tuple-element.27.refs_1_, f32[3,16384]{1,0:T(4,128)S(1)} %get-tuple-element.41.refs_2_, f32[3,16384]{1,0:T(4,128)S(1)} %get-tuple-element.42.refs_3_, f32[1,16384]{1,0:T(1,128)S(1)} %bitcast.4, s32[2,16384]{1,0:T(2,128)S(1)} %copy-done.4, ...), custom_call_target="tpu_custom_call" | custom-call | flops 14000000000 | bytes 42000000 | tf_op jit(solution)/shard_map/step_1/pallas_call | solution.py:571
  126.1 3.2 %all-to-all-done.2.place_ref = f32[16,32,4,128]{3,2,1,0:T(4,128)S(1)} async-done(((f32[16,32,4,128]{3,2,1,0:T(4,128)}), f32[16,32,4,128]{3,2,1,0:T(4,128)S(1)}, u32[]{:S(2)}, u32[]{:S(2)}) %all-to-all-start.2) | async-done | bytes 1048608 | tf_op jit(solution)/shard_map/all_to_all | solution.py:389
  129.3 27.2 %all_to_all.21.speed_ref = f32[16,96,128]{2,1,0:T(8,128)S(1)} all-to-all(f32[16,96,128]{2,1,0:T(8,128)S(1)} %step_1.1), channel_id=1, replica_groups=mesh['rad'=16,'azi'=16] {'azi'}, dimensions={0} | all-to-all | bytes 1572864 | tf_op jit(solution)/shard_map/all_to_all | solution.py:389
  156.5 3.2 %assemble.1 = f32[7,65536]{1,0:T(8,128)} custom-call(f32[16,32,4,128]{3,2,1,0:T(4,128)S(1)} %all-to-all-done.2.place_ref, f32[16,96,128]{2,1,0:T(8,128)S(1)} %all_to_all.21.speed_ref), custom_call_target="tpu_custom_call" | custom-call | flops 4000000000 | bytes 12000000 | tf_op jit(solution)/shard_map/assemble/pallas_call | solution.py:610
  (32 shorter events, 0.1 us)
Async XLA Ops:
  0.6 13.0 %copy-start.5 = (f32[16384]{0:T(1024)S(1)}, f32[16384]{0:T(1024)}, u32[]{:S(2)}) copy-start(f32[16384]{0:T(1024)} %param.13) | copy-start | bytes 196612
  0.6 13.0 %copy-start.4 = (s32[2,16384]{1,0:T(2,128)S(1)}, s32[2,16384]{1,0:T(2,128)}, u32[]{:S(2)}) copy-start(s32[2,16384]{1,0:T(2,128)} %refs_5_.3) | copy-start | bytes 393220
  0.7 13.0 %copy-start.8 = (s32[128]{0:T(128)S(1)}, s32[128]{0:T(128)}, u32[]{:S(2)}) copy-start(s32[128]{0:T(128)} %dest_ref.1) | copy-start | bytes 1540
  0.7 29.0 %copy-start.6 = (f32[64,64]{1,0:T(8,128)S(1)}, f32[64,64]{1,0:T(8,128)}, u32[]{:S(2)}) copy-start(f32[64,64]{1,0:T(8,128)} %refs_9_.1) | copy-start | bytes 49156
  0.7 29.0 %copy-start.7 = (s32[2,16]{1,0:T(2,128)S(1)}, s32[2,16]{1,0:T(2,128)}, u32[]{:S(2)}) copy-start(s32[2,16]{1,0:T(2,128)} %shear_ref.3) | copy-start | bytes 388
  2.4 28.6 %copy-start.14 = (s32[128,4]{0,1:T(4,128)S(1)}, s32[128,4]{0,1:T(4,128)}, u32[]{:S(2)}) copy-start(s32[128,4]{0,1:T(4,128)} %param.14) | copy-start | bytes 6148
  2.4 34.0 %copy-start.2 = (f32[3,16384]{1,0:T(4,128)S(1)}, f32[3,16384]{1,0:T(4,128)}, u32[]{:S(2)}) copy-start(f32[3,16384]{1,0:T(4,128)} %refs_2_.1) | copy-start | bytes 589828
  2.4 34.0 %copy-start.3 = (f32[3,16384]{1,0:T(4,128)S(1)}, f32[3,16384]{1,0:T(4,128)}, u32[]{:S(2)}) copy-start(f32[3,16384]{1,0:T(4,128)} %refs_3_.1) | copy-start | bytes 589828
  2.4 27.3 %all-to-all-start = ((f32[16,8,896]{2,1,0:T(8,128)}), f32[16,8,896]{2,1,0:T(8,128)S(1)}, u32[]{:S(2)}, u32[]{:S(2)}) async-start(f32[16,8,896]{2,1,0:T(8,128)} %edges.1), calls=%async_computation | async-start | bytes 917504 | tf_op jit(solution)/shard_map/all_to_all | solution.py:389
  19.9 5.5 %collective-permute-start = (f32[1,64,128]{2,1,0:T(8,128)S(1)}, f32[1,64,128]{2,1,0:T(8,128)S(1)}, u32[]{:S(2)}, u32[]{:S(2)}) collective-permute-start(f32[1,64,128]{2,1,0:T(8,128)S(1)} %get-tuple-element.29), channel_id=1, source_target_pairs={{0,128},{16,144},{32,160},{48,176},{64,192},{80,208},{96,224},{112... | collective-permute-start | bytes 98312 | tf_op jit(solution)/shard_map/ppermute | solution.py:374
  25.4 4.3 %collective-permute-start.1 = (f32[2,64,128]{2,1,0:T(8,128)S(1)}, f32[2,64,128]{2,1,0:T(8,128)S(1)}, u32[]{:S(2)}, u32[]{:S(2)}) collective-permute-start(f32[2,64,128]{2,1,0:T(8,128)S(1)} %pad_maximum_fusion.4), channel_id=1, source_target_pairs={{0,64},{16,80},{32,96},{48,112},{64,0},{80,16},{96,32},{112,48},{1... | collective-permute-start | bytes 196616 | tf_op jit(solution)/shard_map/ppermute | solution.py:374
  30.3 5.2 %collective-permute-start.4 = (f32[4,64,128]{2,1,0:T(8,128)S(1)}, f32[4,64,128]{2,1,0:T(8,128)S(1)}, u32[]{:S(2)}, u32[]{:S(2)}) collective-permute-start(f32[4,64,128]{2,1,0:T(8,128)S(1)} %pad_maximum_fusion.2), channel_id=1, source_target_pairs={{0,32},{16,48},{32,0},{48,16},{64,96},{80,112},{96,64},{112,80},{1... | collective-permute-start | bytes 393224 | tf_op jit(solution)/shard_map/ppermute | solution.py:374
  31.1 5.3 %collective-permute-start.2 = (f32[4,640]{1,0:T(4,128)S(1)}, f32[4,640]{1,0:T(4,128)S(1)}, u32[]{:S(2)}, u32[]{:S(2)}) collective-permute-start(f32[4,640]{1,0:T(4,128)S(1)} %get-tuple-element.32), channel_id=1, source_target_pairs={{0,16},{16,32},{32,48},{48,64},{64,80},{80,96},{96,112},{112,128},... | collective-permute-start | bytes 30728 | tf_op jit(solution)/shard_map/ppermute | solution.py:623
  31.2 5.2 %collective-permute-start.3 = (f32[4,640]{1,0:T(4,128)S(1)}, f32[4,640]{1,0:T(4,128)S(1)}, u32[]{:S(2)}, u32[]{:S(2)}) collective-permute-start(f32[4,640]{1,0:T(4,128)S(1)} %get-tuple-element.33), channel_id=1, source_target_pairs={{0,240},{16,0},{32,16},{48,32},{64,48},{80,64},{96,80},{112,96},{1... | collective-permute-start | bytes 30728 | tf_op jit(solution)/shard_map/ppermute | solution.py:623
  35.5 15.8 %copy-start.10 = (f32[8,64,128]{2,1,0:T(8,128)}, f32[8,64,128]{2,1,0:T(8,128)S(1)}, u32[]{:S(2)}) copy-start(f32[8,64,128]{2,1,0:T(8,128)S(1)} %constant_dynamic-update-slice_fusion.dens_ref) | copy-start | bytes 786436
  35.5 16.5 %collective-permute-start.5 = (f32[8,64,128]{2,1,0:T(8,128)S(1)}, f32[8,64,128]{2,1,0:T(8,128)S(1)}, u32[]{:S(2)}, u32[]{:S(2)}) collective-permute-start(f32[8,64,128]{2,1,0:T(8,128)S(1)} %constant_dynamic-update-slice_fusion.dens_ref), channel_id=1, source_target_pairs={{0,16},{16,0},{32,48},{48,32},{64,80},{80,64},{96,112},{112,96},{1... | collective-permute-start | bytes 786440 | tf_op jit(solution)/shard_map/ppermute | solution.py:374
  51.3 0.8 copy-start.1
  52.0 0.7 copy-start.13
  81.0 14.7 %copy-start = (f32[16,8,896]{2,1,0:T(8,128)S(1)}, f32[16,8,896]{2,1,0:T(8,128)}, u32[]{:S(2)}) copy-start(f32[16,8,896]{2,1,0:T(8,128)} %all_to_all.20.far_ref.refs_6_) | copy-start | bytes 1376260
  83.9 19.4 %copy-start.11 = (f32[1,72,128]{2,1,0:T(8,128)S(1)}, f32[1,72,128]{2,1,0:T(8,128)}, u32[]{:S(2)}) copy-start(f32[1,72,128]{2,1,0:T(8,128)} %solve_y.1) | copy-start | bytes 110596
  83.9 5.8 %collective-permute-start.8 = (f32[1,72,128]{2,1,0:T(8,128)}, f32[1,72,128]{2,1,0:T(8,128)S(1)}, u32[]{:S(2)}, u32[]{:S(2)}) collective-permute-start(f32[1,72,128]{2,1,0:T(8,128)} %solve_y.1), channel_id=1, source_target_pairs={{0,128},{16,144},{32,160},{48,176},{64,192},{80,208},{96,224},{112... | collective-permute-start | bytes 110600 | tf_op jit(solution)/shard_map/ppermute | solution.py:374
  90.5 4.4 %collective-permute-start.9 = (f32[2,72,128]{2,1,0:T(8,128)S(1)}, f32[2,72,128]{2,1,0:T(8,128)S(1)}, u32[]{:S(2)}, u32[]{:S(2)}) collective-permute-start(f32[2,72,128]{2,1,0:T(8,128)S(1)} %pad_maximum_fusion.3), channel_id=1, source_target_pairs={{0,64},{16,80},{32,96},{48,112},{64,0},{80,16},{96,32},{112,48},{1... | collective-permute-start | bytes 221192 | tf_op jit(solution)/shard_map/ppermute | solution.py:374
  95.6 7.8 %collective-permute-start.10 = (f32[4,72,128]{2,1,0:T(8,128)S(1)}, f32[4,72,128]{2,1,0:T(8,128)S(1)}, u32[]{:S(2)}, u32[]{:S(2)}) collective-permute-start(f32[4,72,128]{2,1,0:T(8,128)S(1)} %pad_maximum_fusion.1), channel_id=1, source_target_pairs={{0,32},{16,48},{32,0},{48,16},{64,96},{80,112},{96,64},{112,80},{1... | collective-permute-start | bytes 442376 | tf_op jit(solution)/shard_map/ppermute | solution.py:374
  96.3 33.0 %all-to-all-start.2 = ((f32[16,32,4,128]{3,2,1,0:T(4,128)}), f32[16,32,4,128]{3,2,1,0:T(4,128)S(1)}, u32[]{:S(2)}, u32[]{:S(2)}) async-start(f32[16,32,4,128]{3,2,1,0:T(4,128)} %get-tuple-element.40), calls=%async_computation.2 | async-start | bytes 2097152 | tf_op jit(solution)/shard_map/all_to_all | solution.py:389
  103.4 4.0 %copy-start.12 = (f32[8,72,128]{2,1,0:T(8,128)}, f32[8,72,128]{2,1,0:T(8,128)S(1)}, u32[]{:S(2)}) copy-start(f32[8,72,128]{2,1,0:T(8,128)S(1)} %pad_maximum_fusion.in_ref) | copy-start | bytes 884740
  103.4 4.0 %collective-permute-start.11 = (f32[8,72,128]{2,1,0:T(8,128)S(1)}, f32[8,72,128]{2,1,0:T(8,128)S(1)}, u32[]{:S(2)}, u32[]{:S(2)}) collective-permute-start(f32[8,72,128]{2,1,0:T(8,128)S(1)} %pad_maximum_fusion.in_ref), channel_id=1, source_target_pairs={{0,16},{16,0},{32,48},{48,32},{64,80},{80,64},{96,112},{112,96},{1... | collective-permute-start | bytes 884744 | tf_op jit(solution)/shard_map/ppermute | solution.py:374
  103.5 8.0 %collective-permute-start.6 = (f32[4,512]{1,0:T(4,128)S(1)}, f32[4,512]{1,0:T(4,128)S(1)}, u32[]{:S(2)}, u32[]{:S(2)}) collective-permute-start(f32[4,512]{1,0:T(4,128)S(1)} %get-tuple-element.43), channel_id=1, source_target_pairs={{0,16},{16,32},{32,48},{48,64},{64,80},{80,96},{96,112},{112,128},... | collective-permute-start | bytes 24584 | tf_op jit(solution)/shard_map/ppermute | solution.py:623
  104.0 7.5 %collective-permute-start.7 = (f32[4,512]{1,0:T(4,128)S(1)}, f32[4,512]{1,0:T(4,128)S(1)}, u32[]{:S(2)}, u32[]{:S(2)}) collective-permute-start(f32[4,512]{1,0:T(4,128)S(1)} %get-tuple-element.44), channel_id=1, source_target_pairs={{0,240},{16,0},{32,16},{48,32},{64,48},{80,64},{96,80},{112,96},{1... | collective-permute-start | bytes 24584 | tf_op jit(solution)/shard_map/ppermute | solution.py:623
  107.4 0.7 copy-start.15
  111.5 0.9 copy-start.9

commit v4 on v3

--- a/solution.py
+++ b/solution.py
@@ -248,9 +248,10 @@
 def forward_x_kernel(high_ref, low_ref, power_ref, dens_ref, more_ref, edges_ref, sums_ref, sent_ref,
                      ends_ref, all_ref, scan_ref, h_ref, l_ref, p_ref, sem_ref):
     r, _, _, _ = places()
-    copies = fetch(((high_ref.at[r], h_ref), (low_ref.at[r], l_ref), (power_ref.at[r], p_ref)), sem_ref)
+    pairs = [(high_ref.at[r], h_ref), (low_ref.at[r], l_ref), (power_ref.at[r], p_ref)]
     for ref, p, d in blocks_of((dens_ref, more_ref)):
-        all_ref[pl.ds(pl.multiple_of(d * G, G), G)] = ref[p]
+        pairs.append((ref.at[p], all_ref.at[pl.ds(pl.multiple_of(d * G, G), G)]))
+    copies = fetch(pairs, sem_ref)
     for copy in copies:
         copy.wait()
     lines = dot3(h_ref[1 : G + 1], l_ref[1 : G + 1], all_ref[...])
@@ -291,7 +292,7 @@
         for b in range(count):
             n = (a - b) * G + row - 1 - lane
             n = jnp.where(n < 0, n + size, n)
-            total += (n * (size - n)).astype(F32) * (parts[b] - mean)
+            total += ((n * (size - n)).astype(F32) - (size * size - 1) / 6.0) * (parts[b] - mean)
         constant.append(jnp.sum(total, axis=1, keepdims=True) * (GRAV / (2.0 * size)))
     copies[0].wait()
     start = jnp.zeros((1, 2 * G), F32)
@@ -319,18 +320,19 @@
     out_ref[0, G + 1 : G + 2] = lines[G + 1 : G + 2]
 
 
-def inverse_x_kernel(high_ref, low_ref, in_ref, more_ref, grad_ref, pot_ref, all_ref, halo_ref, side_ref,
+def inverse_x_kernel(high_ref, low_ref, in_ref, more_ref, grad_ref, pot_ref, all_ref, halo_ref, blocks_ref,
                      turn_ref, h_ref, l_ref, sem_ref):
     r, _, _, _ = places()
-    copies = fetch(((high_ref.at[r], h_ref), (low_ref.at[r], l_ref)), sem_ref)
+    pairs = [(high_ref.at[r], h_ref), (low_ref.at[r], l_ref)]
+    for ref, p, d in blocks_of((in_ref, more_ref)):
+        pairs.append((ref.at[p], blocks_ref.at[d]))
+    copies = fetch(pairs, sem_ref)
     halo_ref[...] = jnp.zeros_like(halo_ref)
-    for ref, p, d in blocks_of((in_ref, more_ref)):
-        all_ref[pl.ds(pl.multiple_of(d * G, G), G)] = ref[p, 0:G]
-        side_ref[d] = ref[p, G : G + 8, 0:G]
-    for d in range(side_ref.shape[0]):
-        halo_ref[:, d * G : (d + 1) * G] = side_ref[d]
     for copy in copies:
         copy.wait()
+    for d in range(blocks_ref.shape[0]):
+        all_ref[d * G : (d + 1) * G] = blocks_ref[d, 0:G]
+        halo_ref[:, d * G : (d + 1) * G] = blocks_ref[d, G : G + 8, 0:G]
     grid = dot3(h_ref[...], l_ref[...], all_ref[...])
     pot_ref[...] = grid[1 : G + 1, G : 2 * G]
     b_high, b_low = split2(halo_ref[...])
@@ -645,10 +647,10 @@
         0, neighbours, target, positions, velocities, mass, deposit_cells, far, up, down, (old_potential,), azi_count,
     )
     sums, sent_1 = solve_call(
-        forward_x_kernel, "forward_x", (rows_high, rows_low, power), (dens, dens_more, edges_1),
+        forward_x_kernel, "forward_x", (rows_high, rows_low, power, dens, dens_more), (edges_1,),
         (jax.ShapeDtypeStruct((3, G, 2 * G), F32), jax.ShapeDtypeStruct((azi_count, 8, HALO + 2 * G), F32)),
         (pltpu.VMEM((8, 2 * G), F32), pltpu.VMEM((size_x, 2 * G), F32), pltpu.VMEM((2 * G, 2 * G), F32), block, block,
-         power_block, pltpu.SemaphoreType.DMA((3,))), 2,
+         power_block, pltpu.SemaphoreType.DMA((3 + rad_count,))), 2,
     )
     far_1 = exchange(sent_1, "azi")
     up_1, down_1 = pick(1, shear_offsets, far_1)
@@ -657,13 +659,13 @@
         (jax.ShapeDtypeStruct((1, G + 8, 2 * G), F32),),
         (power_block, pltpu.VMEM((G + 8, 2 * G), F32), pltpu.SemaphoreType.DMA((1,))), 2,
     )
-    solved, solved_more, _ = gathered(solved, "rad")
+    solved, solved_more, (up_1, down_1) = gathered(solved, "rad", (up_1, down_1), 1)
     gradient, potential = solve_call(
-        inverse_x_kernel, "inverse_x", (rows_high, rows_low), (solved, solved_more),
+        inverse_x_kernel, "inverse_x", (rows_high, rows_low, solved, solved_more), (),
         (jax.ShapeDtypeStruct((2 * G, 3 * G), F32), jax.ShapeDtypeStruct((G, G), F32)),
         (pltpu.VMEM((size_x, 2 * G), F32), pltpu.VMEM((8, size_x), F32),
-         pltpu.VMEM((rad_count, 8, G), F32), pltpu.VMEM((G + 16, G), F32),
-         block, block, pltpu.SemaphoreType.DMA((2,))), 2,
+         pltpu.VMEM((rad_count, G + 8, 2 * G), F32), pltpu.VMEM((G + 16, G), F32),
+         block, block, pltpu.SemaphoreType.DMA((2 + rad_count,))), 2,
     )
 
     pack_place, up_1, down_1 = lax.optimization_barrier((pack_place, up_1, down_1))

time: 160 us -> 163 us (1.019)
  blocking collectives: 51.9 us -> 56.8 us
    all_to_all x2, blocking collectives: 51.9 us -> 56.8 us  [exchange(): return lax.all_to_all(value, axis, split_axis=0, concat_axis=0, tiled=True)]
    all_to_all x2, waiting for transfers between devices: 3.23 us -> 0.01 us  [exchange(): return lax.all_to_all(value, axis, split_axis=0, concat_axis=0, tiled=True)]
    ppermute x8, waiting for transfers between devices: 11.1 us -> 13.1 us  [gathered(): lax.ppermute(whole, axis, [(i, i ^ d) for i in range(count)])]
    all_to_all x2, starting transfers between devices: 18.2 us -> 16.5 us  [exchange(): return lax.all_to_all(value, axis, split_axis=0, concat_axis=0, tiled=True)]
    unnamed x34 -> x37, local copies, waits for them, and re-layouts: 3.22 us -> 4.2 us
  transfers between devices with their start and end apart: 14 -> 14, of which waited for: 7 -> 6; matrix products, arithmetic and copies ran while one was open for 0% -> 2% of each run, Pallas kernels for 24% -> 23%
where the time goes in v4:
time: 163 us
  blocking collectives  56.8 us (35%)
  Pallas kernels  49.9 us (31%)
  starting transfers between devices  35.4 us (22%)
  waiting for transfers between devices  13.9 us (9%)
  local copies, waits for them, and re-layouts  4.22 us (3%)
    all_to_all x2, blocking collectives, exchange(): return lax.all_to_all(value, axis, split_axis=0, concat_axis=0, tiled=True)  56.8 us
    pallas_call x2, Pallas kernels, step(): pl.pallas_call(functools.partial(step_kernel, last), in_specs=[SMEM] * 2...  28.6 us
    all_to_all x2, starting transfers between devices, exchange(): return lax.all_to_all(value, axis, split_axis=0, concat_axis=0, tiled=True)  16.5 us
    ppermute x8, waiting for transfers between devices, gathered(): lax.ppermute(whole, axis, [(i, i ^ d) for i in range(count)])  13.1 us
    ppermute x8, starting transfers between devices, gathered(): lax.ppermute(whole, axis, [(i, i ^ d) for i in range(count)])  11 us
    pallas_call x3, Pallas kernels, solve_call(): pl.pallas_call(kernel, in_specs=[HBM] * len(tables_in) + [VMEM] * len(arr...  8.98 us
    ppermute x4, starting transfers between devices, shifted(): lax.ppermute(value, axis, [(i, (i + steps) % count) for i in range(count)])  7.85 us
    pallas_call x1, Pallas kernels, densities(): pl.pallas_call(density_kernel, in_specs=[VMEM, VMEM, SMEM], out_specs=[VM...  6.25 us
  transfers between devices with their start and end apart: 14, of which 6 were waited for; matrix products, arithmetic and copies ran while one was open for 2% of the time, Pallas kernels for 23%

profile of v4, /device:TPU:32, one launch (start us, length us, event | category | flops | bytes accessed | tf_op | source)
XLA Modules:
  0.0 162.6 jit_solution(6204338919558338206)
XLA Ops:
  0.7 1.7 %edges.1 = f32[16,8,896]{2,1,0:T(8,128)} custom-call(f32[3,16384]{1,0:T(4,128)} %refs_2_.1, f32[1,16384]{1,0:T(1,128)} %bitcast.1, f32[64,64]{1,0:T(8,128)} %refs_9_.1), custom_call_target="tpu_custom_call" | custom-call | flops 1000000000 | bytes 3000000 | tf_op jit(solution)/shard_map/edges/pallas_call | solution.py:134
  2.4 11.2 %all-to-all-start = ((f32[16,8,896]{2,1,0:T(8,128)}), f32[16,8,896]{2,1,0:T(8,128)S(1)}, u32[]{:S(2)}, u32[]{:S(2)}) async-start(f32[16,8,896]{2,1,0:T(8,128)} %edges.1), calls=%async_computation | async-start | bytes 917504 | tf_op jit(solution)/shard_map/all_to_all | solution.py:391
  13.6 6.2 %densities.1 = (f32[1,64,128]{2,1,0:T(8,128)S(1)}, s32[128]{0:T(128)S(1)}) custom-call(s32[2,16384]{1,0:T(2,128)S(1)} %copy-done.5, f32[1,16384]{1,0:T(1,128)S(1)} %bitcast.2, s32[128]{0:T(128)S(1)} %copy-done.9), custom_call_target="tpu_custom_call" | custom-call | flops 300000000 | bytes 900000 | tf_op jit(solution)/shard_map/densities/pallas_call | solution.py:218
  19.9 3.3 %collective-permute-start = (f32[1,64,128]{2,1,0:T(8,128)S(1)}, f32[1,64,128]{2,1,0:T(8,128)S(1)}, u32[]{:S(2)}, u32[]{:S(2)}) collective-permute-start(f32[1,64,128]{2,1,0:T(8,128)S(1)} %get-tuple-element.32), channel_id=1, source_target_pairs={{0,128},{16,144},{32,160},{48,176},{64,192},{80,208},{96,224},{112... | collective-permute-start | bytes 98312 | tf_op jit(solution)/shard_map/ppermute | solution.py:376
  23.2 2.2 %collective-permute-done = f32[1,64,128]{2,1,0:T(8,128)S(1)} collective-permute-done((f32[1,64,128]{2,1,0:T(8,128)S(1)}, f32[1,64,128]{2,1,0:T(8,128)S(1)}, u32[]{:S(2)}, u32[]{:S(2)}) %collective-permute-start) | collective-permute-done | bytes 32800 | tf_op jit(solution)/shard_map/ppermute | solution.py:376
  25.4 1.6 collective-permute-start.1
  27.0 2.7 %collective-permute-done.1 = f32[2,64,128]{2,1,0:T(8,128)S(1)} collective-permute-done((f32[2,64,128]{2,1,0:T(8,128)S(1)}, f32[2,64,128]{2,1,0:T(8,128)S(1)}, u32[]{:S(2)}, u32[]{:S(2)}) %collective-permute-start.1) | collective-permute-done | bytes 65568 | tf_op jit(solution)/shard_map/ppermute | solution.py:376
  29.7 0.0 all-to-all-done.far_ref.refs_6_
  29.7 0.6 pick.2
  30.3 0.7 collective-permute-start.4
  31.0 0.1 copy.13.refs_0_
  31.1 0.1 collective-permute-start.2
  31.2 3.8 %collective-permute-start.3 = (f32[4,640]{1,0:T(4,128)S(1)}, f32[4,640]{1,0:T(4,128)S(1)}, u32[]{:S(2)}, u32[]{:S(2)}) collective-permute-start(f32[4,640]{1,0:T(4,128)S(1)} %get-tuple-element.36), channel_id=1, source_target_pairs={{0,240},{16,0},{32,16},{48,32},{64,48},{80,64},{96,80},{112,96},{1... | collective-permute-start | bytes 30728 | tf_op jit(solution)/shard_map/ppermute | solution.py:625
  35.0 0.4 collective-permute-done.4
  35.5 0.1 collective-permute-start.5
  35.6 0.8 collective-permute-done.2.refs_7_
  36.4 0.0 collective-permute-done.3.refs_8_
  36.4 14.9 %step_0.1 = (f32[3,16384]{1,0:T(4,128)S(1)}, f32[3,16384]{1,0:T(4,128)S(1)}, f32[16,8,768]{2,1,0:T(8,128)S(1)}, f32[16,32,4,128]{3,2,1,0:T(4,128)}) custom-call(s32[128,4]{1,0:T(8,128)S(1)} %copy.13.refs_0_, s32[128]{0:T(128)S(1)} %get-tuple-element.30.refs_1_, f32[3,16384]{1,0:T(4,128)S(1)} %copy-done.3, f32[3,16384]{1,0:T(4,128)S(1)} %copy-done.4, ...), custom_call_target="tpu_custom_call" | custom-call | flops 14000000000 | bytes 42000000 | tf_op jit(solution)/shard_map/step_0/pallas_call | solution.py:573
  51.3 0.8 copy-done.2
  52.0 0.0 collective-permute-done.5.more_ref
  52.0 0.7 copy-done.12
  52.7 3.6 %forward_x.1 = (f32[3,64,128]{2,1,0:T(8,128)}, f32[16,8,896]{2,1,0:T(8,128)}) custom-call(bf16[16,80,1024]{2,1,0:T(8,128)(2,1)} %constant.6.clone.high_ref, bf16[16,80,1024]{2,1,0:T(8,128)(2,1)} %constant.7.clone.low_ref, f32[16,152,128]{2,1,0:T(8,128)} %constant.8.clone.power_ref, f32[8,64,128]{2,1,0:T(8,128)} %copy-done.11, f32[8,64,128]{2,1,0:T(8,128)} %copy-done.12, ...), custom_call_target="tpu_custom_call" | custom-call | flops 2000000000 | bytes 6000000 | tf_op jit(solution)/shard_map/forward_x/pallas_call | solution.py:356
  56.3 24.6 %all_to_all.20.far_ref.refs_6_ = f32[16,8,896]{2,1,0:T(8,128)S(1)} all-to-all(f32[16,8,896]{2,1,0:T(8,128)} %get-tuple-element.40), channel_id=1, replica_groups=mesh['rad'=16,'azi'=16] {'azi'}, dimensions={0} | all-to-all | bytes 917504 | tf_op jit(solution)/shard_map/all_to_all | solution.py:391
  80.9 0.6 pick.3
  81.5 0.2 copy-done
  81.7 2.8 %solve_y.1 = f32[1,72,128]{2,1,0:T(8,128)} custom-call(f32[16,152,128]{2,1,0:T(8,128)} %constant.8.clone.power_ref, f32[16,8,896]{2,1,0:T(8,128)} %copy-done, f32[3,64,128]{2,1,0:T(8,128)} %get-tuple-element.41.sums_ref), custom_call_target="tpu_custom_call" | custom-call | flops 2000000000 | bytes 6000000 | tf_op jit(solution)/shard_map/solve_y/pallas_call | solution.py:356
  84.6 3.0 %collective-permute-start.8 = (f32[1,72,128]{2,1,0:T(8,128)}, f32[1,72,128]{2,1,0:T(8,128)S(1)}, u32[]{:S(2)}, u32[]{:S(2)}) collective-permute-start(f32[1,72,128]{2,1,0:T(8,128)} %solve_y.1), channel_id=1, source_target_pairs={{0,128},{16,144},{32,160},{48,176},{64,192},{80,208},{96,224},{112... | collective-permute-start | bytes 110600 | tf_op jit(solution)/shard_map/ppermute | solution.py:376
  87.6 5.3 %all-to-all-start.2 = ((f32[16,32,4,128]{3,2,1,0:T(4,128)}), f32[16,32,4,128]{3,2,1,0:T(4,128)S(1)}, u32[]{:S(2)}, u32[]{:S(2)}) async-start(f32[16,32,4,128]{3,2,1,0:T(4,128)} %get-tuple-element.46), calls=%async_computation.2 | async-start | bytes 2097152 | tf_op jit(solution)/shard_map/all_to_all | solution.py:391
  92.9 0.0 collective-permute-done.8
  92.9 0.8 pad_maximum_fusion.2
  93.7 0.8 collective-permute-start.9
  94.5 0.8 constant_dynamic-update-slice_fusion.5
  95.3 2.8 %collective-permute-done.9 = f32[2,72,128]{2,1,0:T(8,128)S(1)} collective-permute-done((f32[2,72,128]{2,1,0:T(8,128)S(1)}, f32[2,72,128]{2,1,0:T(8,128)S(1)}, u32[]{:S(2)}, u32[]{:S(2)}) %collective-permute-start.9) | collective-permute-done | bytes 73760 | tf_op jit(solution)/shard_map/ppermute | solution.py:376
  98.1 0.8 pad_maximum_fusion
  98.9 1.4 collective-permute-start.10
  100.3 4.9 %collective-permute-done.10 = f32[4,72,128]{2,1,0:T(8,128)S(1)} collective-permute-done((f32[4,72,128]{2,1,0:T(8,128)S(1)}, f32[4,72,128]{2,1,0:T(8,128)S(1)}, u32[]{:S(2)}, u32[]{:S(2)}) %collective-permute-start.10) | collective-permute-done | bytes 147488 | tf_op jit(solution)/shard_map/ppermute | solution.py:376
  105.3 0.1 collective-permute-start.11
  105.4 0.5 collective-permute-start.6
  105.9 3.4 %collective-permute-start.7 = (f32[4,512]{1,0:T(4,128)S(1)}, f32[4,512]{1,0:T(4,128)S(1)}, u32[]{:S(2)}, u32[]{:S(2)}) collective-permute-start(f32[4,512]{1,0:T(4,128)S(1)} %get-tuple-element.50), channel_id=1, source_target_pairs={{0,240},{16,0},{32,16},{48,32},{64,48},{80,64},{96,80},{112,96},{1... | collective-permute-start | bytes 24584 | tf_op jit(solution)/shard_map/ppermute | solution.py:625
  109.3 0.0 collective-permute-done.11.more_ref
  109.3 0.7 copy-done.15
  110.0 2.5 %inverse_x.1 = (f32[128,192]{1,0:T(8,128)}, f32[64,64]{1,0:T(8,128)}) custom-call(bf16[16,80,1024]{2,1,0:T(8,128)(2,1)} %constant.6.clone.high_ref, bf16[16,80,1024]{2,1,0:T(8,128)(2,1)} %constant.7.clone.low_ref, f32[8,72,128]{2,1,0:T(8,128)} %copy-done.13, f32[8,72,128]{2,1,0:T(8,128)} %copy-done.15), custom_call_target="tpu_custom_call" | custom-call | flops 2000000000 | bytes 6000000 | tf_op jit(solution)/shard_map/inverse_x/pallas_call | solution.py:356
  112.6 0.0 collective-permute-done.6.refs_7_
  112.6 0.0 collective-permute-done.7.refs_8_
  112.6 0.9 copy-done.10
  113.5 13.7 %step_1.1 = f32[16,96,128]{2,1,0:T(8,128)S(1)} custom-call(s32[128,4]{1,0:T(8,128)S(1)} %copy.13.refs_0_, s32[128]{0:T(128)S(1)} %get-tuple-element.30.refs_1_, f32[3,16384]{1,0:T(4,128)S(1)} %get-tuple-element.47.refs_2_, f32[3,16384]{1,0:T(4,128)S(1)} %get-tuple-element.48.refs_3_, f32[1,16384]{1,0:T(1,128)S(1)} %bitcast.4, s32[2,16384]{1,0:T(2,128)S(1)} %copy-done.5, ...), custom_call_target="tpu_custom_call" | custom-call | flops 14000000000 | bytes 42000000 | tf_op jit(solution)/shard_map/step_1/pallas_call | solution.py:573
  127.2 32.2 %all_to_all.21.speed_ref = f32[16,96,128]{2,1,0:T(8,128)S(1)} all-to-all(f32[16,96,128]{2,1,0:T(8,128)S(1)} %step_1.1), channel_id=1, replica_groups=mesh['rad'=16,'azi'=16] {'azi'}, dimensions={0} | all-to-all | bytes 1572864 | tf_op jit(solution)/shard_map/all_to_all | solution.py:391
  159.4 3.2 %assemble.1 = f32[7,65536]{1,0:T(8,128)} custom-call(f32[16,32,4,128]{3,2,1,0:T(4,128)S(1)} %all-to-all-done.2.place_ref, f32[16,96,128]{2,1,0:T(8,128)S(1)} %all_to_all.21.speed_ref), custom_call_target="tpu_custom_call" | custom-call | flops 4000000000 | bytes 12000000 | tf_op jit(solution)/shard_map/assemble/pallas_call | solution.py:612
  (35 shorter events, 0.1 us)
Async XLA Ops:
  0.6 13.0 %copy-start.6 = (f32[16384]{0:T(1024)S(1)}, f32[16384]{0:T(1024)}, u32[]{:S(2)}) copy-start(f32[16384]{0:T(1024)} %param.13) | copy-start | bytes 196612
  0.6 13.0 %copy-start.5 = (s32[2,16384]{1,0:T(2,128)S(1)}, s32[2,16384]{1,0:T(2,128)}, u32[]{:S(2)}) copy-start(s32[2,16384]{1,0:T(2,128)} %refs_5_.3) | copy-start | bytes 393220
  0.7 13.0 %copy-start.9 = (s32[128]{0:T(128)S(1)}, s32[128]{0:T(128)}, u32[]{:S(2)}) copy-start(s32[128]{0:T(128)} %dest_ref.1) | copy-start | bytes 1540
  0.7 29.0 %copy-start.7 = (f32[64,64]{1,0:T(8,128)S(1)}, f32[64,64]{1,0:T(8,128)}, u32[]{:S(2)}) copy-start(f32[64,64]{1,0:T(8,128)} %refs_9_.1) | copy-start | bytes 49156
  0.7 29.0 %copy-start.8 = (s32[2,16]{1,0:T(2,128)S(1)}, s32[2,16]{1,0:T(2,128)}, u32[]{:S(2)}) copy-start(s32[2,16]{1,0:T(2,128)} %shear_ref.3) | copy-start | bytes 388
  2.4 28.6 %copy-start.14 = (s32[128,4]{0,1:T(4,128)S(1)}, s32[128,4]{0,1:T(4,128)}, u32[]{:S(2)}) copy-start(s32[128,4]{0,1:T(4,128)} %param.14) | copy-start | bytes 6148
  2.4 34.0 %copy-start.3 = (f32[3,16384]{1,0:T(4,128)S(1)}, f32[3,16384]{1,0:T(4,128)}, u32[]{:S(2)}) copy-start(f32[3,16384]{1,0:T(4,128)} %refs_2_.1) | copy-start | bytes 589828
  2.4 34.0 %copy-start.4 = (f32[3,16384]{1,0:T(4,128)S(1)}, f32[3,16384]{1,0:T(4,128)}, u32[]{:S(2)}) copy-start(f32[3,16384]{1,0:T(4,128)} %refs_3_.1) | copy-start | bytes 589828
  2.4 27.3 %all-to-all-start = ((f32[16,8,896]{2,1,0:T(8,128)}), f32[16,8,896]{2,1,0:T(8,128)S(1)}, u32[]{:S(2)}, u32[]{:S(2)}) async-start(f32[16,8,896]{2,1,0:T(8,128)} %edges.1), calls=%async_computation | async-start | bytes 917504 | tf_op jit(solution)/shard_map/all_to_all | solution.py:391
  19.9 5.5 %collective-permute-start = (f32[1,64,128]{2,1,0:T(8,128)S(1)}, f32[1,64,128]{2,1,0:T(8,128)S(1)}, u32[]{:S(2)}, u32[]{:S(2)}) collective-permute-start(f32[1,64,128]{2,1,0:T(8,128)S(1)} %get-tuple-element.32), channel_id=1, source_target_pairs={{0,128},{16,144},{32,160},{48,176},{64,192},{80,208},{96,224},{112... | collective-permute-start | bytes 98312 | tf_op jit(solution)/shard_map/ppermute | solution.py:376
  25.4 4.3 %collective-permute-start.1 = (f32[2,64,128]{2,1,0:T(8,128)S(1)}, f32[2,64,128]{2,1,0:T(8,128)S(1)}, u32[]{:S(2)}, u32[]{:S(2)}) collective-permute-start(f32[2,64,128]{2,1,0:T(8,128)S(1)} %pad_maximum_fusion.3), channel_id=1, source_target_pairs={{0,64},{16,80},{32,96},{48,112},{64,0},{80,16},{96,32},{112,48},{1... | collective-permute-start | bytes 196616 | tf_op jit(solution)/shard_map/ppermute | solution.py:376
  30.3 5.2 %collective-permute-start.4 = (f32[4,64,128]{2,1,0:T(8,128)S(1)}, f32[4,64,128]{2,1,0:T(8,128)S(1)}, u32[]{:S(2)}, u32[]{:S(2)}) collective-permute-start(f32[4,64,128]{2,1,0:T(8,128)S(1)} %pad_maximum_fusion.1), channel_id=1, source_target_pairs={{0,32},{16,48},{32,0},{48,16},{64,96},{80,112},{96,64},{112,80},{1... | collective-permute-start | bytes 393224 | tf_op jit(solution)/shard_map/ppermute | solution.py:376
  31.1 5.3 %collective-permute-start.2 = (f32[4,640]{1,0:T(4,128)S(1)}, f32[4,640]{1,0:T(4,128)S(1)}, u32[]{:S(2)}, u32[]{:S(2)}) collective-permute-start(f32[4,640]{1,0:T(4,128)S(1)} %get-tuple-element.35), channel_id=1, source_target_pairs={{0,16},{16,32},{32,48},{48,64},{64,80},{80,96},{96,112},{112,128},... | collective-permute-start | bytes 30728 | tf_op jit(solution)/shard_map/ppermute | solution.py:625
  31.2 5.2 %collective-permute-start.3 = (f32[4,640]{1,0:T(4,128)S(1)}, f32[4,640]{1,0:T(4,128)S(1)}, u32[]{:S(2)}, u32[]{:S(2)}) collective-permute-start(f32[4,640]{1,0:T(4,128)S(1)} %get-tuple-element.36), channel_id=1, source_target_pairs={{0,240},{16,0},{32,16},{48,32},{64,48},{80,64},{96,80},{112,96},{1... | collective-permute-start | bytes 30728 | tf_op jit(solution)/shard_map/ppermute | solution.py:625
  35.5 15.8 %copy-start.11 = (f32[8,64,128]{2,1,0:T(8,128)}, f32[8,64,128]{2,1,0:T(8,128)S(1)}, u32[]{:S(2)}) copy-start(f32[8,64,128]{2,1,0:T(8,128)S(1)} %constant_dynamic-update-slice_fusion.dens_ref) | copy-start | bytes 786436
  35.5 16.5 %collective-permute-start.5 = (f32[8,64,128]{2,1,0:T(8,128)S(1)}, f32[8,64,128]{2,1,0:T(8,128)S(1)}, u32[]{:S(2)}, u32[]{:S(2)}) collective-permute-start(f32[8,64,128]{2,1,0:T(8,128)S(1)} %constant_dynamic-update-slice_fusion.dens_ref), channel_id=1, source_target_pairs={{0,16},{16,0},{32,48},{48,32},{64,80},{80,64},{96,112},{112,96},{1... | collective-permute-start | bytes 786440 | tf_op jit(solution)/shard_map/ppermute | solution.py:376
  51.3 0.8 copy-start.2
  52.0 0.7 copy-start.12
  80.9 0.8 copy-start
  84.6 8.4 %collective-permute-start.8 = (f32[1,72,128]{2,1,0:T(8,128)}, f32[1,72,128]{2,1,0:T(8,128)S(1)}, u32[]{:S(2)}, u32[]{:S(2)}) collective-permute-start(f32[1,72,128]{2,1,0:T(8,128)} %solve_y.1), channel_id=1, source_target_pairs={{0,128},{16,144},{32,160},{48,176},{64,192},{80,208},{96,224},{112... | collective-permute-start | bytes 110600 | tf_op jit(solution)/shard_map/ppermute | solution.py:376
  87.6 39.6 %all-to-all-start.2 = ((f32[16,32,4,128]{3,2,1,0:T(4,128)}), f32[16,32,4,128]{3,2,1,0:T(4,128)S(1)}, u32[]{:S(2)}, u32[]{:S(2)}) async-start(f32[16,32,4,128]{3,2,1,0:T(4,128)} %get-tuple-element.46), calls=%async_computation.2 | async-start | bytes 2097152 | tf_op jit(solution)/shard_map/all_to_all | solution.py:391
  93.7 4.4 %collective-permute-start.9 = (f32[2,72,128]{2,1,0:T(8,128)S(1)}, f32[2,72,128]{2,1,0:T(8,128)S(1)}, u32[]{:S(2)}, u32[]{:S(2)}) collective-permute-start(f32[2,72,128]{2,1,0:T(8,128)S(1)} %pad_maximum_fusion.2), channel_id=1, source_target_pairs={{0,64},{16,80},{32,96},{48,112},{64,0},{80,16},{96,32},{112,48},{1... | collective-permute-start | bytes 221192 | tf_op jit(solution)/shard_map/ppermute | solution.py:376
  98.9 6.4 %collective-permute-start.10 = (f32[4,72,128]{2,1,0:T(8,128)S(1)}, f32[4,72,128]{2,1,0:T(8,128)S(1)}, u32[]{:S(2)}, u32[]{:S(2)}) collective-permute-start(f32[4,72,128]{2,1,0:T(8,128)S(1)} %pad_maximum_fusion), channel_id=1, source_target_pairs={{0,32},{16,48},{32,0},{48,16},{64,96},{80,112},{96,64},{112,80},{1... | collective-permute-start | bytes 442376 | tf_op jit(solution)/shard_map/ppermute | solution.py:376
  105.3 4.1 %copy-start.13 = (f32[8,72,128]{2,1,0:T(8,128)}, f32[8,72,128]{2,1,0:T(8,128)S(1)}, u32[]{:S(2)}) copy-start(f32[8,72,128]{2,1,0:T(8,128)S(1)} %constant_dynamic-update-slice_fusion.2.in_ref) | copy-start | bytes 884740
  105.3 7.3 %copy-start.1 = (f32[16,8,896]{2,1,0:T(8,128)S(1)}, f32[16,8,896]{2,1,0:T(8,128)}, u32[]{:S(2)}) copy-start(f32[16,8,896]{2,1,0:T(8,128)} %copy-done) | copy-start | bytes 1376260
  105.3 4.0 %collective-permute-start.11 = (f32[8,72,128]{2,1,0:T(8,128)S(1)}, f32[8,72,128]{2,1,0:T(8,128)S(1)}, u32[]{:S(2)}, u32[]{:S(2)}) collective-permute-start(f32[8,72,128]{2,1,0:T(8,128)S(1)} %constant_dynamic-update-slice_fusion.2.in_ref), channel_id=1, source_target_pairs={{0,16},{16,0},{32,48},{48,32},{64,80},{80,64},{96,112},{112,96},{1... | collective-permute-start | bytes 884744 | tf_op jit(solution)/shard_map/ppermute | solution.py:376
  105.4 7.2 %collective-permute-start.6 = (f32[4,512]{1,0:T(4,128)S(1)}, f32[4,512]{1,0:T(4,128)S(1)}, u32[]{:S(2)}, u32[]{:S(2)}) collective-permute-start(f32[4,512]{1,0:T(4,128)S(1)} %get-tuple-element.49), channel_id=1, source_target_pairs={{0,16},{16,32},{32,48},{48,64},{64,80},{80,96},{96,112},{112,128},... | collective-permute-start | bytes 24584 | tf_op jit(solution)/shard_map/ppermute | solution.py:625
  105.9 6.7 %collective-permute-start.7 = (f32[4,512]{1,0:T(4,128)S(1)}, f32[4,512]{1,0:T(4,128)S(1)}, u32[]{:S(2)}, u32[]{:S(2)}) collective-permute-start(f32[4,512]{1,0:T(4,128)S(1)} %get-tuple-element.50), channel_id=1, source_target_pairs={{0,240},{16,0},{32,16},{48,32},{64,48},{80,64},{96,80},{112,96},{1... | collective-permute-start | bytes 24584 | tf_op jit(solution)/shard_map/ppermute | solution.py:625
  109.3 0.7 copy-start.15
  112.6 0.9 copy-start.10
